TPU v7x, 32 devices: a whole 2x2x4 slice. The times are simulated.
32 devices in a mesh: contact: 8 (over y, x, core), body: 4 (over z).
Axes of the slice: x: 2, y: 2, z: 4, core: 2. Of those that a mesh axis runs over, the one named last changes fastest.
Arguments:
- jacobian: bfloat16 [512, 2, 384, 384], P(('contact', 'body')), may hold values from -0.21875 to 0.21875
- tile_block: int32 [512, 2], P(('contact', 'body')), may hold values from 0 to 31
- tile_count: int32 [32], P(('contact', 'body')), may hold values from 8 to 16, as said below
- vel_free: float32 [128, 384], P('body'), may hold values from -6 to 6
- inv_mass: float32 [128, 384], P('body'), may hold values from 0.25 to 2
- bias: float32 [512, 384], P(('contact', 'body')), may hold values from -6 to 6
- step_scale: float32 [512, 384], P(('contact', 'body')), may hold values from 0.05 to 0.5
- friction: float32 [512, 128], P(('contact', 'body')), may hold values from 0.2 to 1
- impulse_start: float32 [512, 384], P(('contact', 'body')), may hold values from -6 to 6
Outputs:
- impulse: float32 [512, 384], P(('contact', 'body'))
- velocity: float32 [128, 384], P('body')
Inputs may be any that keep to these rules, and one draw needn't show every extreme that they name: `tile_count`: some device has all 16 tile slots live in every draw.
All inputs are finite; a program needn't handle non-finite values.
Results may differ from a plain program's by a relative error of at most 0.0062.
Values may be sent and summed in bfloat16 or wider, within the bound.
No kernel may reach another device: no remote copies, remote signals or barrier semaphores. Data moves between devices by JAX's collectives and lax.ppermute only.
A program may use at most 64 MiB of HBM per device.

v0:
```python
import functools

import jax
import jax.numpy as jnp
from jax import lax
from jax.experimental import pallas as pl
from jax.experimental.pallas import tpu as pltpu
from jax.sharding import PartitionSpec as P

ITERS = 2


def crossed(value, target):
    count, groups = lax.axis_size("body"), lax.axis_size("contact")
    cross = 1 if groups % 2 == 0 else 0
    pairs = [
        (group * count + place, (group ^ cross) * count + target(place) % count)
        for group in range(groups)
        for place in range(count)
    ]
    return lax.ppermute(value, ("contact", "body"), pairs)


def ahead_of(place):
    return place + 1


def traded(ahead, back, even, *extra):
    both = lambda value: jnp.concatenate([value, *extra]) if extra else value
    if lax.axis_size("body") % 2:
        return crossed(ahead, ahead_of), crossed(both(back), lambda place: place - 1)
    far, close = lax.optimization_barrier(
        (both(jnp.where(even, back, ahead)), both(jnp.where(even, ahead, back)))
    )
    wide = crossed(far, lambda place: place + 2 * (place % 2) - 1)
    near = crossed(close, lambda place: place ^ 1)
    rows = ahead.shape[0]
    return jnp.where(even, wide[:rows], near[:rows]), jnp.where(even, near, wide)


def rounded(value):
    return value.astype(jnp.bfloat16)


def tree(values):
    while len(values) > 1:
        values = [left + right for left, right in zip(values[::2], values[1::2])]
    return values[0]


def pair_sum(value):
    count = lax.axis_size("contact")
    if count % 2:
        return value
    return value + lax.ppermute(value, "contact", [(place, place ^ 1) for place in range(count)])


def pair_count():
    count = lax.axis_size("contact")
    return count if count % 2 else count // 2


def over_pairs(value):
    count = lax.axis_size("contact")
    if count & (count - 1):
        mine = (lax.axis_index("contact") & 1) == 0
        return [lax.psum(value if count % 2 else jnp.where(mine, value, 0.0), "contact")]
    stride, parts = 2, [value]
    while stride < count:
        radix = min(count // stride, 4)
        value = rounded(tree([part.astype(jnp.float32) for part in parts]))
        parts = []
        for digit in range(1, radix):
            pairs = [(place, place ^ (digit * stride) ^ 1) for place in range(count)]
            parts.append(lax.ppermute(value, "contact", pairs))
        parts.append(value)
        stride *= radix
    return parts


def project(trial, friction, contacts):
    normal = trial[:, :contacts]
    first = trial[:, contacts : 2 * contacts]
    second = trial[:, 2 * contacts :]
    tangent = jnp.sqrt(first * first + second * second)
    inside = tangent <= friction * normal
    below = friction * tangent <= -normal
    moved = (normal + friction * tangent) / (1.0 + friction * friction)
    safe = jnp.where(inside | below, 1.0, tangent)
    factor = jnp.where(inside, 1.0, jnp.where(below, 0.0, friction * moved / safe))
    new_normal = jnp.where(inside, normal, jnp.where(below, 0.0, moved))
    return jnp.concatenate([new_normal, first * factor, second * factor], axis=1)


def push_tile(tile, lam_ref, turned_ref, block_ref, sums_ref):
    blocks, dofs = sums_ref.shape[0] // 2, sums_ref.shape[1]
    row = jnp.broadcast_to(lam_ref[pl.ds(tile, 1), :], (16, lam_ref.shape[1]))
    push = jnp.dot(
        row.astype(jnp.bfloat16), turned_ref[tile], preferred_element_type=jnp.float32
    )
    sums_ref[pl.ds(block_ref[0, tile], 1), :] += push[:1, :dofs]
    sums_ref[pl.ds(blocks + block_ref[1, tile], 1), :] += push[:1, dofs:]


def first_kernel(
    count_ref, block_ref, jac_ref, start_ref, kept_ref, turned_ref, live_ref, lam_ref, sums_ref,
    block, sems, small_sems,
):
    tiles = start_ref.shape[0]
    small = [
        pltpu.make_async_copy(source, target, small_sems.at[place])
        for place, (source, target) in enumerate(
            [(block_ref, block), (start_ref, lam_ref)]
        )
    ]
    copies = [
        pltpu.make_async_copy(jac_ref.at[tile], kept_ref.at[tile], sems.at[tile])
        for tile in range(tiles)
    ]
    cuts = sorted({*range(0, tiles, GROUP), max(tiles - GROUP // 2, 0), tiles})
    started = 2 * GROUP
    for copy in small + copies[:started]:
        copy.start()
    sums_ref[...] = jnp.zeros_like(sums_ref)
    for copy in small:
        copy.wait()
    order = lax.broadcasted_iota(jnp.int32, lam_ref.shape, 0)
    live_ref[...] = jnp.where(order < count_ref[0], 1.0, 0.0)
    lam_ref[...] = lam_ref[...] * live_ref[...]
    for group in [range(first, after) for first, after in zip(cuts, cuts[1:])]:
        for tile in group:
            copies[tile].wait()
        for copy in copies[started : group[-1] + 1 + 2 * GROUP]:
            copy.start()
        started = max(started, group[-1] + 1 + 2 * GROUP)
        for tile in group:
            turned_ref[tile] = kept_ref[tile].T
        for tile in group:
            push_tile(tile, lam_ref, turned_ref, block, sums_ref)


def sweep_kernel(
    parts, block_ref, live_ref, jac_ref, turned_ref, bias_ref, step_ref, friction_ref, old_ref, *refs
):
    part_refs, (out_ref, sums_ref, vel_ref, rel_ref, lam_ref, sem) = refs[:parts], refs[parts:]
    tiles = old_ref.shape[0]
    blocks, dofs = vel_ref.shape[0] // 2, vel_ref.shape[1]
    vel_ref[...] = tree([ref[...].astype(jnp.float32) for ref in part_refs])
    sums_ref[...] = jnp.zeros_like(sums_ref)
    for tile in range(tiles):
        own_row = vel_ref[pl.ds(block_ref[0, tile], 1), :]
        next_row = vel_ref[pl.ds(blocks + block_ref[1, tile], 1), :]
        row = jnp.broadcast_to(jnp.concatenate([own_row, next_row], axis=1), (16, 2 * dofs))
        rel = jnp.dot(row.astype(jnp.bfloat16), jac_ref[tile], preferred_element_type=jnp.float32)
        rel_ref[pl.ds(tile, 1), :] = rel[:1]
    trial = old_ref[...] - step_ref[...] * (rel_ref[...] + bias_ref[...])
    lam = project(trial, friction_ref[...], friction_ref.shape[1])
    lam_ref[...] = lam * live_ref[...]
    copy = pltpu.make_async_copy(lam_ref, out_ref, sem)
    copy.start()
    for tile in range(tiles):
        push_tile(tile, lam_ref, turned_ref, block_ref, sums_ref)
    copy.wait()


GROUP = 4
LIMIT = 24 * 1024 * 1024
SMEM = pl.BlockSpec(memory_space=pltpu.SMEM)
VMEM = pl.BlockSpec(memory_space=pltpu.VMEM)


def result_shapes(lam, blocks, dofs):
    return [
        jax.ShapeDtypeStruct(lam.shape, jnp.float32),
        jax.ShapeDtypeStruct((2 * blocks, dofs), jnp.float32),
    ]


def first_push(jacobian, tile_block, tile_count, start, blocks):
    tiles, rows, cols = jacobian.shape
    lam_shape, sums_shape = result_shapes(start, blocks, rows // 2)
    held = [
        pltpu.with_memory_space_constraint(array, pltpu.HBM)
        for array in (tile_block, jacobian, start)
    ]
    return pl.pallas_call(
        first_kernel,
        out_shape=[
            pltpu.VMEM((tiles, rows, cols), jacobian.dtype),
            pltpu.VMEM((tiles, cols, rows), jacobian.dtype),
            lam_shape, lam_shape, sums_shape,
        ],
        in_specs=[SMEM] + [pl.BlockSpec(memory_space=pltpu.HBM)] * 3,
        out_specs=[VMEM] * 5,
        scratch_shapes=[
            pltpu.SMEM(tile_block.shape, jnp.int32),
            pltpu.SemaphoreType.DMA((tiles,)),
            pltpu.SemaphoreType.DMA((2,)),
        ],
        compiler_params=pltpu.CompilerParams(vmem_limit_bytes=LIMIT),
        cost_estimate=pl.CostEstimate(
            flops=2 * jacobian.size, bytes_accessed=2 * jacobian.size, transcendentals=0
        ),
        name="first_push",
    )(tile_count, *held)


def sweep_step(kept, turned, tile_block, live, bias, step, friction, lam, parts):
    rows, dofs = parts[0].shape
    kept = pltpu.with_memory_space_constraint(kept, pltpu.VMEM)
    turned = pltpu.with_memory_space_constraint(turned, pltpu.VMEM)
    return pl.pallas_call(
        functools.partial(sweep_kernel, len(parts)),
        out_shape=result_shapes(lam, rows // 2, dofs),
        in_specs=[SMEM] + [VMEM] * (7 + len(parts)),
        out_specs=[pl.BlockSpec(memory_space=pl.ANY), VMEM],
        scratch_shapes=[
            pltpu.VMEM((rows, dofs), jnp.float32),
            pltpu.VMEM(lam.shape, jnp.float32),
            pltpu.VMEM(lam.shape, jnp.float32),
            pltpu.SemaphoreType.DMA,
        ],
        compiler_params=pltpu.CompilerParams(vmem_limit_bytes=LIMIT),
        cost_estimate=pl.CostEstimate(
            flops=4 * kept.size, bytes_accessed=4 * kept.size, transcendentals=0
        ),
        name="sweep_step",
    )(tile_block, live, kept, turned, bias, step, friction, lam, *parts)


def per_device(
    jacobian, tile_block, tile_count, vel_free, inv_mass, bias, step_scale, friction, impulse_start
):
    tiles, sides, dofs, rows = jacobian.shape
    blocks = vel_free.shape[0]
    flat = jacobian.reshape(tiles, sides * dofs, rows)
    even = (lax.axis_index("body") & 1) == 0
    even, tile_block = lax.optimization_barrier((even, tile_block.T))
    kept, turned, live, lam, sums = first_push(
        flat, tile_block, tile_count, impulse_start, blocks
    )
    share, mass_next = vel_free * (1.0 / pair_count()), None
    for sweep in range(ITERS):
        both = pair_sum(sums)
        own, later = both[:blocks], both[blocks:]
        extra = [rounded(inv_mass)] if mass_next is None else []
        from_last, from_next = traded(
            rounded(later), rounded(share + inv_mass * own), even, *extra
        )
        if mass_next is None:
            mass_next = from_next[blocks:].astype(jnp.float32)
        parts = over_pairs(
            jnp.concatenate(
                [share + inv_mass * (own + from_last), from_next[:blocks] + mass_next * later]
            )
        )
        lam, sums = sweep_step(
            kept, turned, tile_block, live, bias, step_scale, friction, lam, parts
        )
    both = pair_sum(sums)
    from_last = crossed(rounded(both[blocks:]), ahead_of)
    total = tree([part.astype(jnp.float32) for part in over_pairs(both[:blocks] + from_last)])
    velocity = vel_free + inv_mass * total
    return (lam, velocity)


def solution(mesh):
    placed = (
        P(("contact", "body"), None, None, None),
        P(("contact", "body"), None),
        P(("contact", "body")),
        P("body", None),
        P("body", None),
        P(("contact", "body"), None),
        P(("contact", "body"), None),
        P(("contact", "body"), None),
        P(("contact", "body"), None),
    )
    return jax.shard_map(
        per_device,
        mesh=mesh,
        in_specs=placed,
        out_specs=(P(("contact", "body"), None), P("body", None)),
        check_vma=False,
    )
```

profile of v0, /device:TPU:0, one launch (start us, length us, event | category | flops | bytes accessed | tf_op | source)
XLA Modules:
  0.0 55.9 jit_solution(14886765686838355158)
XLA Ops:
  0.6 0.0 copy-start.3
  0.6 0.0 copy-start.4
  0.7 0.0 copy-start.5
  0.7 0.0 copy-start.2
  0.7 0.0 copy-start.1
  0.7 0.0 copy-start
  1.4 5.6 %first_push.1 = (bf16[16,768,384]{2,1,0:T(8,128)(2,1)S(1)}, bf16[16,384,768]{2,1,0:T(8,128)(2,1)S(1)}, f32[16,384]{1,0:T(8,128)S(1)}, f32[16,384]{1,0:T(8,128)S(1)}, f32[64,384]{1,0:T(8,128)S(1)}) custom-call(s32[1]{0:T(128)S(6)} %copy.11.count_ref, s32[2,16]{1,0:T(2,128)} %bitcast.2, bf16[16,768,384]{2,1,0:T(8,128)(2,1)} %bitcast.5, f32[16,384]{1,0:T(8,128)} %start_ref.1), custom_call_target="tpu_custom_call" | custom-call | flops 9437184 | bytes 9437184 | tf_op jit(solution)/shard_map/first_push/pallas_call | solution.py:186
  6.9 0.5 collective-permute-start
  7.4 0.0 copy-done.4
  7.5 0.9 %collective-permute-done = f32[64,384]{1,0:T(8,128)S(1)} collective-permute-done((f32[64,384]{1,0:T(8,128)S(1)}, f32[64,384]{1,0:T(8,128)S(1)}, u32[]{:S(2)}, u32[]{:S(2)}) %collective-permute-start) | collective-permute-done | bytes 98336 | tf_op jit(solution)/shard_map/ppermute | solution.py:55
  8.4 0.0 copy-done.5
  8.5 4.8 %collective-permute-start.1 = (bf16[64,384]{1,0:T(8,128)(2,1)S(1)}, bf16[64,384]{1,0:T(8,128)(2,1)S(1)}, u32[]{:S(2)}, u32[]{:S(2)}) collective-permute-start(bf16[64,384]{1,0:T(8,128)(2,1)S(1)} %get-tuple-element.24), channel_id=1, source_target_pairs={{0,7},{1,6},{2,5},{3,4},{4,3},{5,2},{6,1},{7,0},{8,15},{9,14},{10,... | collective-permute-start | bytes 147464 | tf_op jit(solution)/shard_map/ppermute | solution.py:21
  13.3 0.0 collective-permute-start.2
  13.3 2.1 %collective-permute-done.1 = bf16[64,384]{1,0:T(8,128)(2,1)S(1)} collective-permute-done((bf16[64,384]{1,0:T(8,128)(2,1)S(1)}, bf16[64,384]{1,0:T(8,128)(2,1)S(1)}, u32[]{:S(2)}, u32[]{:S(2)}) %collective-permute-start.1) | collective-permute-done | bytes 49184 | tf_op jit(solution)/shard_map/ppermute | solution.py:21
  15.4 1.4 %collective-permute-done.2 = bf16[64,384]{1,0:T(8,128)(2,1)S(1)} collective-permute-done((bf16[64,384]{1,0:T(8,128)(2,1)S(1)}, bf16[64,384]{1,0:T(8,128)(2,1)S(1)}, u32[]{:S(2)}, u32[]{:S(2)}) %collective-permute-start.2) | collective-permute-done | bytes 49184 | tf_op jit(solution)/shard_map/ppermute | solution.py:21
  16.9 2.5 %collective-permute-start.5 = (bf16[64,384]{1,0:T(8,128)(2,1)S(1)}, bf16[64,384]{1,0:T(8,128)(2,1)S(1)}, u32[]{:S(2)}, u32[]{:S(2)}) collective-permute-start(bf16[64,384]{1,0:T(8,128)(2,1)S(1)} %pad_maximum_fusion.2.refs_3_), channel_id=1, source_target_pairs={{0,28},{4,24},{8,20},{12,16},{16,12},{20,8},{24,4},{28,0},{1,29},{... | collective-permute-start | bytes 147464 | tf_op jit(solution)/shard_map/ppermute | solution.py:75
  19.3 0.3 collective-permute-start.4
  19.6 0.5 collective-permute-start.3
  20.1 1.3 %collective-permute-done.5.refs_2_ = bf16[64,384]{1,0:T(8,128)(2,1)S(1)} collective-permute-done((bf16[64,384]{1,0:T(8,128)(2,1)S(1)}, bf16[64,384]{1,0:T(8,128)(2,1)S(1)}, u32[]{:S(2)}, u32[]{:S(2)}) %collective-permute-start.5) | collective-permute-done | bytes 49184 | tf_op jit(solution)/shard_map/ppermute | solution.py:75
  21.3 1.7 %collective-permute-done.4.refs_1_ = bf16[64,384]{1,0:T(8,128)(2,1)S(1)} collective-permute-done((bf16[64,384]{1,0:T(8,128)(2,1)S(1)}, bf16[64,384]{1,0:T(8,128)(2,1)S(1)}, u32[]{:S(2)}, u32[]{:S(2)}) %collective-permute-start.4) | collective-permute-done | bytes 49184 | tf_op jit(solution)/shard_map/ppermute | solution.py:75
  23.0 0.1 collective-permute-done.3.refs_0_
  23.1 0.0 copy-done.3
  23.1 0.0 copy-done.2
  23.1 0.0 copy-done.1
  23.1 0.0 copy-done
  23.1 3.3 %sweep_step.2 = (f32[16,384]{1,0:T(8,128)S(1)}, f32[64,384]{1,0:T(8,128)S(1)}) custom-call(s32[2,16]{1,0:T(2,128)S(1)} %bitcast.3, f32[16,384]{1,0:T(8,128)S(1)} %get-tuple-element.18.live_ref, bf16[16,768,384]{2,1,0:T(8,128)(2,1)S(1)} %get-tuple-element.19.jac_ref, bf16[16,384,768]{2,1,0:T(8,128)(2,1)S(1)} %get-tuple-element.20.turned_ref, ...), custom_call_target="tpu_custom_call" | custom-call | flops 18874368 | bytes 18874368 | tf_op jit(solution)/shard_map/sweep_step/pallas_call | solution.py:212
  26.5 0.4 collective-permute-start.6
  26.9 1.0 %collective-permute-done.6 = f32[64,384]{1,0:T(8,128)S(1)} collective-permute-done((f32[64,384]{1,0:T(8,128)S(1)}, f32[64,384]{1,0:T(8,128)S(1)}, u32[]{:S(2)}, u32[]{:S(2)}) %collective-permute-start.6) | collective-permute-done | bytes 98336 | tf_op jit(solution)/shard_map/ppermute | solution.py:55
  27.9 2.4 %collective-permute-start.7 = (bf16[32,384]{1,0:T(8,128)(2,1)S(1)}, bf16[32,384]{1,0:T(8,128)(2,1)S(1)}, u32[]{:S(2)}, u32[]{:S(2)}) collective-permute-start(bf16[32,384]{1,0:T(8,128)(2,1)S(1)} %broadcast_select_fusion.2), channel_id=1, source_target_pairs={{0,7},{1,6},{2,5},{3,4},{4,3},{5,2},{6,1},{7,0},{8,15},{9,14},{10,... | collective-permute-start | bytes 73736 | tf_op jit(solution)/shard_map/ppermute | solution.py:21
  30.3 0.0 collective-permute-start.8
  30.3 2.7 %collective-permute-done.7 = bf16[32,384]{1,0:T(8,128)(2,1)S(1)} collective-permute-done((bf16[32,384]{1,0:T(8,128)(2,1)S(1)}, bf16[32,384]{1,0:T(8,128)(2,1)S(1)}, u32[]{:S(2)}, u32[]{:S(2)}) %collective-permute-start.7) | collective-permute-done | bytes 24608 | tf_op jit(solution)/shard_map/ppermute | solution.py:21
  33.0 0.8 %collective-permute-done.8 = bf16[32,384]{1,0:T(8,128)(2,1)S(1)} collective-permute-done((bf16[32,384]{1,0:T(8,128)(2,1)S(1)}, bf16[32,384]{1,0:T(8,128)(2,1)S(1)}, u32[]{:S(2)}, u32[]{:S(2)}) %collective-permute-start.8) | collective-permute-done | bytes 24608 | tf_op jit(solution)/shard_map/ppermute | solution.py:21
  33.9 1.3 %collective-permute-start.11 = (bf16[64,384]{1,0:T(8,128)(2,1)S(1)}, bf16[64,384]{1,0:T(8,128)(2,1)S(1)}, u32[]{:S(2)}, u32[]{:S(2)}) collective-permute-start(bf16[64,384]{1,0:T(8,128)(2,1)S(1)} %pad_maximum_fusion.3.refs_3_), channel_id=1, source_target_pairs={{0,28},{4,24},{8,20},{12,16},{16,12},{20,8},{24,4},{28,0},{1,29},{... | collective-permute-start | bytes 147464 | tf_op jit(solution)/shard_map/ppermute | solution.py:75
  35.2 1.0 %collective-permute-start.10 = (bf16[64,384]{1,0:T(8,128)(2,1)S(1)}, bf16[64,384]{1,0:T(8,128)(2,1)S(1)}, u32[]{:S(2)}, u32[]{:S(2)}) collective-permute-start(bf16[64,384]{1,0:T(8,128)(2,1)S(1)} %pad_maximum_fusion.3.refs_3_), channel_id=1, source_target_pairs={{0,20},{4,16},{8,28},{12,24},{16,4},{20,0},{24,12},{28,8},{1,21},{... | collective-permute-start | bytes 147464 | tf_op jit(solution)/shard_map/ppermute | solution.py:75
  36.2 0.7 %collective-permute-start.9 = (bf16[64,384]{1,0:T(8,128)(2,1)S(1)}, bf16[64,384]{1,0:T(8,128)(2,1)S(1)}, u32[]{:S(2)}, u32[]{:S(2)}) collective-permute-start(bf16[64,384]{1,0:T(8,128)(2,1)S(1)} %pad_maximum_fusion.3.refs_3_), channel_id=1, source_target_pairs={{0,12},{4,8},{8,4},{12,0},{16,28},{20,24},{24,20},{28,16},{1,13},{... | collective-permute-start | bytes 147464 | tf_op jit(solution)/shard_map/ppermute | solution.py:75
  36.9 1.8 %collective-permute-done.11.refs_2_ = bf16[64,384]{1,0:T(8,128)(2,1)S(1)} collective-permute-done((bf16[64,384]{1,0:T(8,128)(2,1)S(1)}, bf16[64,384]{1,0:T(8,128)(2,1)S(1)}, u32[]{:S(2)}, u32[]{:S(2)}) %collective-permute-start.11) | collective-permute-done | bytes 49184 | tf_op jit(solution)/shard_map/ppermute | solution.py:75
  38.7 1.2 %collective-permute-done.10.refs_1_ = bf16[64,384]{1,0:T(8,128)(2,1)S(1)} collective-permute-done((bf16[64,384]{1,0:T(8,128)(2,1)S(1)}, bf16[64,384]{1,0:T(8,128)(2,1)S(1)}, u32[]{:S(2)}, u32[]{:S(2)}) %collective-permute-start.10) | collective-permute-done | bytes 49184 | tf_op jit(solution)/shard_map/ppermute | solution.py:75
  39.9 0.1 collective-permute-done.9.refs_0_
  40.0 3.3 %sweep_step.3 = (f32[16,384]{1,0:T(8,128)}, f32[64,384]{1,0:T(8,128)S(1)}) custom-call(s32[2,16]{1,0:T(2,128)S(1)} %bitcast.4, f32[16,384]{1,0:T(8,128)S(1)} %get-tuple-element.18.live_ref, bf16[16,768,384]{2,1,0:T(8,128)(2,1)S(1)} %get-tuple-element.19.jac_ref, bf16[16,384,768]{2,1,0:T(8,128)(2,1)S(1)} %get-tuple-element.20.turned_ref, ...), custom_call_target="tpu_custom_call" | custom-call | flops 18874368 | bytes 18874368 | tf_op jit(solution)/shard_map/sweep_step/pallas_call | solution.py:212
  43.3 0.2 collective-permute-start.12
  43.5 1.2 %collective-permute-done.12 = f32[64,384]{1,0:T(8,128)S(1)} collective-permute-done((f32[64,384]{1,0:T(8,128)S(1)}, f32[64,384]{1,0:T(8,128)S(1)}, u32[]{:S(2)}, u32[]{:S(2)}) %collective-permute-start.12) | collective-permute-done | bytes 98336 | tf_op jit(solution)/shard_map/ppermute | solution.py:55
  44.7 0.1 collective-permute-start.13
  44.8 5.0 %collective-permute-done.13 = bf16[32,384]{1,0:T(8,128)(2,1)S(1)} collective-permute-done((bf16[32,384]{1,0:T(8,128)(2,1)S(1)}, bf16[32,384]{1,0:T(8,128)(2,1)S(1)}, u32[]{:S(2)}, u32[]{:S(2)}) %collective-permute-start.13) | collective-permute-done | bytes 24608 | tf_op jit(solution)/shard_map/ppermute | solution.py:21
  49.8 1.8 %collective-permute-start.16 = (bf16[32,384]{1,0:T(8,128)(2,1)S(1)}, bf16[32,384]{1,0:T(8,128)(2,1)S(1)}, u32[]{:S(2)}, u32[]{:S(2)}) collective-permute-start(bf16[32,384]{1,0:T(8,128)(2,1)S(1)} %fusion.4), channel_id=1, source_target_pairs={{0,28},{4,24},{8,20},{12,16},{16,12},{20,8},{24,4},{28,0},{1,29},{... | collective-permute-start | bytes 73736 | tf_op jit(solution)/shard_map/ppermute | solution.py:75
  51.6 0.4 collective-permute-start.15
  52.0 0.8 %collective-permute-start.14 = (bf16[32,384]{1,0:T(8,128)(2,1)S(1)}, bf16[32,384]{1,0:T(8,128)(2,1)S(1)}, u32[]{:S(2)}, u32[]{:S(2)}) collective-permute-start(bf16[32,384]{1,0:T(8,128)(2,1)S(1)} %fusion.4), channel_id=1, source_target_pairs={{0,12},{4,8},{8,4},{12,0},{16,28},{20,24},{24,20},{28,16},{1,13},{... | collective-permute-start | bytes 73736 | tf_op jit(solution)/shard_map/ppermute | solution.py:75
  52.8 1.2 %collective-permute-done.16 = bf16[32,384]{1,0:T(8,128)(2,1)S(1)} collective-permute-done((bf16[32,384]{1,0:T(8,128)(2,1)S(1)}, bf16[32,384]{1,0:T(8,128)(2,1)S(1)}, u32[]{:S(2)}, u32[]{:S(2)}) %collective-permute-start.16) | collective-permute-done | bytes 24608 | tf_op jit(solution)/shard_map/ppermute | solution.py:75
  54.0 0.8 %collective-permute-done.15 = bf16[32,384]{1,0:T(8,128)(2,1)S(1)} collective-permute-done((bf16[32,384]{1,0:T(8,128)(2,1)S(1)}, bf16[32,384]{1,0:T(8,128)(2,1)S(1)}, u32[]{:S(2)}, u32[]{:S(2)}) %collective-permute-start.15) | collective-permute-done | bytes 24608 | tf_op jit(solution)/shard_map/ppermute | solution.py:75
  54.8 0.4 collective-permute-done.14
  55.3 0.6 %multiply_add_fusion = f32[32,384]{1,0:T(8,128)} fusion(f32[32,384]{1,0:T(8,128)S(1)} %copy-done.5, f32[32,384]{1,0:T(8,128)S(1)} %copy-done.4, bf16[32,384]{1,0:T(8,128)(2,1)S(1)} %fusion.4, bf16[32,384]{1,0:T(8,128)(2,1)S(1)} %collective-permute-done.16, bf16[32,384]{1,0:T(8,128)(2,1)S(1)} %collective-permute-done.15, ...), kind=kLoop, calls=%fused_computation.13 | loop fusion | flops 110592 | bytes 245760 | tf_op jit(solution)/shard_map/add | solution.py:263
  (16 shorter events, 0.2 us)
Async XLA Ops:
  0.6 22.5 %copy-start.3 = (s32[16,2]{0,1:T(2,128)S(1)}, s32[16,2]{0,1:T(2,128)}, u32[]{:S(2)}) copy-start(s32[16,2]{0,1:T(2,128)} %param.10) | copy-start | bytes 388
  0.6 6.8 %copy-start.4 = (f32[32,384]{1,0:T(8,128)S(1)}, f32[32,384]{1,0:T(8,128)}, u32[]{:S(2)}) copy-start(f32[32,384]{1,0:T(8,128)} %param.13) | copy-start | bytes 147460
  0.7 7.8 %copy-start.5 = (f32[32,384]{1,0:T(8,128)S(1)}, f32[32,384]{1,0:T(8,128)}, u32[]{:S(2)}) copy-start(f32[32,384]{1,0:T(8,128)} %param.12) | copy-start | bytes 147460
  0.7 22.4 %copy-start.2 = (f32[16,128]{1,0:T(8,128)S(1)}, f32[16,128]{1,0:T(8,128)}, u32[]{:S(2)}) copy-start(f32[16,128]{1,0:T(8,128)} %friction_ref.3) | copy-start | bytes 24580
  0.7 22.4 %copy-start.1 = (f32[16,384]{1,0:T(8,128)S(1)}, f32[16,384]{1,0:T(8,128)}, u32[]{:S(2)}) copy-start(f32[16,384]{1,0:T(8,128)} %step_ref.3) | copy-start | bytes 73732
  0.7 22.4 %copy-start = (f32[16,384]{1,0:T(8,128)S(1)}, f32[16,384]{1,0:T(8,128)}, u32[]{:S(2)}) copy-start(f32[16,384]{1,0:T(8,128)} %bias_ref.3) | copy-start | bytes 73732
  6.9 1.5 %collective-permute-start = (f32[64,384]{1,0:T(8,128)S(1)}, f32[64,384]{1,0:T(8,128)S(1)}, u32[]{:S(2)}, u32[]{:S(2)}) collective-permute-start(f32[64,384]{1,0:T(8,128)S(1)} %get-tuple-element.22), channel_id=1, source_target_pairs={{0,4},{4,0},{8,12},{12,8},{16,20},{20,16},{24,28},{28,24},{1,5},{5... | collective-permute-start | bytes 294920 | tf_op jit(solution)/shard_map/ppermute | solution.py:55
  8.5 6.9 %collective-permute-start.1 = (bf16[64,384]{1,0:T(8,128)(2,1)S(1)}, bf16[64,384]{1,0:T(8,128)(2,1)S(1)}, u32[]{:S(2)}, u32[]{:S(2)}) collective-permute-start(bf16[64,384]{1,0:T(8,128)(2,1)S(1)} %get-tuple-element.24), channel_id=1, source_target_pairs={{0,7},{1,6},{2,5},{3,4},{4,3},{5,2},{6,1},{7,0},{8,15},{9,14},{10,... | collective-permute-start | bytes 147464 | tf_op jit(solution)/shard_map/ppermute | solution.py:21
  13.3 3.5 %collective-permute-start.2 = (bf16[64,384]{1,0:T(8,128)(2,1)S(1)}, bf16[64,384]{1,0:T(8,128)(2,1)S(1)}, u32[]{:S(2)}, u32[]{:S(2)}) collective-permute-start(bf16[64,384]{1,0:T(8,128)(2,1)S(1)} %get-tuple-element.25), channel_id=1, source_target_pairs={{0,5},{1,4},{2,7},{3,6},{4,1},{5,0},{6,3},{7,2},{8,13},{9,12},{10,... | collective-permute-start | bytes 147464 | tf_op jit(solution)/shard_map/ppermute | solution.py:21
  16.9 4.5 %collective-permute-start.5 = (bf16[64,384]{1,0:T(8,128)(2,1)S(1)}, bf16[64,384]{1,0:T(8,128)(2,1)S(1)}, u32[]{:S(2)}, u32[]{:S(2)}) collective-permute-start(bf16[64,384]{1,0:T(8,128)(2,1)S(1)} %pad_maximum_fusion.2.refs_3_), channel_id=1, source_target_pairs={{0,28},{4,24},{8,20},{12,16},{16,12},{20,8},{24,4},{28,0},{1,29},{... | collective-permute-start | bytes 147464 | tf_op jit(solution)/shard_map/ppermute | solution.py:75
  19.3 3.7 %collective-permute-start.4 = (bf16[64,384]{1,0:T(8,128)(2,1)S(1)}, bf16[64,384]{1,0:T(8,128)(2,1)S(1)}, u32[]{:S(2)}, u32[]{:S(2)}) collective-permute-start(bf16[64,384]{1,0:T(8,128)(2,1)S(1)} %pad_maximum_fusion.2.refs_3_), channel_id=1, source_target_pairs={{0,20},{4,16},{8,28},{12,24},{16,4},{20,0},{24,12},{28,8},{1,21},{... | collective-permute-start | bytes 147464 | tf_op jit(solution)/shard_map/ppermute | solution.py:75
  19.6 3.5 %collective-permute-start.3 = (bf16[64,384]{1,0:T(8,128)(2,1)S(1)}, bf16[64,384]{1,0:T(8,128)(2,1)S(1)}, u32[]{:S(2)}, u32[]{:S(2)}) collective-permute-start(bf16[64,384]{1,0:T(8,128)(2,1)S(1)} %pad_maximum_fusion.2.refs_3_), channel_id=1, source_target_pairs={{0,12},{4,8},{8,4},{12,0},{16,28},{20,24},{24,20},{28,16},{1,13},{... | collective-permute-start | bytes 147464 | tf_op jit(solution)/shard_map/ppermute | solution.py:75
  26.5 1.4 %collective-permute-start.6 = (f32[64,384]{1,0:T(8,128)S(1)}, f32[64,384]{1,0:T(8,128)S(1)}, u32[]{:S(2)}, u32[]{:S(2)}) collective-permute-start(f32[64,384]{1,0:T(8,128)S(1)} %get-tuple-element.27), channel_id=1, source_target_pairs={{0,4},{4,0},{8,12},{12,8},{16,20},{20,16},{24,28},{28,24},{1,5},{5... | collective-permute-start | bytes 294920 | tf_op jit(solution)/shard_map/ppermute | solution.py:55
  27.9 5.1 %collective-permute-start.7 = (bf16[32,384]{1,0:T(8,128)(2,1)S(1)}, bf16[32,384]{1,0:T(8,128)(2,1)S(1)}, u32[]{:S(2)}, u32[]{:S(2)}) collective-permute-start(bf16[32,384]{1,0:T(8,128)(2,1)S(1)} %broadcast_select_fusion.2), channel_id=1, source_target_pairs={{0,7},{1,6},{2,5},{3,4},{4,3},{5,2},{6,1},{7,0},{8,15},{9,14},{10,... | collective-permute-start | bytes 73736 | tf_op jit(solution)/shard_map/ppermute | solution.py:21
  30.3 3.6 %collective-permute-start.8 = (bf16[32,384]{1,0:T(8,128)(2,1)S(1)}, bf16[32,384]{1,0:T(8,128)(2,1)S(1)}, u32[]{:S(2)}, u32[]{:S(2)}) collective-permute-start(bf16[32,384]{1,0:T(8,128)(2,1)S(1)} %get-tuple-element.29), channel_id=1, source_target_pairs={{0,5},{1,4},{2,7},{3,6},{4,1},{5,0},{6,3},{7,2},{8,13},{9,12},{10,... | collective-permute-start | bytes 73736 | tf_op jit(solution)/shard_map/ppermute | solution.py:21
  33.9 4.8 %collective-permute-start.11 = (bf16[64,384]{1,0:T(8,128)(2,1)S(1)}, bf16[64,384]{1,0:T(8,128)(2,1)S(1)}, u32[]{:S(2)}, u32[]{:S(2)}) collective-permute-start(bf16[64,384]{1,0:T(8,128)(2,1)S(1)} %pad_maximum_fusion.3.refs_3_), channel_id=1, source_target_pairs={{0,28},{4,24},{8,20},{12,16},{16,12},{20,8},{24,4},{28,0},{1,29},{... | collective-permute-start | bytes 147464 | tf_op jit(solution)/shard_map/ppermute | solution.py:75
  35.2 4.7 %collective-permute-start.10 = (bf16[64,384]{1,0:T(8,128)(2,1)S(1)}, bf16[64,384]{1,0:T(8,128)(2,1)S(1)}, u32[]{:S(2)}, u32[]{:S(2)}) collective-permute-start(bf16[64,384]{1,0:T(8,128)(2,1)S(1)} %pad_maximum_fusion.3.refs_3_), channel_id=1, source_target_pairs={{0,20},{4,16},{8,28},{12,24},{16,4},{20,0},{24,12},{28,8},{1,21},{... | collective-permute-start | bytes 147464 | tf_op jit(solution)/shard_map/ppermute | solution.py:75
  36.2 3.8 %collective-permute-start.9 = (bf16[64,384]{1,0:T(8,128)(2,1)S(1)}, bf16[64,384]{1,0:T(8,128)(2,1)S(1)}, u32[]{:S(2)}, u32[]{:S(2)}) collective-permute-start(bf16[64,384]{1,0:T(8,128)(2,1)S(1)} %pad_maximum_fusion.3.refs_3_), channel_id=1, source_target_pairs={{0,12},{4,8},{8,4},{12,0},{16,28},{20,24},{24,20},{28,16},{1,13},{... | collective-permute-start | bytes 147464 | tf_op jit(solution)/shard_map/ppermute | solution.py:75
  43.3 1.4 %collective-permute-start.12 = (f32[64,384]{1,0:T(8,128)S(1)}, f32[64,384]{1,0:T(8,128)S(1)}, u32[]{:S(2)}, u32[]{:S(2)}) collective-permute-start(f32[64,384]{1,0:T(8,128)S(1)} %get-tuple-element.31), channel_id=1, source_target_pairs={{0,4},{4,0},{8,12},{12,8},{16,20},{20,16},{24,28},{28,24},{1,5},{5... | collective-permute-start | bytes 294920 | tf_op jit(solution)/shard_map/ppermute | solution.py:55
  44.7 5.1 %collective-permute-start.13 = (bf16[32,384]{1,0:T(8,128)(2,1)S(1)}, bf16[32,384]{1,0:T(8,128)(2,1)S(1)}, u32[]{:S(2)}, u32[]{:S(2)}) collective-permute-start(bf16[32,384]{1,0:T(8,128)(2,1)S(1)} %slice.78), channel_id=1, source_target_pairs={{0,5},{1,6},{2,7},{3,4},{4,1},{5,2},{6,3},{7,0},{8,13},{9,14},{10,... | collective-permute-start | bytes 73736 | tf_op jit(solution)/shard_map/ppermute | solution.py:21
  49.8 4.2 %collective-permute-start.16 = (bf16[32,384]{1,0:T(8,128)(2,1)S(1)}, bf16[32,384]{1,0:T(8,128)(2,1)S(1)}, u32[]{:S(2)}, u32[]{:S(2)}) collective-permute-start(bf16[32,384]{1,0:T(8,128)(2,1)S(1)} %fusion.4), channel_id=1, source_target_pairs={{0,28},{4,24},{8,20},{12,16},{16,12},{20,8},{24,4},{28,0},{1,29},{... | collective-permute-start | bytes 73736 | tf_op jit(solution)/shard_map/ppermute | solution.py:75
  51.6 3.3 %collective-permute-start.15 = (bf16[32,384]{1,0:T(8,128)(2,1)S(1)}, bf16[32,384]{1,0:T(8,128)(2,1)S(1)}, u32[]{:S(2)}, u32[]{:S(2)}) collective-permute-start(bf16[32,384]{1,0:T(8,128)(2,1)S(1)} %fusion.4), channel_id=1, source_target_pairs={{0,20},{4,16},{8,28},{12,24},{16,4},{20,0},{24,12},{28,8},{1,21},{... | collective-permute-start | bytes 73736 | tf_op jit(solution)/shard_map/ppermute | solution.py:75
  52.0 3.3 %collective-permute-start.14 = (bf16[32,384]{1,0:T(8,128)(2,1)S(1)}, bf16[32,384]{1,0:T(8,128)(2,1)S(1)}, u32[]{:S(2)}, u32[]{:S(2)}) collective-permute-start(bf16[32,384]{1,0:T(8,128)(2,1)S(1)} %fusion.4), channel_id=1, source_target_pairs={{0,12},{4,8},{8,4},{12,0},{16,28},{20,24},{24,20},{28,16},{1,13},{... | collective-permute-start | bytes 73736 | tf_op jit(solution)/shard_map/ppermute | solution.py:75
where the time goes:
time: 56.1 us; the launch traced here: 55.9 us
  waiting for transfers between devices  23.7 us (42%)
  starting transfers between devices  17.7 us (32%)
  Pallas kernels  12.2 us (22%)
  between operations  1.48 us (3%)
  other arithmetic  0.85 us (2%)
    ppermute x5, waiting for transfers between devices, crossed(): return lax.ppermute(value, ('contact', 'body'), pairs)  12.1 us
    ppermute x9, starting transfers between devices, over_pairs(): parts.append(lax.ppermute(value, 'contact', pairs))  9.26 us
    ppermute x9, waiting for transfers between devices, over_pairs(): parts.append(lax.ppermute(value, 'contact', pairs))  8.57 us
    ppermute x5, starting transfers between devices, crossed(): return lax.ppermute(value, ('contact', 'body'), pairs)  7.29 us
    pallas_call x2, Pallas kernels, sweep_step(): pl.pallas_call(functools.partial(sweep_kernel, len(parts)), out_shape=res...  6.6 us
    pallas_call x1, Pallas kernels, first_push(): pl.pallas_call(first_kernel, out_shape=[pltpu.VMEM((tiles, rows, cols), j...  5.57 us
    ppermute x3, waiting for transfers between devices, pair_sum(): lax.ppermute(value, 'contact', [(place, place ^ 1) for place in range(cou...  3.07 us
  transfers between devices with their start and end apart: 17, of which 17 were waited for; matrix products, arithmetic and copies ran while one was open for 0% of the time, Pallas kernels for 0%

commit v1 on v0

--- a/solution.py
+++ b/solution.py
@@ -117,7 +117,7 @@
         pltpu.make_async_copy(jac_ref.at[tile], kept_ref.at[tile], sems.at[tile])
         for tile in range(tiles)
     ]
-    cuts = sorted({*range(0, tiles, GROUP), max(tiles - GROUP // 2, 0), tiles})
+    groups = [range(first, min(first + GROUP, tiles)) for first in range(0, tiles, GROUP)]
     started = 2 * GROUP
     for copy in small + copies[:started]:
         copy.start()
@@ -127,15 +127,15 @@
     order = lax.broadcasted_iota(jnp.int32, lam_ref.shape, 0)
     live_ref[...] = jnp.where(order < count_ref[0], 1.0, 0.0)
     lam_ref[...] = lam_ref[...] * live_ref[...]
-    for group in [range(first, after) for first, after in zip(cuts, cuts[1:])]:
+    for group, before in zip(groups + [[]], [[]] + groups):
         for tile in group:
             copies[tile].wait()
-        for copy in copies[started : group[-1] + 1 + 2 * GROUP]:
+        for copy in copies[started : started + len(group)]:
             copy.start()
-        started = max(started, group[-1] + 1 + 2 * GROUP)
+        started += len(group)
         for tile in group:
             turned_ref[tile] = kept_ref[tile].T
-        for tile in group:
+        for tile in before:
             push_tile(tile, lam_ref, turned_ref, block, sums_ref)
 
 

time: 56.1 us -> 55.9 us (level)
  no operation moved by 1% of the time
where the time goes in v1:
time: 55.9 us; the launch traced here: 55.7 us
  waiting for transfers between devices  23.7 us (42%)
  starting transfers between devices  17.7 us (32%)
  Pallas kernels  12 us (21%)
  between operations  1.48 us (3%)
  other arithmetic  0.85 us (2%)
    ppermute x5, waiting for transfers between devices, crossed(): return lax.ppermute(value, ('contact', 'body'), pairs)  12.1 us
    ppermute x9, starting transfers between devices, over_pairs(): parts.append(lax.ppermute(value, 'contact', pairs))  9.26 us
    ppermute x9, waiting for transfers between devices, over_pairs(): parts.append(lax.ppermute(value, 'contact', pairs))  8.57 us
    ppermute x5, starting transfers between devices, crossed(): return lax.ppermute(value, ('contact', 'body'), pairs)  7.29 us
    pallas_call x2, Pallas kernels, sweep_step(): pl.pallas_call(functools.partial(sweep_kernel, len(parts)), out_shape=res...  6.6 us
    pallas_call x1, Pallas kernels, first_push(): pl.pallas_call(first_kernel, out_shape=[pltpu.VMEM((tiles, rows, cols), j...  5.41 us
    ppermute x3, waiting for transfers between devices, pair_sum(): lax.ppermute(value, 'contact', [(place, place ^ 1) for place in range(cou...  3.07 us
  transfers between devices with their start and end apart: 17, of which 17 were waited for; matrix products, arithmetic and copies ran while one was open for 0% of the time, Pallas kernels for 0%

profile of v1, /device:TPU:0, one launch (start us, length us, event | category | flops | bytes accessed | tf_op | source)
XLA Modules:
  0.0 55.7 jit_solution(14727513283466323233)
XLA Ops:
  0.6 0.0 copy-start.3
  0.6 0.0 copy-start.4
  0.7 0.0 copy-start.5
  0.7 0.0 copy-start.2
  0.7 0.0 copy-start.1
  0.7 0.0 copy-start
  1.4 5.4 %first_push.1 = (bf16[16,768,384]{2,1,0:T(8,128)(2,1)S(1)}, bf16[16,384,768]{2,1,0:T(8,128)(2,1)S(1)}, f32[16,384]{1,0:T(8,128)S(1)}, f32[16,384]{1,0:T(8,128)S(1)}, f32[64,384]{1,0:T(8,128)S(1)}) custom-call(s32[1]{0:T(128)S(6)} %copy.11.count_ref, s32[2,16]{1,0:T(2,128)} %bitcast.2, bf16[16,768,384]{2,1,0:T(8,128)(2,1)} %bitcast.5, f32[16,384]{1,0:T(8,128)} %start_ref.1), custom_call_target="tpu_custom_call" | custom-call | flops 9437184 | bytes 9437184 | tf_op jit(solution)/shard_map/first_push/pallas_call | solution.py:186
  6.8 0.5 collective-permute-start
  7.3 0.0 copy-done.4
  7.3 0.9 %collective-permute-done = f32[64,384]{1,0:T(8,128)S(1)} collective-permute-done((f32[64,384]{1,0:T(8,128)S(1)}, f32[64,384]{1,0:T(8,128)S(1)}, u32[]{:S(2)}, u32[]{:S(2)}) %collective-permute-start) | collective-permute-done | bytes 98336 | tf_op jit(solution)/shard_map/ppermute | solution.py:55
  8.2 0.0 copy-done.5
  8.3 4.8 %collective-permute-start.1 = (bf16[64,384]{1,0:T(8,128)(2,1)S(1)}, bf16[64,384]{1,0:T(8,128)(2,1)S(1)}, u32[]{:S(2)}, u32[]{:S(2)}) collective-permute-start(bf16[64,384]{1,0:T(8,128)(2,1)S(1)} %get-tuple-element.24), channel_id=1, source_target_pairs={{0,7},{1,6},{2,5},{3,4},{4,3},{5,2},{6,1},{7,0},{8,15},{9,14},{10,... | collective-permute-start | bytes 147464 | tf_op jit(solution)/shard_map/ppermute | solution.py:21
  13.1 0.0 collective-permute-start.2
  13.1 2.1 %collective-permute-done.1 = bf16[64,384]{1,0:T(8,128)(2,1)S(1)} collective-permute-done((bf16[64,384]{1,0:T(8,128)(2,1)S(1)}, bf16[64,384]{1,0:T(8,128)(2,1)S(1)}, u32[]{:S(2)}, u32[]{:S(2)}) %collective-permute-start.1) | collective-permute-done | bytes 49184 | tf_op jit(solution)/shard_map/ppermute | solution.py:21
  15.2 1.4 %collective-permute-done.2 = bf16[64,384]{1,0:T(8,128)(2,1)S(1)} collective-permute-done((bf16[64,384]{1,0:T(8,128)(2,1)S(1)}, bf16[64,384]{1,0:T(8,128)(2,1)S(1)}, u32[]{:S(2)}, u32[]{:S(2)}) %collective-permute-start.2) | collective-permute-done | bytes 49184 | tf_op jit(solution)/shard_map/ppermute | solution.py:21
  16.7 2.5 %collective-permute-start.5 = (bf16[64,384]{1,0:T(8,128)(2,1)S(1)}, bf16[64,384]{1,0:T(8,128)(2,1)S(1)}, u32[]{:S(2)}, u32[]{:S(2)}) collective-permute-start(bf16[64,384]{1,0:T(8,128)(2,1)S(1)} %pad_maximum_fusion.2.refs_3_), channel_id=1, source_target_pairs={{0,28},{4,24},{8,20},{12,16},{16,12},{20,8},{24,4},{28,0},{1,29},{... | collective-permute-start | bytes 147464 | tf_op jit(solution)/shard_map/ppermute | solution.py:75
  19.2 0.3 collective-permute-start.4
  19.4 0.5 collective-permute-start.3
  19.9 1.3 %collective-permute-done.5.refs_2_ = bf16[64,384]{1,0:T(8,128)(2,1)S(1)} collective-permute-done((bf16[64,384]{1,0:T(8,128)(2,1)S(1)}, bf16[64,384]{1,0:T(8,128)(2,1)S(1)}, u32[]{:S(2)}, u32[]{:S(2)}) %collective-permute-start.5) | collective-permute-done | bytes 49184 | tf_op jit(solution)/shard_map/ppermute | solution.py:75
  21.2 1.7 %collective-permute-done.4.refs_1_ = bf16[64,384]{1,0:T(8,128)(2,1)S(1)} collective-permute-done((bf16[64,384]{1,0:T(8,128)(2,1)S(1)}, bf16[64,384]{1,0:T(8,128)(2,1)S(1)}, u32[]{:S(2)}, u32[]{:S(2)}) %collective-permute-start.4) | collective-permute-done | bytes 49184 | tf_op jit(solution)/shard_map/ppermute | solution.py:75
  22.8 0.1 collective-permute-done.3.refs_0_
  22.9 0.0 copy-done.3
  22.9 0.0 copy-done.2
  22.9 0.0 copy-done.1
  23.0 0.0 copy-done
  23.0 3.3 %sweep_step.2 = (f32[16,384]{1,0:T(8,128)S(1)}, f32[64,384]{1,0:T(8,128)S(1)}) custom-call(s32[2,16]{1,0:T(2,128)S(1)} %bitcast.3, f32[16,384]{1,0:T(8,128)S(1)} %get-tuple-element.18.live_ref, bf16[16,768,384]{2,1,0:T(8,128)(2,1)S(1)} %get-tuple-element.19.jac_ref, bf16[16,384,768]{2,1,0:T(8,128)(2,1)S(1)} %get-tuple-element.20.turned_ref, ...), custom_call_target="tpu_custom_call" | custom-call | flops 18874368 | bytes 18874368 | tf_op jit(solution)/shard_map/sweep_step/pallas_call | solution.py:212
  26.3 0.4 collective-permute-start.6
  26.7 1.0 %collective-permute-done.6 = f32[64,384]{1,0:T(8,128)S(1)} collective-permute-done((f32[64,384]{1,0:T(8,128)S(1)}, f32[64,384]{1,0:T(8,128)S(1)}, u32[]{:S(2)}, u32[]{:S(2)}) %collective-permute-start.6) | collective-permute-done | bytes 98336 | tf_op jit(solution)/shard_map/ppermute | solution.py:55
  27.7 2.4 %collective-permute-start.7 = (bf16[32,384]{1,0:T(8,128)(2,1)S(1)}, bf16[32,384]{1,0:T(8,128)(2,1)S(1)}, u32[]{:S(2)}, u32[]{:S(2)}) collective-permute-start(bf16[32,384]{1,0:T(8,128)(2,1)S(1)} %broadcast_select_fusion.2), channel_id=1, source_target_pairs={{0,7},{1,6},{2,5},{3,4},{4,3},{5,2},{6,1},{7,0},{8,15},{9,14},{10,... | collective-permute-start | bytes 73736 | tf_op jit(solution)/shard_map/ppermute | solution.py:21
  30.1 0.0 collective-permute-start.8
  30.1 2.7 %collective-permute-done.7 = bf16[32,384]{1,0:T(8,128)(2,1)S(1)} collective-permute-done((bf16[32,384]{1,0:T(8,128)(2,1)S(1)}, bf16[32,384]{1,0:T(8,128)(2,1)S(1)}, u32[]{:S(2)}, u32[]{:S(2)}) %collective-permute-start.7) | collective-permute-done | bytes 24608 | tf_op jit(solution)/shard_map/ppermute | solution.py:21
  32.9 0.8 %collective-permute-done.8 = bf16[32,384]{1,0:T(8,128)(2,1)S(1)} collective-permute-done((bf16[32,384]{1,0:T(8,128)(2,1)S(1)}, bf16[32,384]{1,0:T(8,128)(2,1)S(1)}, u32[]{:S(2)}, u32[]{:S(2)}) %collective-permute-start.8) | collective-permute-done | bytes 24608 | tf_op jit(solution)/shard_map/ppermute | solution.py:21
  33.7 1.3 %collective-permute-start.11 = (bf16[64,384]{1,0:T(8,128)(2,1)S(1)}, bf16[64,384]{1,0:T(8,128)(2,1)S(1)}, u32[]{:S(2)}, u32[]{:S(2)}) collective-permute-start(bf16[64,384]{1,0:T(8,128)(2,1)S(1)} %pad_maximum_fusion.3.refs_3_), channel_id=1, source_target_pairs={{0,28},{4,24},{8,20},{12,16},{16,12},{20,8},{24,4},{28,0},{1,29},{... | collective-permute-start | bytes 147464 | tf_op jit(solution)/shard_map/ppermute | solution.py:75
  35.0 1.0 %collective-permute-start.10 = (bf16[64,384]{1,0:T(8,128)(2,1)S(1)}, bf16[64,384]{1,0:T(8,128)(2,1)S(1)}, u32[]{:S(2)}, u32[]{:S(2)}) collective-permute-start(bf16[64,384]{1,0:T(8,128)(2,1)S(1)} %pad_maximum_fusion.3.refs_3_), channel_id=1, source_target_pairs={{0,20},{4,16},{8,28},{12,24},{16,4},{20,0},{24,12},{28,8},{1,21},{... | collective-permute-start | bytes 147464 | tf_op jit(solution)/shard_map/ppermute | solution.py:75
  36.1 0.7 %collective-permute-start.9 = (bf16[64,384]{1,0:T(8,128)(2,1)S(1)}, bf16[64,384]{1,0:T(8,128)(2,1)S(1)}, u32[]{:S(2)}, u32[]{:S(2)}) collective-permute-start(bf16[64,384]{1,0:T(8,128)(2,1)S(1)} %pad_maximum_fusion.3.refs_3_), channel_id=1, source_target_pairs={{0,12},{4,8},{8,4},{12,0},{16,28},{20,24},{24,20},{28,16},{1,13},{... | collective-permute-start | bytes 147464 | tf_op jit(solution)/shard_map/ppermute | solution.py:75
  36.7 1.8 %collective-permute-done.11.refs_2_ = bf16[64,384]{1,0:T(8,128)(2,1)S(1)} collective-permute-done((bf16[64,384]{1,0:T(8,128)(2,1)S(1)}, bf16[64,384]{1,0:T(8,128)(2,1)S(1)}, u32[]{:S(2)}, u32[]{:S(2)}) %collective-permute-start.11) | collective-permute-done | bytes 49184 | tf_op jit(solution)/shard_map/ppermute | solution.py:75
  38.5 1.2 %collective-permute-done.10.refs_1_ = bf16[64,384]{1,0:T(8,128)(2,1)S(1)} collective-permute-done((bf16[64,384]{1,0:T(8,128)(2,1)S(1)}, bf16[64,384]{1,0:T(8,128)(2,1)S(1)}, u32[]{:S(2)}, u32[]{:S(2)}) %collective-permute-start.10) | collective-permute-done | bytes 49184 | tf_op jit(solution)/shard_map/ppermute | solution.py:75
  39.7 0.1 collective-permute-done.9.refs_0_
  39.8 3.3 %sweep_step.3 = (f32[16,384]{1,0:T(8,128)}, f32[64,384]{1,0:T(8,128)S(1)}) custom-call(s32[2,16]{1,0:T(2,128)S(1)} %bitcast.4, f32[16,384]{1,0:T(8,128)S(1)} %get-tuple-element.18.live_ref, bf16[16,768,384]{2,1,0:T(8,128)(2,1)S(1)} %get-tuple-element.19.jac_ref, bf16[16,384,768]{2,1,0:T(8,128)(2,1)S(1)} %get-tuple-element.20.turned_ref, ...), custom_call_target="tpu_custom_call" | custom-call | flops 18874368 | bytes 18874368 | tf_op jit(solution)/shard_map/sweep_step/pallas_call | solution.py:212
  43.1 0.2 collective-permute-start.12
  43.3 1.2 %collective-permute-done.12 = f32[64,384]{1,0:T(8,128)S(1)} collective-permute-done((f32[64,384]{1,0:T(8,128)S(1)}, f32[64,384]{1,0:T(8,128)S(1)}, u32[]{:S(2)}, u32[]{:S(2)}) %collective-permute-start.12) | collective-permute-done | bytes 98336 | tf_op jit(solution)/shard_map/ppermute | solution.py:55
  44.5 0.1 collective-permute-start.13
  44.6 5.0 %collective-permute-done.13 = bf16[32,384]{1,0:T(8,128)(2,1)S(1)} collective-permute-done((bf16[32,384]{1,0:T(8,128)(2,1)S(1)}, bf16[32,384]{1,0:T(8,128)(2,1)S(1)}, u32[]{:S(2)}, u32[]{:S(2)}) %collective-permute-start.13) | collective-permute-done | bytes 24608 | tf_op jit(solution)/shard_map/ppermute | solution.py:21
  49.6 1.8 %collective-permute-start.16 = (bf16[32,384]{1,0:T(8,128)(2,1)S(1)}, bf16[32,384]{1,0:T(8,128)(2,1)S(1)}, u32[]{:S(2)}, u32[]{:S(2)}) collective-permute-start(bf16[32,384]{1,0:T(8,128)(2,1)S(1)} %fusion.4), channel_id=1, source_target_pairs={{0,28},{4,24},{8,20},{12,16},{16,12},{20,8},{24,4},{28,0},{1,29},{... | collective-permute-start | bytes 73736 | tf_op jit(solution)/shard_map/ppermute | solution.py:75
  51.4 0.4 collective-permute-start.15
  51.9 0.8 %collective-permute-start.14 = (bf16[32,384]{1,0:T(8,128)(2,1)S(1)}, bf16[32,384]{1,0:T(8,128)(2,1)S(1)}, u32[]{:S(2)}, u32[]{:S(2)}) collective-permute-start(bf16[32,384]{1,0:T(8,128)(2,1)S(1)} %fusion.4), channel_id=1, source_target_pairs={{0,12},{4,8},{8,4},{12,0},{16,28},{20,24},{24,20},{28,16},{1,13},{... | collective-permute-start | bytes 73736 | tf_op jit(solution)/shard_map/ppermute | solution.py:75
  52.7 1.2 %collective-permute-done.16 = bf16[32,384]{1,0:T(8,128)(2,1)S(1)} collective-permute-done((bf16[32,384]{1,0:T(8,128)(2,1)S(1)}, bf16[32,384]{1,0:T(8,128)(2,1)S(1)}, u32[]{:S(2)}, u32[]{:S(2)}) %collective-permute-start.16) | collective-permute-done | bytes 24608 | tf_op jit(solution)/shard_map/ppermute | solution.py:75
  53.8 0.8 %collective-permute-done.15 = bf16[32,384]{1,0:T(8,128)(2,1)S(1)} collective-permute-done((bf16[32,384]{1,0:T(8,128)(2,1)S(1)}, bf16[32,384]{1,0:T(8,128)(2,1)S(1)}, u32[]{:S(2)}, u32[]{:S(2)}) %collective-permute-start.15) | collective-permute-done | bytes 24608 | tf_op jit(solution)/shard_map/ppermute | solution.py:75
  54.7 0.4 collective-permute-done.14
  55.1 0.6 %multiply_add_fusion = f32[32,384]{1,0:T(8,128)} fusion(f32[32,384]{1,0:T(8,128)S(1)} %copy-done.5, f32[32,384]{1,0:T(8,128)S(1)} %copy-done.4, bf16[32,384]{1,0:T(8,128)(2,1)S(1)} %fusion.4, bf16[32,384]{1,0:T(8,128)(2,1)S(1)} %collective-permute-done.16, bf16[32,384]{1,0:T(8,128)(2,1)S(1)} %collective-permute-done.15, ...), kind=kLoop, calls=%fused_computation.13 | loop fusion | flops 110592 | bytes 245760 | tf_op jit(solution)/shard_map/add | solution.py:263
  (16 shorter events, 0.2 us)
Async XLA Ops:
  0.6 22.3 %copy-start.3 = (s32[16,2]{0,1:T(2,128)S(1)}, s32[16,2]{0,1:T(2,128)}, u32[]{:S(2)}) copy-start(s32[16,2]{0,1:T(2,128)} %param.10) | copy-start | bytes 388
  0.6 6.6 %copy-start.4 = (f32[32,384]{1,0:T(8,128)S(1)}, f32[32,384]{1,0:T(8,128)}, u32[]{:S(2)}) copy-start(f32[32,384]{1,0:T(8,128)} %param.13) | copy-start | bytes 147460
  0.7 7.6 %copy-start.5 = (f32[32,384]{1,0:T(8,128)S(1)}, f32[32,384]{1,0:T(8,128)}, u32[]{:S(2)}) copy-start(f32[32,384]{1,0:T(8,128)} %param.12) | copy-start | bytes 147460
  0.7 22.3 %copy-start.2 = (f32[16,128]{1,0:T(8,128)S(1)}, f32[16,128]{1,0:T(8,128)}, u32[]{:S(2)}) copy-start(f32[16,128]{1,0:T(8,128)} %friction_ref.3) | copy-start | bytes 24580
  0.7 22.3 %copy-start.1 = (f32[16,384]{1,0:T(8,128)S(1)}, f32[16,384]{1,0:T(8,128)}, u32[]{:S(2)}) copy-start(f32[16,384]{1,0:T(8,128)} %step_ref.3) | copy-start | bytes 73732
  0.7 22.3 %copy-start = (f32[16,384]{1,0:T(8,128)S(1)}, f32[16,384]{1,0:T(8,128)}, u32[]{:S(2)}) copy-start(f32[16,384]{1,0:T(8,128)} %bias_ref.3) | copy-start | bytes 73732
  6.8 1.5 %collective-permute-start = (f32[64,384]{1,0:T(8,128)S(1)}, f32[64,384]{1,0:T(8,128)S(1)}, u32[]{:S(2)}, u32[]{:S(2)}) collective-permute-start(f32[64,384]{1,0:T(8,128)S(1)} %get-tuple-element.22), channel_id=1, source_target_pairs={{0,4},{4,0},{8,12},{12,8},{16,20},{20,16},{24,28},{28,24},{1,5},{5... | collective-permute-start | bytes 294920 | tf_op jit(solution)/shard_map/ppermute | solution.py:55
  8.3 6.9 %collective-permute-start.1 = (bf16[64,384]{1,0:T(8,128)(2,1)S(1)}, bf16[64,384]{1,0:T(8,128)(2,1)S(1)}, u32[]{:S(2)}, u32[]{:S(2)}) collective-permute-start(bf16[64,384]{1,0:T(8,128)(2,1)S(1)} %get-tuple-element.24), channel_id=1, source_target_pairs={{0,7},{1,6},{2,5},{3,4},{4,3},{5,2},{6,1},{7,0},{8,15},{9,14},{10,... | collective-permute-start | bytes 147464 | tf_op jit(solution)/shard_map/ppermute | solution.py:21
  13.1 3.5 %collective-permute-start.2 = (bf16[64,384]{1,0:T(8,128)(2,1)S(1)}, bf16[64,384]{1,0:T(8,128)(2,1)S(1)}, u32[]{:S(2)}, u32[]{:S(2)}) collective-permute-start(bf16[64,384]{1,0:T(8,128)(2,1)S(1)} %get-tuple-element.25), channel_id=1, source_target_pairs={{0,5},{1,4},{2,7},{3,6},{4,1},{5,0},{6,3},{7,2},{8,13},{9,12},{10,... | collective-permute-start | bytes 147464 | tf_op jit(solution)/shard_map/ppermute | solution.py:21
  16.7 4.5 %collective-permute-start.5 = (bf16[64,384]{1,0:T(8,128)(2,1)S(1)}, bf16[64,384]{1,0:T(8,128)(2,1)S(1)}, u32[]{:S(2)}, u32[]{:S(2)}) collective-permute-start(bf16[64,384]{1,0:T(8,128)(2,1)S(1)} %pad_maximum_fusion.2.refs_3_), channel_id=1, source_target_pairs={{0,28},{4,24},{8,20},{12,16},{16,12},{20,8},{24,4},{28,0},{1,29},{... | collective-permute-start | bytes 147464 | tf_op jit(solution)/shard_map/ppermute | solution.py:75
  19.2 3.7 %collective-permute-start.4 = (bf16[64,384]{1,0:T(8,128)(2,1)S(1)}, bf16[64,384]{1,0:T(8,128)(2,1)S(1)}, u32[]{:S(2)}, u32[]{:S(2)}) collective-permute-start(bf16[64,384]{1,0:T(8,128)(2,1)S(1)} %pad_maximum_fusion.2.refs_3_), channel_id=1, source_target_pairs={{0,20},{4,16},{8,28},{12,24},{16,4},{20,0},{24,12},{28,8},{1,21},{... | collective-permute-start | bytes 147464 | tf_op jit(solution)/shard_map/ppermute | solution.py:75
  19.4 3.5 %collective-permute-start.3 = (bf16[64,384]{1,0:T(8,128)(2,1)S(1)}, bf16[64,384]{1,0:T(8,128)(2,1)S(1)}, u32[]{:S(2)}, u32[]{:S(2)}) collective-permute-start(bf16[64,384]{1,0:T(8,128)(2,1)S(1)} %pad_maximum_fusion.2.refs_3_), channel_id=1, source_target_pairs={{0,12},{4,8},{8,4},{12,0},{16,28},{20,24},{24,20},{28,16},{1,13},{... | collective-permute-start | bytes 147464 | tf_op jit(solution)/shard_map/ppermute | solution.py:75
  26.3 1.4 %collective-permute-start.6 = (f32[64,384]{1,0:T(8,128)S(1)}, f32[64,384]{1,0:T(8,128)S(1)}, u32[]{:S(2)}, u32[]{:S(2)}) collective-permute-start(f32[64,384]{1,0:T(8,128)S(1)} %get-tuple-element.27), channel_id=1, source_target_pairs={{0,4},{4,0},{8,12},{12,8},{16,20},{20,16},{24,28},{28,24},{1,5},{5... | collective-permute-start | bytes 294920 | tf_op jit(solution)/shard_map/ppermute | solution.py:55
  27.7 5.1 %collective-permute-start.7 = (bf16[32,384]{1,0:T(8,128)(2,1)S(1)}, bf16[32,384]{1,0:T(8,128)(2,1)S(1)}, u32[]{:S(2)}, u32[]{:S(2)}) collective-permute-start(bf16[32,384]{1,0:T(8,128)(2,1)S(1)} %broadcast_select_fusion.2), channel_id=1, source_target_pairs={{0,7},{1,6},{2,5},{3,4},{4,3},{5,2},{6,1},{7,0},{8,15},{9,14},{10,... | collective-permute-start | bytes 73736 | tf_op jit(solution)/shard_map/ppermute | solution.py:21
  30.1 3.6 %collective-permute-start.8 = (bf16[32,384]{1,0:T(8,128)(2,1)S(1)}, bf16[32,384]{1,0:T(8,128)(2,1)S(1)}, u32[]{:S(2)}, u32[]{:S(2)}) collective-permute-start(bf16[32,384]{1,0:T(8,128)(2,1)S(1)} %get-tuple-element.29), channel_id=1, source_target_pairs={{0,5},{1,4},{2,7},{3,6},{4,1},{5,0},{6,3},{7,2},{8,13},{9,12},{10,... | collective-permute-start | bytes 73736 | tf_op jit(solution)/shard_map/ppermute | solution.py:21
  33.7 4.8 %collective-permute-start.11 = (bf16[64,384]{1,0:T(8,128)(2,1)S(1)}, bf16[64,384]{1,0:T(8,128)(2,1)S(1)}, u32[]{:S(2)}, u32[]{:S(2)}) collective-permute-start(bf16[64,384]{1,0:T(8,128)(2,1)S(1)} %pad_maximum_fusion.3.refs_3_), channel_id=1, source_target_pairs={{0,28},{4,24},{8,20},{12,16},{16,12},{20,8},{24,4},{28,0},{1,29},{... | collective-permute-start | bytes 147464 | tf_op jit(solution)/shard_map/ppermute | solution.py:75
  35.0 4.7 %collective-permute-start.10 = (bf16[64,384]{1,0:T(8,128)(2,1)S(1)}, bf16[64,384]{1,0:T(8,128)(2,1)S(1)}, u32[]{:S(2)}, u32[]{:S(2)}) collective-permute-start(bf16[64,384]{1,0:T(8,128)(2,1)S(1)} %pad_maximum_fusion.3.refs_3_), channel_id=1, source_target_pairs={{0,20},{4,16},{8,28},{12,24},{16,4},{20,0},{24,12},{28,8},{1,21},{... | collective-permute-start | bytes 147464 | tf_op jit(solution)/shard_map/ppermute | solution.py:75
  36.1 3.8 %collective-permute-start.9 = (bf16[64,384]{1,0:T(8,128)(2,1)S(1)}, bf16[64,384]{1,0:T(8,128)(2,1)S(1)}, u32[]{:S(2)}, u32[]{:S(2)}) collective-permute-start(bf16[64,384]{1,0:T(8,128)(2,1)S(1)} %pad_maximum_fusion.3.refs_3_), channel_id=1, source_target_pairs={{0,12},{4,8},{8,4},{12,0},{16,28},{20,24},{24,20},{28,16},{1,13},{... | collective-permute-start | bytes 147464 | tf_op jit(solution)/shard_map/ppermute | solution.py:75
  43.1 1.4 %collective-permute-start.12 = (f32[64,384]{1,0:T(8,128)S(1)}, f32[64,384]{1,0:T(8,128)S(1)}, u32[]{:S(2)}, u32[]{:S(2)}) collective-permute-start(f32[64,384]{1,0:T(8,128)S(1)} %get-tuple-element.31), channel_id=1, source_target_pairs={{0,4},{4,0},{8,12},{12,8},{16,20},{20,16},{24,28},{28,24},{1,5},{5... | collective-permute-start | bytes 294920 | tf_op jit(solution)/shard_map/ppermute | solution.py:55
  44.5 5.1 %collective-permute-start.13 = (bf16[32,384]{1,0:T(8,128)(2,1)S(1)}, bf16[32,384]{1,0:T(8,128)(2,1)S(1)}, u32[]{:S(2)}, u32[]{:S(2)}) collective-permute-start(bf16[32,384]{1,0:T(8,128)(2,1)S(1)} %slice.78), channel_id=1, source_target_pairs={{0,5},{1,6},{2,7},{3,4},{4,1},{5,2},{6,3},{7,0},{8,13},{9,14},{10,... | collective-permute-start | bytes 73736 | tf_op jit(solution)/shard_map/ppermute | solution.py:21
  49.6 4.2 %collective-permute-start.16 = (bf16[32,384]{1,0:T(8,128)(2,1)S(1)}, bf16[32,384]{1,0:T(8,128)(2,1)S(1)}, u32[]{:S(2)}, u32[]{:S(2)}) collective-permute-start(bf16[32,384]{1,0:T(8,128)(2,1)S(1)} %fusion.4), channel_id=1, source_target_pairs={{0,28},{4,24},{8,20},{12,16},{16,12},{20,8},{24,4},{28,0},{1,29},{... | collective-permute-start | bytes 73736 | tf_op jit(solution)/shard_map/ppermute | solution.py:75
  51.4 3.3 %collective-permute-start.15 = (bf16[32,384]{1,0:T(8,128)(2,1)S(1)}, bf16[32,384]{1,0:T(8,128)(2,1)S(1)}, u32[]{:S(2)}, u32[]{:S(2)}) collective-permute-start(bf16[32,384]{1,0:T(8,128)(2,1)S(1)} %fusion.4), channel_id=1, source_target_pairs={{0,20},{4,16},{8,28},{12,24},{16,4},{20,0},{24,12},{28,8},{1,21},{... | collective-permute-start | bytes 73736 | tf_op jit(solution)/shard_map/ppermute | solution.py:75
  51.9 3.3 %collective-permute-start.14 = (bf16[32,384]{1,0:T(8,128)(2,1)S(1)}, bf16[32,384]{1,0:T(8,128)(2,1)S(1)}, u32[]{:S(2)}, u32[]{:S(2)}) collective-permute-start(bf16[32,384]{1,0:T(8,128)(2,1)S(1)} %fusion.4), channel_id=1, source_target_pairs={{0,12},{4,8},{8,4},{12,0},{16,28},{20,24},{24,20},{28,16},{1,13},{... | collective-permute-start | bytes 73736 | tf_op jit(solution)/shard_map/ppermute | solution.py:75

commit v2 on v1

--- a/solution.py
+++ b/solution.py
@@ -118,8 +118,7 @@
         for tile in range(tiles)
     ]
     groups = [range(first, min(first + GROUP, tiles)) for first in range(0, tiles, GROUP)]
-    started = 2 * GROUP
-    for copy in small + copies[:started]:
+    for copy in small + copies:
         copy.start()
     sums_ref[...] = jnp.zeros_like(sums_ref)
     for copy in small:
@@ -130,9 +129,6 @@
     for group, before in zip(groups + [[]], [[]] + groups):
         for tile in group:
             copies[tile].wait()
-        for copy in copies[started : started + len(group)]:
-            copy.start()
-        started += len(group)
         for tile in group:
             turned_ref[tile] = kept_ref[tile].T
         for tile in before:
@@ -142,7 +138,8 @@
 def sweep_kernel(
     parts, block_ref, live_ref, jac_ref, turned_ref, bias_ref, step_ref, friction_ref, old_ref, *refs
 ):
-    part_refs, (out_ref, sums_ref, vel_ref, rel_ref, lam_ref, sem) = refs[:parts], refs[parts:]
+    part_refs, (out_ref, sums_ref, vel_ref, rel_ref, *held) = refs[:parts], refs[parts:]
+    lam_ref = held[0] if held else out_ref
     tiles = old_ref.shape[0]
     blocks, dofs = vel_ref.shape[0] // 2, vel_ref.shape[1]
     vel_ref[...] = tree([ref[...].astype(jnp.float32) for ref in part_refs])
@@ -156,11 +153,13 @@
     trial = old_ref[...] - step_ref[...] * (rel_ref[...] + bias_ref[...])
     lam = project(trial, friction_ref[...], friction_ref.shape[1])
     lam_ref[...] = lam * live_ref[...]
-    copy = pltpu.make_async_copy(lam_ref, out_ref, sem)
-    copy.start()
+    copies = [pltpu.make_async_copy(lam_ref, out_ref, held[1])] if held else []
+    for copy in copies:
+        copy.start()
     for tile in range(tiles):
         push_tile(tile, lam_ref, turned_ref, block_ref, sums_ref)
-    copy.wait()
+    for copy in copies:
+        copy.wait()
 
 
 GROUP = 4
@@ -205,7 +204,7 @@
     )(tile_count, *held)
 
 
-def sweep_step(kept, turned, tile_block, live, bias, step, friction, lam, parts):
+def sweep_step(kept, turned, tile_block, live, bias, step, friction, lam, parts, last):
     rows, dofs = parts[0].shape
     kept = pltpu.with_memory_space_constraint(kept, pltpu.VMEM)
     turned = pltpu.with_memory_space_constraint(turned, pltpu.VMEM)
@@ -213,13 +212,12 @@
         functools.partial(sweep_kernel, len(parts)),
         out_shape=result_shapes(lam, rows // 2, dofs),
         in_specs=[SMEM] + [VMEM] * (7 + len(parts)),
-        out_specs=[pl.BlockSpec(memory_space=pl.ANY), VMEM],
+        out_specs=[pl.BlockSpec(memory_space=pl.ANY) if last else VMEM, VMEM],
         scratch_shapes=[
             pltpu.VMEM((rows, dofs), jnp.float32),
             pltpu.VMEM(lam.shape, jnp.float32),
-            pltpu.VMEM(lam.shape, jnp.float32),
-            pltpu.SemaphoreType.DMA,
-        ],
+        ]
+        + ([pltpu.VMEM(lam.shape, jnp.float32), pltpu.SemaphoreType.DMA] if last else []),
         compiler_params=pltpu.CompilerParams(vmem_limit_bytes=LIMIT),
         cost_estimate=pl.CostEstimate(
             flops=4 * kept.size, bytes_accessed=4 * kept.size, transcendentals=0
@@ -255,7 +253,8 @@
             )
         )
         lam, sums = sweep_step(
-            kept, turned, tile_block, live, bias, step_scale, friction, lam, parts
+            kept, turned, tile_block, live, bias, step_scale, friction, lam, parts,
+            last=sweep == ITERS - 1,
         )
     both = pair_sum(sums)
     from_last = crossed(rounded(both[blocks:]), ahead_of)

time: 55.9 us -> 56.6 us (1.013)
  Pallas kernels: 12 us -> 12.7 us
    pallas_call x1, Pallas kernels: 5.41 us -> 6.34 us  [first_push(): pl.pallas_call(first_kernel, out_shape=[pltpu.VMEM((tiles, rows, cols), j...]
where the time goes in v2:
time: 56.6 us; the launch traced here: 56.5 us
  waiting for transfers between devices  23.7 us (42%)
  starting transfers between devices  17.7 us (31%)
  Pallas kernels  12.7 us (22%)
  between operations  1.47 us (3%)
  other arithmetic  0.85 us (2%)
    ppermute x5, waiting for transfers between devices, crossed(): return lax.ppermute(value, ('contact', 'body'), pairs)  12.1 us
    ppermute x9, starting transfers between devices, over_pairs(): parts.append(lax.ppermute(value, 'contact', pairs))  9.26 us
    ppermute x9, waiting for transfers between devices, over_pairs(): parts.append(lax.ppermute(value, 'contact', pairs))  8.57 us
    ppermute x5, starting transfers between devices, crossed(): return lax.ppermute(value, ('contact', 'body'), pairs)  7.29 us
    pallas_call x2, Pallas kernels, sweep_step(): pl.pallas_call(functools.partial(sweep_kernel, len(parts)), out_shape=res...  6.41 us
    pallas_call x1, Pallas kernels, first_push(): pl.pallas_call(first_kernel, out_shape=[pltpu.VMEM((tiles, rows, cols), j...  6.34 us
    ppermute x3, waiting for transfers between devices, pair_sum(): lax.ppermute(value, 'contact', [(place, place ^ 1) for place in range(cou...  3.07 us
  transfers between devices with their start and end apart: 17, of which 17 were waited for; matrix products, arithmetic and copies ran while one was open for 0% of the time, Pallas kernels for 0%

profile of v2, /device:TPU:0, one launch (start us, length us, event | category | flops | bytes accessed | tf_op | source)
XLA Modules:
  0.0 56.5 jit_solution(9757958337000854103)
XLA Ops:
  0.6 0.0 copy-start.3
  0.6 0.0 copy-start.4
  0.7 0.0 copy-start.5
  0.7 0.0 copy-start.2
  0.7 0.0 copy-start.1
  0.7 0.0 copy-start
  1.4 6.3 %first_push.1 = (bf16[16,768,384]{2,1,0:T(8,128)(2,1)S(1)}, bf16[16,384,768]{2,1,0:T(8,128)(2,1)S(1)}, f32[16,384]{1,0:T(8,128)S(1)}, f32[16,384]{1,0:T(8,128)S(1)}, f32[64,384]{1,0:T(8,128)S(1)}) custom-call(s32[1]{0:T(128)S(6)} %copy.11.count_ref, s32[2,16]{1,0:T(2,128)} %bitcast.2, bf16[16,768,384]{2,1,0:T(8,128)(2,1)} %bitcast.5, f32[16,384]{1,0:T(8,128)} %start_ref.1), custom_call_target="tpu_custom_call" | custom-call | flops 9437184 | bytes 9437184 | tf_op jit(solution)/shard_map/first_push/pallas_call | solution.py:185
  7.7 0.5 collective-permute-start
  8.2 0.0 copy-done.4
  8.2 0.9 %collective-permute-done = f32[64,384]{1,0:T(8,128)S(1)} collective-permute-done((f32[64,384]{1,0:T(8,128)S(1)}, f32[64,384]{1,0:T(8,128)S(1)}, u32[]{:S(2)}, u32[]{:S(2)}) %collective-permute-start) | collective-permute-done | bytes 98336 | tf_op jit(solution)/shard_map/ppermute | solution.py:55
  9.2 0.0 copy-done.5
  9.2 4.8 %collective-permute-start.1 = (bf16[64,384]{1,0:T(8,128)(2,1)S(1)}, bf16[64,384]{1,0:T(8,128)(2,1)S(1)}, u32[]{:S(2)}, u32[]{:S(2)}) collective-permute-start(bf16[64,384]{1,0:T(8,128)(2,1)S(1)} %get-tuple-element.24), channel_id=1, source_target_pairs={{0,7},{1,6},{2,5},{3,4},{4,3},{5,2},{6,1},{7,0},{8,15},{9,14},{10,... | collective-permute-start | bytes 147464 | tf_op jit(solution)/shard_map/ppermute | solution.py:21
  14.0 0.0 collective-permute-start.2
  14.0 2.1 %collective-permute-done.1 = bf16[64,384]{1,0:T(8,128)(2,1)S(1)} collective-permute-done((bf16[64,384]{1,0:T(8,128)(2,1)S(1)}, bf16[64,384]{1,0:T(8,128)(2,1)S(1)}, u32[]{:S(2)}, u32[]{:S(2)}) %collective-permute-start.1) | collective-permute-done | bytes 49184 | tf_op jit(solution)/shard_map/ppermute | solution.py:21
  16.2 1.4 %collective-permute-done.2 = bf16[64,384]{1,0:T(8,128)(2,1)S(1)} collective-permute-done((bf16[64,384]{1,0:T(8,128)(2,1)S(1)}, bf16[64,384]{1,0:T(8,128)(2,1)S(1)}, u32[]{:S(2)}, u32[]{:S(2)}) %collective-permute-start.2) | collective-permute-done | bytes 49184 | tf_op jit(solution)/shard_map/ppermute | solution.py:21
  17.6 2.5 %collective-permute-start.5 = (bf16[64,384]{1,0:T(8,128)(2,1)S(1)}, bf16[64,384]{1,0:T(8,128)(2,1)S(1)}, u32[]{:S(2)}, u32[]{:S(2)}) collective-permute-start(bf16[64,384]{1,0:T(8,128)(2,1)S(1)} %pad_maximum_fusion.2.refs_3_), channel_id=1, source_target_pairs={{0,28},{4,24},{8,20},{12,16},{16,12},{20,8},{24,4},{28,0},{1,29},{... | collective-permute-start | bytes 147464 | tf_op jit(solution)/shard_map/ppermute | solution.py:75
  20.1 0.3 collective-permute-start.4
  20.4 0.5 collective-permute-start.3
  20.9 1.3 %collective-permute-done.5.refs_2_ = bf16[64,384]{1,0:T(8,128)(2,1)S(1)} collective-permute-done((bf16[64,384]{1,0:T(8,128)(2,1)S(1)}, bf16[64,384]{1,0:T(8,128)(2,1)S(1)}, u32[]{:S(2)}, u32[]{:S(2)}) %collective-permute-start.5) | collective-permute-done | bytes 49184 | tf_op jit(solution)/shard_map/ppermute | solution.py:75
  22.1 1.7 %collective-permute-done.4.refs_1_ = bf16[64,384]{1,0:T(8,128)(2,1)S(1)} collective-permute-done((bf16[64,384]{1,0:T(8,128)(2,1)S(1)}, bf16[64,384]{1,0:T(8,128)(2,1)S(1)}, u32[]{:S(2)}, u32[]{:S(2)}) %collective-permute-start.4) | collective-permute-done | bytes 49184 | tf_op jit(solution)/shard_map/ppermute | solution.py:75
  23.8 0.1 collective-permute-done.3.refs_0_
  23.9 0.0 copy-done.3
  23.9 0.0 copy-done.2
  23.9 0.0 copy-done.1
  23.9 0.0 copy-done
  23.9 3.2 %sweep_step.2 = (f32[16,384]{1,0:T(8,128)S(1)}, f32[64,384]{1,0:T(8,128)S(1)}) custom-call(s32[2,16]{1,0:T(2,128)S(1)} %bitcast.3, f32[16,384]{1,0:T(8,128)S(1)} %get-tuple-element.18.live_ref, bf16[16,768,384]{2,1,0:T(8,128)(2,1)S(1)} %get-tuple-element.19.jac_ref, bf16[16,384,768]{2,1,0:T(8,128)(2,1)S(1)} %get-tuple-element.20.turned_ref, ...), custom_call_target="tpu_custom_call" | custom-call | flops 18874368 | bytes 18874368 | tf_op jit(solution)/shard_map/sweep_step/pallas_call | solution.py:211
  27.0 0.4 collective-permute-start.6
  27.4 1.0 %collective-permute-done.6 = f32[64,384]{1,0:T(8,128)S(1)} collective-permute-done((f32[64,384]{1,0:T(8,128)S(1)}, f32[64,384]{1,0:T(8,128)S(1)}, u32[]{:S(2)}, u32[]{:S(2)}) %collective-permute-start.6) | collective-permute-done | bytes 98336 | tf_op jit(solution)/shard_map/ppermute | solution.py:55
  28.5 2.4 %collective-permute-start.7 = (bf16[32,384]{1,0:T(8,128)(2,1)S(1)}, bf16[32,384]{1,0:T(8,128)(2,1)S(1)}, u32[]{:S(2)}, u32[]{:S(2)}) collective-permute-start(bf16[32,384]{1,0:T(8,128)(2,1)S(1)} %broadcast_select_fusion.2), channel_id=1, source_target_pairs={{0,7},{1,6},{2,5},{3,4},{4,3},{5,2},{6,1},{7,0},{8,15},{9,14},{10,... | collective-permute-start | bytes 73736 | tf_op jit(solution)/shard_map/ppermute | solution.py:21
  30.8 0.0 collective-permute-start.8
  30.8 2.7 %collective-permute-done.7 = bf16[32,384]{1,0:T(8,128)(2,1)S(1)} collective-permute-done((bf16[32,384]{1,0:T(8,128)(2,1)S(1)}, bf16[32,384]{1,0:T(8,128)(2,1)S(1)}, u32[]{:S(2)}, u32[]{:S(2)}) %collective-permute-start.7) | collective-permute-done | bytes 24608 | tf_op jit(solution)/shard_map/ppermute | solution.py:21
  33.6 0.8 %collective-permute-done.8 = bf16[32,384]{1,0:T(8,128)(2,1)S(1)} collective-permute-done((bf16[32,384]{1,0:T(8,128)(2,1)S(1)}, bf16[32,384]{1,0:T(8,128)(2,1)S(1)}, u32[]{:S(2)}, u32[]{:S(2)}) %collective-permute-start.8) | collective-permute-done | bytes 24608 | tf_op jit(solution)/shard_map/ppermute | solution.py:21
  34.5 1.3 %collective-permute-start.11 = (bf16[64,384]{1,0:T(8,128)(2,1)S(1)}, bf16[64,384]{1,0:T(8,128)(2,1)S(1)}, u32[]{:S(2)}, u32[]{:S(2)}) collective-permute-start(bf16[64,384]{1,0:T(8,128)(2,1)S(1)} %pad_maximum_fusion.3.refs_3_), channel_id=1, source_target_pairs={{0,28},{4,24},{8,20},{12,16},{16,12},{20,8},{24,4},{28,0},{1,29},{... | collective-permute-start | bytes 147464 | tf_op jit(solution)/shard_map/ppermute | solution.py:75
  35.7 1.0 %collective-permute-start.10 = (bf16[64,384]{1,0:T(8,128)(2,1)S(1)}, bf16[64,384]{1,0:T(8,128)(2,1)S(1)}, u32[]{:S(2)}, u32[]{:S(2)}) collective-permute-start(bf16[64,384]{1,0:T(8,128)(2,1)S(1)} %pad_maximum_fusion.3.refs_3_), channel_id=1, source_target_pairs={{0,20},{4,16},{8,28},{12,24},{16,4},{20,0},{24,12},{28,8},{1,21},{... | collective-permute-start | bytes 147464 | tf_op jit(solution)/shard_map/ppermute | solution.py:75
  36.8 0.7 %collective-permute-start.9 = (bf16[64,384]{1,0:T(8,128)(2,1)S(1)}, bf16[64,384]{1,0:T(8,128)(2,1)S(1)}, u32[]{:S(2)}, u32[]{:S(2)}) collective-permute-start(bf16[64,384]{1,0:T(8,128)(2,1)S(1)} %pad_maximum_fusion.3.refs_3_), channel_id=1, source_target_pairs={{0,12},{4,8},{8,4},{12,0},{16,28},{20,24},{24,20},{28,16},{1,13},{... | collective-permute-start | bytes 147464 | tf_op jit(solution)/shard_map/ppermute | solution.py:75
  37.5 1.8 %collective-permute-done.11.refs_2_ = bf16[64,384]{1,0:T(8,128)(2,1)S(1)} collective-permute-done((bf16[64,384]{1,0:T(8,128)(2,1)S(1)}, bf16[64,384]{1,0:T(8,128)(2,1)S(1)}, u32[]{:S(2)}, u32[]{:S(2)}) %collective-permute-start.11) | collective-permute-done | bytes 49184 | tf_op jit(solution)/shard_map/ppermute | solution.py:75
  39.2 1.2 %collective-permute-done.10.refs_1_ = bf16[64,384]{1,0:T(8,128)(2,1)S(1)} collective-permute-done((bf16[64,384]{1,0:T(8,128)(2,1)S(1)}, bf16[64,384]{1,0:T(8,128)(2,1)S(1)}, u32[]{:S(2)}, u32[]{:S(2)}) %collective-permute-start.10) | collective-permute-done | bytes 49184 | tf_op jit(solution)/shard_map/ppermute | solution.py:75
  40.5 0.1 collective-permute-done.9.refs_0_
  40.6 3.3 %sweep_step.3 = (f32[16,384]{1,0:T(8,128)}, f32[64,384]{1,0:T(8,128)S(1)}) custom-call(s32[2,16]{1,0:T(2,128)S(1)} %bitcast.4, f32[16,384]{1,0:T(8,128)S(1)} %get-tuple-element.18.live_ref, bf16[16,768,384]{2,1,0:T(8,128)(2,1)S(1)} %get-tuple-element.19.jac_ref, bf16[16,384,768]{2,1,0:T(8,128)(2,1)S(1)} %get-tuple-element.20.turned_ref, ...), custom_call_target="tpu_custom_call" | custom-call | flops 18874368 | bytes 18874368 | tf_op jit(solution)/shard_map/sweep_step/pallas_call | solution.py:211
  43.8 0.2 collective-permute-start.12
  44.0 1.2 %collective-permute-done.12 = f32[64,384]{1,0:T(8,128)S(1)} collective-permute-done((f32[64,384]{1,0:T(8,128)S(1)}, f32[64,384]{1,0:T(8,128)S(1)}, u32[]{:S(2)}, u32[]{:S(2)}) %collective-permute-start.12) | collective-permute-done | bytes 98336 | tf_op jit(solution)/shard_map/ppermute | solution.py:55
  45.2 0.1 collective-permute-start.13
  45.4 5.0 %collective-permute-done.13 = bf16[32,384]{1,0:T(8,128)(2,1)S(1)} collective-permute-done((bf16[32,384]{1,0:T(8,128)(2,1)S(1)}, bf16[32,384]{1,0:T(8,128)(2,1)S(1)}, u32[]{:S(2)}, u32[]{:S(2)}) %collective-permute-start.13) | collective-permute-done | bytes 24608 | tf_op jit(solution)/shard_map/ppermute | solution.py:21
  50.3 1.8 %collective-permute-start.16 = (bf16[32,384]{1,0:T(8,128)(2,1)S(1)}, bf16[32,384]{1,0:T(8,128)(2,1)S(1)}, u32[]{:S(2)}, u32[]{:S(2)}) collective-permute-start(bf16[32,384]{1,0:T(8,128)(2,1)S(1)} %fusion.4), channel_id=1, source_target_pairs={{0,28},{4,24},{8,20},{12,16},{16,12},{20,8},{24,4},{28,0},{1,29},{... | collective-permute-start | bytes 73736 | tf_op jit(solution)/shard_map/ppermute | solution.py:75
  52.1 0.4 collective-permute-start.15
  52.6 0.8 %collective-permute-start.14 = (bf16[32,384]{1,0:T(8,128)(2,1)S(1)}, bf16[32,384]{1,0:T(8,128)(2,1)S(1)}, u32[]{:S(2)}, u32[]{:S(2)}) collective-permute-start(bf16[32,384]{1,0:T(8,128)(2,1)S(1)} %fusion.4), channel_id=1, source_target_pairs={{0,12},{4,8},{8,4},{12,0},{16,28},{20,24},{24,20},{28,16},{1,13},{... | collective-permute-start | bytes 73736 | tf_op jit(solution)/shard_map/ppermute | solution.py:75
  53.4 1.2 %collective-permute-done.16 = bf16[32,384]{1,0:T(8,128)(2,1)S(1)} collective-permute-done((bf16[32,384]{1,0:T(8,128)(2,1)S(1)}, bf16[32,384]{1,0:T(8,128)(2,1)S(1)}, u32[]{:S(2)}, u32[]{:S(2)}) %collective-permute-start.16) | collective-permute-done | bytes 24608 | tf_op jit(solution)/shard_map/ppermute | solution.py:75
  54.6 0.8 %collective-permute-done.15 = bf16[32,384]{1,0:T(8,128)(2,1)S(1)} collective-permute-done((bf16[32,384]{1,0:T(8,128)(2,1)S(1)}, bf16[32,384]{1,0:T(8,128)(2,1)S(1)}, u32[]{:S(2)}, u32[]{:S(2)}) %collective-permute-start.15) | collective-permute-done | bytes 24608 | tf_op jit(solution)/shard_map/ppermute | solution.py:75
  55.4 0.4 collective-permute-done.14
  55.8 0.6 %multiply_add_fusion = f32[32,384]{1,0:T(8,128)} fusion(f32[32,384]{1,0:T(8,128)S(1)} %copy-done.5, f32[32,384]{1,0:T(8,128)S(1)} %copy-done.4, bf16[32,384]{1,0:T(8,128)(2,1)S(1)} %fusion.4, bf16[32,384]{1,0:T(8,128)(2,1)S(1)} %collective-permute-done.16, bf16[32,384]{1,0:T(8,128)(2,1)S(1)} %collective-permute-done.15, ...), kind=kLoop, calls=%fused_computation.13 | loop fusion | flops 110592 | bytes 245760 | tf_op jit(solution)/shard_map/add | solution.py:262
  (16 shorter events, 0.2 us)
Async XLA Ops:
  0.6 23.2 %copy-start.3 = (s32[16,2]{0,1:T(2,128)S(1)}, s32[16,2]{0,1:T(2,128)}, u32[]{:S(2)}) copy-start(s32[16,2]{0,1:T(2,128)} %param.10) | copy-start | bytes 388
  0.6 7.6 %copy-start.4 = (f32[32,384]{1,0:T(8,128)S(1)}, f32[32,384]{1,0:T(8,128)}, u32[]{:S(2)}) copy-start(f32[32,384]{1,0:T(8,128)} %param.13) | copy-start | bytes 147460
  0.7 8.5 %copy-start.5 = (f32[32,384]{1,0:T(8,128)S(1)}, f32[32,384]{1,0:T(8,128)}, u32[]{:S(2)}) copy-start(f32[32,384]{1,0:T(8,128)} %param.12) | copy-start | bytes 147460
  0.7 23.2 %copy-start.2 = (f32[16,128]{1,0:T(8,128)S(1)}, f32[16,128]{1,0:T(8,128)}, u32[]{:S(2)}) copy-start(f32[16,128]{1,0:T(8,128)} %friction_ref.3) | copy-start | bytes 24580
  0.7 23.2 %copy-start.1 = (f32[16,384]{1,0:T(8,128)S(1)}, f32[16,384]{1,0:T(8,128)}, u32[]{:S(2)}) copy-start(f32[16,384]{1,0:T(8,128)} %step_ref.3) | copy-start | bytes 73732
  0.7 23.2 %copy-start = (f32[16,384]{1,0:T(8,128)S(1)}, f32[16,384]{1,0:T(8,128)}, u32[]{:S(2)}) copy-start(f32[16,384]{1,0:T(8,128)} %bias_ref.3) | copy-start | bytes 73732
  7.7 1.5 %collective-permute-start = (f32[64,384]{1,0:T(8,128)S(1)}, f32[64,384]{1,0:T(8,128)S(1)}, u32[]{:S(2)}, u32[]{:S(2)}) collective-permute-start(f32[64,384]{1,0:T(8,128)S(1)} %get-tuple-element.22), channel_id=1, source_target_pairs={{0,4},{4,0},{8,12},{12,8},{16,20},{20,16},{24,28},{28,24},{1,5},{5... | collective-permute-start | bytes 294920 | tf_op jit(solution)/shard_map/ppermute | solution.py:55
  9.2 6.9 %collective-permute-start.1 = (bf16[64,384]{1,0:T(8,128)(2,1)S(1)}, bf16[64,384]{1,0:T(8,128)(2,1)S(1)}, u32[]{:S(2)}, u32[]{:S(2)}) collective-permute-start(bf16[64,384]{1,0:T(8,128)(2,1)S(1)} %get-tuple-element.24), channel_id=1, source_target_pairs={{0,7},{1,6},{2,5},{3,4},{4,3},{5,2},{6,1},{7,0},{8,15},{9,14},{10,... | collective-permute-start | bytes 147464 | tf_op jit(solution)/shard_map/ppermute | solution.py:21
  14.0 3.5 %collective-permute-start.2 = (bf16[64,384]{1,0:T(8,128)(2,1)S(1)}, bf16[64,384]{1,0:T(8,128)(2,1)S(1)}, u32[]{:S(2)}, u32[]{:S(2)}) collective-permute-start(bf16[64,384]{1,0:T(8,128)(2,1)S(1)} %get-tuple-element.25), channel_id=1, source_target_pairs={{0,5},{1,4},{2,7},{3,6},{4,1},{5,0},{6,3},{7,2},{8,13},{9,12},{10,... | collective-permute-start | bytes 147464 | tf_op jit(solution)/shard_map/ppermute | solution.py:21
  17.6 4.5 %collective-permute-start.5 = (bf16[64,384]{1,0:T(8,128)(2,1)S(1)}, bf16[64,384]{1,0:T(8,128)(2,1)S(1)}, u32[]{:S(2)}, u32[]{:S(2)}) collective-permute-start(bf16[64,384]{1,0:T(8,128)(2,1)S(1)} %pad_maximum_fusion.2.refs_3_), channel_id=1, source_target_pairs={{0,28},{4,24},{8,20},{12,16},{16,12},{20,8},{24,4},{28,0},{1,29},{... | collective-permute-start | bytes 147464 | tf_op jit(solution)/shard_map/ppermute | solution.py:75
  20.1 3.7 %collective-permute-start.4 = (bf16[64,384]{1,0:T(8,128)(2,1)S(1)}, bf16[64,384]{1,0:T(8,128)(2,1)S(1)}, u32[]{:S(2)}, u32[]{:S(2)}) collective-permute-start(bf16[64,384]{1,0:T(8,128)(2,1)S(1)} %pad_maximum_fusion.2.refs_3_), channel_id=1, source_target_pairs={{0,20},{4,16},{8,28},{12,24},{16,4},{20,0},{24,12},{28,8},{1,21},{... | collective-permute-start | bytes 147464 | tf_op jit(solution)/shard_map/ppermute | solution.py:75
  20.4 3.5 %collective-permute-start.3 = (bf16[64,384]{1,0:T(8,128)(2,1)S(1)}, bf16[64,384]{1,0:T(8,128)(2,1)S(1)}, u32[]{:S(2)}, u32[]{:S(2)}) collective-permute-start(bf16[64,384]{1,0:T(8,128)(2,1)S(1)} %pad_maximum_fusion.2.refs_3_), channel_id=1, source_target_pairs={{0,12},{4,8},{8,4},{12,0},{16,28},{20,24},{24,20},{28,16},{1,13},{... | collective-permute-start | bytes 147464 | tf_op jit(solution)/shard_map/ppermute | solution.py:75
  27.0 1.4 %collective-permute-start.6 = (f32[64,384]{1,0:T(8,128)S(1)}, f32[64,384]{1,0:T(8,128)S(1)}, u32[]{:S(2)}, u32[]{:S(2)}) collective-permute-start(f32[64,384]{1,0:T(8,128)S(1)} %get-tuple-element.27), channel_id=1, source_target_pairs={{0,4},{4,0},{8,12},{12,8},{16,20},{20,16},{24,28},{28,24},{1,5},{5... | collective-permute-start | bytes 294920 | tf_op jit(solution)/shard_map/ppermute | solution.py:55
  28.5 5.1 %collective-permute-start.7 = (bf16[32,384]{1,0:T(8,128)(2,1)S(1)}, bf16[32,384]{1,0:T(8,128)(2,1)S(1)}, u32[]{:S(2)}, u32[]{:S(2)}) collective-permute-start(bf16[32,384]{1,0:T(8,128)(2,1)S(1)} %broadcast_select_fusion.2), channel_id=1, source_target_pairs={{0,7},{1,6},{2,5},{3,4},{4,3},{5,2},{6,1},{7,0},{8,15},{9,14},{10,... | collective-permute-start | bytes 73736 | tf_op jit(solution)/shard_map/ppermute | solution.py:21
  30.8 3.6 %collective-permute-start.8 = (bf16[32,384]{1,0:T(8,128)(2,1)S(1)}, bf16[32,384]{1,0:T(8,128)(2,1)S(1)}, u32[]{:S(2)}, u32[]{:S(2)}) collective-permute-start(bf16[32,384]{1,0:T(8,128)(2,1)S(1)} %get-tuple-element.29), channel_id=1, source_target_pairs={{0,5},{1,4},{2,7},{3,6},{4,1},{5,0},{6,3},{7,2},{8,13},{9,12},{10,... | collective-permute-start | bytes 73736 | tf_op jit(solution)/shard_map/ppermute | solution.py:21
  34.5 4.8 %collective-permute-start.11 = (bf16[64,384]{1,0:T(8,128)(2,1)S(1)}, bf16[64,384]{1,0:T(8,128)(2,1)S(1)}, u32[]{:S(2)}, u32[]{:S(2)}) collective-permute-start(bf16[64,384]{1,0:T(8,128)(2,1)S(1)} %pad_maximum_fusion.3.refs_3_), channel_id=1, source_target_pairs={{0,28},{4,24},{8,20},{12,16},{16,12},{20,8},{24,4},{28,0},{1,29},{... | collective-permute-start | bytes 147464 | tf_op jit(solution)/shard_map/ppermute | solution.py:75
  35.7 4.7 %collective-permute-start.10 = (bf16[64,384]{1,0:T(8,128)(2,1)S(1)}, bf16[64,384]{1,0:T(8,128)(2,1)S(1)}, u32[]{:S(2)}, u32[]{:S(2)}) collective-permute-start(bf16[64,384]{1,0:T(8,128)(2,1)S(1)} %pad_maximum_fusion.3.refs_3_), channel_id=1, source_target_pairs={{0,20},{4,16},{8,28},{12,24},{16,4},{20,0},{24,12},{28,8},{1,21},{... | collective-permute-start | bytes 147464 | tf_op jit(solution)/shard_map/ppermute | solution.py:75
  36.8 3.8 %collective-permute-start.9 = (bf16[64,384]{1,0:T(8,128)(2,1)S(1)}, bf16[64,384]{1,0:T(8,128)(2,1)S(1)}, u32[]{:S(2)}, u32[]{:S(2)}) collective-permute-start(bf16[64,384]{1,0:T(8,128)(2,1)S(1)} %pad_maximum_fusion.3.refs_3_), channel_id=1, source_target_pairs={{0,12},{4,8},{8,4},{12,0},{16,28},{20,24},{24,20},{28,16},{1,13},{... | collective-permute-start | bytes 147464 | tf_op jit(solution)/shard_map/ppermute | solution.py:75
  43.8 1.4 %collective-permute-start.12 = (f32[64,384]{1,0:T(8,128)S(1)}, f32[64,384]{1,0:T(8,128)S(1)}, u32[]{:S(2)}, u32[]{:S(2)}) collective-permute-start(f32[64,384]{1,0:T(8,128)S(1)} %get-tuple-element.31), channel_id=1, source_target_pairs={{0,4},{4,0},{8,12},{12,8},{16,20},{20,16},{24,28},{28,24},{1,5},{5... | collective-permute-start | bytes 294920 | tf_op jit(solution)/shard_map/ppermute | solution.py:55
  45.2 5.1 %collective-permute-start.13 = (bf16[32,384]{1,0:T(8,128)(2,1)S(1)}, bf16[32,384]{1,0:T(8,128)(2,1)S(1)}, u32[]{:S(2)}, u32[]{:S(2)}) collective-permute-start(bf16[32,384]{1,0:T(8,128)(2,1)S(1)} %slice.78), channel_id=1, source_target_pairs={{0,5},{1,6},{2,7},{3,4},{4,1},{5,2},{6,3},{7,0},{8,13},{9,14},{10,... | collective-permute-start | bytes 73736 | tf_op jit(solution)/shard_map/ppermute | solution.py:21
  50.3 4.2 %collective-permute-start.16 = (bf16[32,384]{1,0:T(8,128)(2,1)S(1)}, bf16[32,384]{1,0:T(8,128)(2,1)S(1)}, u32[]{:S(2)}, u32[]{:S(2)}) collective-permute-start(bf16[32,384]{1,0:T(8,128)(2,1)S(1)} %fusion.4), channel_id=1, source_target_pairs={{0,28},{4,24},{8,20},{12,16},{16,12},{20,8},{24,4},{28,0},{1,29},{... | collective-permute-start | bytes 73736 | tf_op jit(solution)/shard_map/ppermute | solution.py:75
  52.1 3.3 %collective-permute-start.15 = (bf16[32,384]{1,0:T(8,128)(2,1)S(1)}, bf16[32,384]{1,0:T(8,128)(2,1)S(1)}, u32[]{:S(2)}, u32[]{:S(2)}) collective-permute-start(bf16[32,384]{1,0:T(8,128)(2,1)S(1)} %fusion.4), channel_id=1, source_target_pairs={{0,20},{4,16},{8,28},{12,24},{16,4},{20,0},{24,12},{28,8},{1,21},{... | collective-permute-start | bytes 73736 | tf_op jit(solution)/shard_map/ppermute | solution.py:75
  52.6 3.3 %collective-permute-start.14 = (bf16[32,384]{1,0:T(8,128)(2,1)S(1)}, bf16[32,384]{1,0:T(8,128)(2,1)S(1)}, u32[]{:S(2)}, u32[]{:S(2)}) collective-permute-start(bf16[32,384]{1,0:T(8,128)(2,1)S(1)} %fusion.4), channel_id=1, source_target_pairs={{0,12},{4,8},{8,4},{12,0},{16,28},{20,24},{24,20},{28,16},{1,13},{... | collective-permute-start | bytes 73736 | tf_op jit(solution)/shard_map/ppermute | solution.py:75

commit v3 on v2

--- a/solution.py
+++ b/solution.py
@@ -118,7 +118,8 @@
         for tile in range(tiles)
     ]
     groups = [range(first, min(first + GROUP, tiles)) for first in range(0, tiles, GROUP)]
-    for copy in small + copies:
+    started = 3 * GROUP
+    for copy in small + copies[:started]:
         copy.start()
     sums_ref[...] = jnp.zeros_like(sums_ref)
     for copy in small:
@@ -129,6 +130,9 @@
     for group, before in zip(groups + [[]], [[]] + groups):
         for tile in group:
             copies[tile].wait()
+        for copy in copies[started : started + len(group)]:
+            copy.start()
+        started += len(group)
         for tile in group:
             turned_ref[tile] = kept_ref[tile].T
         for tile in before:
@@ -162,7 +166,7 @@
         copy.wait()
 
 
-GROUP = 4
+GROUP = 2
 LIMIT = 24 * 1024 * 1024
 SMEM = pl.BlockSpec(memory_space=pltpu.SMEM)
 VMEM = pl.BlockSpec(memory_space=pltpu.VMEM)

time: 56.6 us -> 55.7 us (0.984)
  Pallas kernels: 12.7 us -> 11.8 us
    pallas_call x1, Pallas kernels: 6.34 us -> 5.38 us  [first_push(): pl.pallas_call(first_kernel, out_shape=[pltpu.VMEM((tiles, rows, cols), j...]
where the time goes in v3:
time: 55.7 us; the launch traced here: 55.5 us
  waiting for transfers between devices  23.7 us (43%)
  starting transfers between devices  17.7 us (32%)
  Pallas kernels  11.8 us (21%)
  between operations  1.47 us (3%)
  other arithmetic  0.85 us (2%)
    ppermute x5, waiting for transfers between devices, crossed(): return lax.ppermute(value, ('contact', 'body'), pairs)  12.1 us
    ppermute x9, starting transfers between devices, over_pairs(): parts.append(lax.ppermute(value, 'contact', pairs))  9.26 us
    ppermute x9, waiting for transfers between devices, over_pairs(): parts.append(lax.ppermute(value, 'contact', pairs))  8.57 us
    ppermute x5, starting transfers between devices, crossed(): return lax.ppermute(value, ('contact', 'body'), pairs)  7.29 us
    pallas_call x2, Pallas kernels, sweep_step(): pl.pallas_call(functools.partial(sweep_kernel, len(parts)), out_shape=res...  6.4 us
    pallas_call x1, Pallas kernels, first_push(): pl.pallas_call(first_kernel, out_shape=[pltpu.VMEM((tiles, rows, cols), j...  5.38 us
    ppermute x3, waiting for transfers between devices, pair_sum(): lax.ppermute(value, 'contact', [(place, place ^ 1) for place in range(cou...  3.07 us
  transfers between devices with their start and end apart: 17, of which 17 were waited for; matrix products, arithmetic and copies ran while one was open for 0% of the time, Pallas kernels for 0%

profile of v3, /device:TPU:0, one launch (start us, length us, event | category | flops | bytes accessed | tf_op | source)
XLA Modules:
  0.0 55.5 jit_solution(11319783852059809090)
XLA Ops:
  0.6 0.0 copy-start.3
  0.6 0.0 copy-start.4
  0.7 0.0 copy-start.5
  0.7 0.0 copy-start.2
  0.7 0.0 copy-start.1
  0.7 0.0 copy-start
  1.4 5.4 %first_push.1 = (bf16[16,768,384]{2,1,0:T(8,128)(2,1)S(1)}, bf16[16,384,768]{2,1,0:T(8,128)(2,1)S(1)}, f32[16,384]{1,0:T(8,128)S(1)}, f32[16,384]{1,0:T(8,128)S(1)}, f32[64,384]{1,0:T(8,128)S(1)}) custom-call(s32[1]{0:T(128)S(6)} %copy.11.count_ref, s32[2,16]{1,0:T(2,128)} %bitcast.2, bf16[16,768,384]{2,1,0:T(8,128)(2,1)} %bitcast.5, f32[16,384]{1,0:T(8,128)} %start_ref.1), custom_call_target="tpu_custom_call" | custom-call | flops 9437184 | bytes 9437184 | tf_op jit(solution)/shard_map/first_push/pallas_call | solution.py:189
  6.7 0.5 collective-permute-start
  7.3 0.0 copy-done.4
  7.3 0.9 %collective-permute-done = f32[64,384]{1,0:T(8,128)S(1)} collective-permute-done((f32[64,384]{1,0:T(8,128)S(1)}, f32[64,384]{1,0:T(8,128)S(1)}, u32[]{:S(2)}, u32[]{:S(2)}) %collective-permute-start) | collective-permute-done | bytes 98336 | tf_op jit(solution)/shard_map/ppermute | solution.py:55
  8.2 0.0 copy-done.5
  8.3 4.8 %collective-permute-start.1 = (bf16[64,384]{1,0:T(8,128)(2,1)S(1)}, bf16[64,384]{1,0:T(8,128)(2,1)S(1)}, u32[]{:S(2)}, u32[]{:S(2)}) collective-permute-start(bf16[64,384]{1,0:T(8,128)(2,1)S(1)} %get-tuple-element.24), channel_id=1, source_target_pairs={{0,7},{1,6},{2,5},{3,4},{4,3},{5,2},{6,1},{7,0},{8,15},{9,14},{10,... | collective-permute-start | bytes 147464 | tf_op jit(solution)/shard_map/ppermute | solution.py:21
  13.1 0.0 collective-permute-start.2
  13.1 2.1 %collective-permute-done.1 = bf16[64,384]{1,0:T(8,128)(2,1)S(1)} collective-permute-done((bf16[64,384]{1,0:T(8,128)(2,1)S(1)}, bf16[64,384]{1,0:T(8,128)(2,1)S(1)}, u32[]{:S(2)}, u32[]{:S(2)}) %collective-permute-start.1) | collective-permute-done | bytes 49184 | tf_op jit(solution)/shard_map/ppermute | solution.py:21
  15.2 1.4 %collective-permute-done.2 = bf16[64,384]{1,0:T(8,128)(2,1)S(1)} collective-permute-done((bf16[64,384]{1,0:T(8,128)(2,1)S(1)}, bf16[64,384]{1,0:T(8,128)(2,1)S(1)}, u32[]{:S(2)}, u32[]{:S(2)}) %collective-permute-start.2) | collective-permute-done | bytes 49184 | tf_op jit(solution)/shard_map/ppermute | solution.py:21
  16.7 2.5 %collective-permute-start.5 = (bf16[64,384]{1,0:T(8,128)(2,1)S(1)}, bf16[64,384]{1,0:T(8,128)(2,1)S(1)}, u32[]{:S(2)}, u32[]{:S(2)}) collective-permute-start(bf16[64,384]{1,0:T(8,128)(2,1)S(1)} %pad_maximum_fusion.2.refs_3_), channel_id=1, source_target_pairs={{0,28},{4,24},{8,20},{12,16},{16,12},{20,8},{24,4},{28,0},{1,29},{... | collective-permute-start | bytes 147464 | tf_op jit(solution)/shard_map/ppermute | solution.py:75
  19.1 0.3 collective-permute-start.4
  19.4 0.5 collective-permute-start.3
  19.9 1.3 %collective-permute-done.5.refs_2_ = bf16[64,384]{1,0:T(8,128)(2,1)S(1)} collective-permute-done((bf16[64,384]{1,0:T(8,128)(2,1)S(1)}, bf16[64,384]{1,0:T(8,128)(2,1)S(1)}, u32[]{:S(2)}, u32[]{:S(2)}) %collective-permute-start.5) | collective-permute-done | bytes 49184 | tf_op jit(solution)/shard_map/ppermute | solution.py:75
  21.1 1.7 %collective-permute-done.4.refs_1_ = bf16[64,384]{1,0:T(8,128)(2,1)S(1)} collective-permute-done((bf16[64,384]{1,0:T(8,128)(2,1)S(1)}, bf16[64,384]{1,0:T(8,128)(2,1)S(1)}, u32[]{:S(2)}, u32[]{:S(2)}) %collective-permute-start.4) | collective-permute-done | bytes 49184 | tf_op jit(solution)/shard_map/ppermute | solution.py:75
  22.8 0.1 collective-permute-done.3.refs_0_
  22.9 0.0 copy-done.3
  22.9 0.0 copy-done.2
  22.9 0.0 copy-done.1
  22.9 0.0 copy-done
  22.9 3.1 %sweep_step.2 = (f32[16,384]{1,0:T(8,128)S(1)}, f32[64,384]{1,0:T(8,128)S(1)}) custom-call(s32[2,16]{1,0:T(2,128)S(1)} %bitcast.3, f32[16,384]{1,0:T(8,128)S(1)} %get-tuple-element.18.live_ref, bf16[16,768,384]{2,1,0:T(8,128)(2,1)S(1)} %get-tuple-element.19.jac_ref, bf16[16,384,768]{2,1,0:T(8,128)(2,1)S(1)} %get-tuple-element.20.turned_ref, ...), custom_call_target="tpu_custom_call" | custom-call | flops 18874368 | bytes 18874368 | tf_op jit(solution)/shard_map/sweep_step/pallas_call | solution.py:215
  26.1 0.4 collective-permute-start.6
  26.5 1.0 %collective-permute-done.6 = f32[64,384]{1,0:T(8,128)S(1)} collective-permute-done((f32[64,384]{1,0:T(8,128)S(1)}, f32[64,384]{1,0:T(8,128)S(1)}, u32[]{:S(2)}, u32[]{:S(2)}) %collective-permute-start.6) | collective-permute-done | bytes 98336 | tf_op jit(solution)/shard_map/ppermute | solution.py:55
  27.5 2.4 %collective-permute-start.7 = (bf16[32,384]{1,0:T(8,128)(2,1)S(1)}, bf16[32,384]{1,0:T(8,128)(2,1)S(1)}, u32[]{:S(2)}, u32[]{:S(2)}) collective-permute-start(bf16[32,384]{1,0:T(8,128)(2,1)S(1)} %broadcast_select_fusion.2), channel_id=1, source_target_pairs={{0,7},{1,6},{2,5},{3,4},{4,3},{5,2},{6,1},{7,0},{8,15},{9,14},{10,... | collective-permute-start | bytes 73736 | tf_op jit(solution)/shard_map/ppermute | solution.py:21
  29.9 0.0 collective-permute-start.8
  29.9 2.7 %collective-permute-done.7 = bf16[32,384]{1,0:T(8,128)(2,1)S(1)} collective-permute-done((bf16[32,384]{1,0:T(8,128)(2,1)S(1)}, bf16[32,384]{1,0:T(8,128)(2,1)S(1)}, u32[]{:S(2)}, u32[]{:S(2)}) %collective-permute-start.7) | collective-permute-done | bytes 24608 | tf_op jit(solution)/shard_map/ppermute | solution.py:21
  32.6 0.8 %collective-permute-done.8 = bf16[32,384]{1,0:T(8,128)(2,1)S(1)} collective-permute-done((bf16[32,384]{1,0:T(8,128)(2,1)S(1)}, bf16[32,384]{1,0:T(8,128)(2,1)S(1)}, u32[]{:S(2)}, u32[]{:S(2)}) %collective-permute-start.8) | collective-permute-done | bytes 24608 | tf_op jit(solution)/shard_map/ppermute | solution.py:21
  33.5 1.3 %collective-permute-start.11 = (bf16[64,384]{1,0:T(8,128)(2,1)S(1)}, bf16[64,384]{1,0:T(8,128)(2,1)S(1)}, u32[]{:S(2)}, u32[]{:S(2)}) collective-permute-start(bf16[64,384]{1,0:T(8,128)(2,1)S(1)} %pad_maximum_fusion.3.refs_3_), channel_id=1, source_target_pairs={{0,28},{4,24},{8,20},{12,16},{16,12},{20,8},{24,4},{28,0},{1,29},{... | collective-permute-start | bytes 147464 | tf_op jit(solution)/shard_map/ppermute | solution.py:75
  34.8 1.0 %collective-permute-start.10 = (bf16[64,384]{1,0:T(8,128)(2,1)S(1)}, bf16[64,384]{1,0:T(8,128)(2,1)S(1)}, u32[]{:S(2)}, u32[]{:S(2)}) collective-permute-start(bf16[64,384]{1,0:T(8,128)(2,1)S(1)} %pad_maximum_fusion.3.refs_3_), channel_id=1, source_target_pairs={{0,20},{4,16},{8,28},{12,24},{16,4},{20,0},{24,12},{28,8},{1,21},{... | collective-permute-start | bytes 147464 | tf_op jit(solution)/shard_map/ppermute | solution.py:75
  35.8 0.7 %collective-permute-start.9 = (bf16[64,384]{1,0:T(8,128)(2,1)S(1)}, bf16[64,384]{1,0:T(8,128)(2,1)S(1)}, u32[]{:S(2)}, u32[]{:S(2)}) collective-permute-start(bf16[64,384]{1,0:T(8,128)(2,1)S(1)} %pad_maximum_fusion.3.refs_3_), channel_id=1, source_target_pairs={{0,12},{4,8},{8,4},{12,0},{16,28},{20,24},{24,20},{28,16},{1,13},{... | collective-permute-start | bytes 147464 | tf_op jit(solution)/shard_map/ppermute | solution.py:75
  36.5 1.8 %collective-permute-done.11.refs_2_ = bf16[64,384]{1,0:T(8,128)(2,1)S(1)} collective-permute-done((bf16[64,384]{1,0:T(8,128)(2,1)S(1)}, bf16[64,384]{1,0:T(8,128)(2,1)S(1)}, u32[]{:S(2)}, u32[]{:S(2)}) %collective-permute-start.11) | collective-permute-done | bytes 49184 | tf_op jit(solution)/shard_map/ppermute | solution.py:75
  38.2 1.2 %collective-permute-done.10.refs_1_ = bf16[64,384]{1,0:T(8,128)(2,1)S(1)} collective-permute-done((bf16[64,384]{1,0:T(8,128)(2,1)S(1)}, bf16[64,384]{1,0:T(8,128)(2,1)S(1)}, u32[]{:S(2)}, u32[]{:S(2)}) %collective-permute-start.10) | collective-permute-done | bytes 49184 | tf_op jit(solution)/shard_map/ppermute | solution.py:75
  39.5 0.1 collective-permute-done.9.refs_0_
  39.6 3.3 %sweep_step.3 = (f32[16,384]{1,0:T(8,128)}, f32[64,384]{1,0:T(8,128)S(1)}) custom-call(s32[2,16]{1,0:T(2,128)S(1)} %bitcast.4, f32[16,384]{1,0:T(8,128)S(1)} %get-tuple-element.18.live_ref, bf16[16,768,384]{2,1,0:T(8,128)(2,1)S(1)} %get-tuple-element.19.jac_ref, bf16[16,384,768]{2,1,0:T(8,128)(2,1)S(1)} %get-tuple-element.20.turned_ref, ...), custom_call_target="tpu_custom_call" | custom-call | flops 18874368 | bytes 18874368 | tf_op jit(solution)/shard_map/sweep_step/pallas_call | solution.py:215
  42.9 0.2 collective-permute-start.12
  43.0 1.2 %collective-permute-done.12 = f32[64,384]{1,0:T(8,128)S(1)} collective-permute-done((f32[64,384]{1,0:T(8,128)S(1)}, f32[64,384]{1,0:T(8,128)S(1)}, u32[]{:S(2)}, u32[]{:S(2)}) %collective-permute-start.12) | collective-permute-done | bytes 98336 | tf_op jit(solution)/shard_map/ppermute | solution.py:55
  44.3 0.1 collective-permute-start.13
  44.4 5.0 %collective-permute-done.13 = bf16[32,384]{1,0:T(8,128)(2,1)S(1)} collective-permute-done((bf16[32,384]{1,0:T(8,128)(2,1)S(1)}, bf16[32,384]{1,0:T(8,128)(2,1)S(1)}, u32[]{:S(2)}, u32[]{:S(2)}) %collective-permute-start.13) | collective-permute-done | bytes 24608 | tf_op jit(solution)/shard_map/ppermute | solution.py:21
  49.4 1.8 %collective-permute-start.16 = (bf16[32,384]{1,0:T(8,128)(2,1)S(1)}, bf16[32,384]{1,0:T(8,128)(2,1)S(1)}, u32[]{:S(2)}, u32[]{:S(2)}) collective-permute-start(bf16[32,384]{1,0:T(8,128)(2,1)S(1)} %fusion.4), channel_id=1, source_target_pairs={{0,28},{4,24},{8,20},{12,16},{16,12},{20,8},{24,4},{28,0},{1,29},{... | collective-permute-start | bytes 73736 | tf_op jit(solution)/shard_map/ppermute | solution.py:75
  51.2 0.4 collective-permute-start.15
  51.6 0.8 %collective-permute-start.14 = (bf16[32,384]{1,0:T(8,128)(2,1)S(1)}, bf16[32,384]{1,0:T(8,128)(2,1)S(1)}, u32[]{:S(2)}, u32[]{:S(2)}) collective-permute-start(bf16[32,384]{1,0:T(8,128)(2,1)S(1)} %fusion.4), channel_id=1, source_target_pairs={{0,12},{4,8},{8,4},{12,0},{16,28},{20,24},{24,20},{28,16},{1,13},{... | collective-permute-start | bytes 73736 | tf_op jit(solution)/shard_map/ppermute | solution.py:75
  52.4 1.2 %collective-permute-done.16 = bf16[32,384]{1,0:T(8,128)(2,1)S(1)} collective-permute-done((bf16[32,384]{1,0:T(8,128)(2,1)S(1)}, bf16[32,384]{1,0:T(8,128)(2,1)S(1)}, u32[]{:S(2)}, u32[]{:S(2)}) %collective-permute-start.16) | collective-permute-done | bytes 24608 | tf_op jit(solution)/shard_map/ppermute | solution.py:75
  53.6 0.8 %collective-permute-done.15 = bf16[32,384]{1,0:T(8,128)(2,1)S(1)} collective-permute-done((bf16[32,384]{1,0:T(8,128)(2,1)S(1)}, bf16[32,384]{1,0:T(8,128)(2,1)S(1)}, u32[]{:S(2)}, u32[]{:S(2)}) %collective-permute-start.15) | collective-permute-done | bytes 24608 | tf_op jit(solution)/shard_map/ppermute | solution.py:75
  54.4 0.4 collective-permute-done.14
  54.9 0.6 %multiply_add_fusion = f32[32,384]{1,0:T(8,128)} fusion(f32[32,384]{1,0:T(8,128)S(1)} %copy-done.5, f32[32,384]{1,0:T(8,128)S(1)} %copy-done.4, bf16[32,384]{1,0:T(8,128)(2,1)S(1)} %fusion.4, bf16[32,384]{1,0:T(8,128)(2,1)S(1)} %collective-permute-done.16, bf16[32,384]{1,0:T(8,128)(2,1)S(1)} %collective-permute-done.15, ...), kind=kLoop, calls=%fused_computation.13 | loop fusion | flops 110592 | bytes 245760 | tf_op jit(solution)/shard_map/add | solution.py:266
  (16 shorter events, 0.2 us)
Async XLA Ops:
  0.6 22.3 %copy-start.3 = (s32[16,2]{0,1:T(2,128)S(1)}, s32[16,2]{0,1:T(2,128)}, u32[]{:S(2)}) copy-start(s32[16,2]{0,1:T(2,128)} %param.10) | copy-start | bytes 388
  0.6 6.6 %copy-start.4 = (f32[32,384]{1,0:T(8,128)S(1)}, f32[32,384]{1,0:T(8,128)}, u32[]{:S(2)}) copy-start(f32[32,384]{1,0:T(8,128)} %param.13) | copy-start | bytes 147460
  0.7 7.6 %copy-start.5 = (f32[32,384]{1,0:T(8,128)S(1)}, f32[32,384]{1,0:T(8,128)}, u32[]{:S(2)}) copy-start(f32[32,384]{1,0:T(8,128)} %param.12) | copy-start | bytes 147460
  0.7 22.3 %copy-start.2 = (f32[16,128]{1,0:T(8,128)S(1)}, f32[16,128]{1,0:T(8,128)}, u32[]{:S(2)}) copy-start(f32[16,128]{1,0:T(8,128)} %friction_ref.3) | copy-start | bytes 24580
  0.7 22.3 %copy-start.1 = (f32[16,384]{1,0:T(8,128)S(1)}, f32[16,384]{1,0:T(8,128)}, u32[]{:S(2)}) copy-start(f32[16,384]{1,0:T(8,128)} %step_ref.3) | copy-start | bytes 73732
  0.7 22.2 %copy-start = (f32[16,384]{1,0:T(8,128)S(1)}, f32[16,384]{1,0:T(8,128)}, u32[]{:S(2)}) copy-start(f32[16,384]{1,0:T(8,128)} %bias_ref.3) | copy-start | bytes 73732
  6.7 1.5 %collective-permute-start = (f32[64,384]{1,0:T(8,128)S(1)}, f32[64,384]{1,0:T(8,128)S(1)}, u32[]{:S(2)}, u32[]{:S(2)}) collective-permute-start(f32[64,384]{1,0:T(8,128)S(1)} %get-tuple-element.22), channel_id=1, source_target_pairs={{0,4},{4,0},{8,12},{12,8},{16,20},{20,16},{24,28},{28,24},{1,5},{5... | collective-permute-start | bytes 294920 | tf_op jit(solution)/shard_map/ppermute | solution.py:55
  8.3 6.9 %collective-permute-start.1 = (bf16[64,384]{1,0:T(8,128)(2,1)S(1)}, bf16[64,384]{1,0:T(8,128)(2,1)S(1)}, u32[]{:S(2)}, u32[]{:S(2)}) collective-permute-start(bf16[64,384]{1,0:T(8,128)(2,1)S(1)} %get-tuple-element.24), channel_id=1, source_target_pairs={{0,7},{1,6},{2,5},{3,4},{4,3},{5,2},{6,1},{7,0},{8,15},{9,14},{10,... | collective-permute-start | bytes 147464 | tf_op jit(solution)/shard_map/ppermute | solution.py:21
  13.1 3.5 %collective-permute-start.2 = (bf16[64,384]{1,0:T(8,128)(2,1)S(1)}, bf16[64,384]{1,0:T(8,128)(2,1)S(1)}, u32[]{:S(2)}, u32[]{:S(2)}) collective-permute-start(bf16[64,384]{1,0:T(8,128)(2,1)S(1)} %get-tuple-element.25), channel_id=1, source_target_pairs={{0,5},{1,4},{2,7},{3,6},{4,1},{5,0},{6,3},{7,2},{8,13},{9,12},{10,... | collective-permute-start | bytes 147464 | tf_op jit(solution)/shard_map/ppermute | solution.py:21
  16.7 4.5 %collective-permute-start.5 = (bf16[64,384]{1,0:T(8,128)(2,1)S(1)}, bf16[64,384]{1,0:T(8,128)(2,1)S(1)}, u32[]{:S(2)}, u32[]{:S(2)}) collective-permute-start(bf16[64,384]{1,0:T(8,128)(2,1)S(1)} %pad_maximum_fusion.2.refs_3_), channel_id=1, source_target_pairs={{0,28},{4,24},{8,20},{12,16},{16,12},{20,8},{24,4},{28,0},{1,29},{... | collective-permute-start | bytes 147464 | tf_op jit(solution)/shard_map/ppermute | solution.py:75
  19.1 3.7 %collective-permute-start.4 = (bf16[64,384]{1,0:T(8,128)(2,1)S(1)}, bf16[64,384]{1,0:T(8,128)(2,1)S(1)}, u32[]{:S(2)}, u32[]{:S(2)}) collective-permute-start(bf16[64,384]{1,0:T(8,128)(2,1)S(1)} %pad_maximum_fusion.2.refs_3_), channel_id=1, source_target_pairs={{0,20},{4,16},{8,28},{12,24},{16,4},{20,0},{24,12},{28,8},{1,21},{... | collective-permute-start | bytes 147464 | tf_op jit(solution)/shard_map/ppermute | solution.py:75
  19.4 3.5 %collective-permute-start.3 = (bf16[64,384]{1,0:T(8,128)(2,1)S(1)}, bf16[64,384]{1,0:T(8,128)(2,1)S(1)}, u32[]{:S(2)}, u32[]{:S(2)}) collective-permute-start(bf16[64,384]{1,0:T(8,128)(2,1)S(1)} %pad_maximum_fusion.2.refs_3_), channel_id=1, source_target_pairs={{0,12},{4,8},{8,4},{12,0},{16,28},{20,24},{24,20},{28,16},{1,13},{... | collective-permute-start | bytes 147464 | tf_op jit(solution)/shard_map/ppermute | solution.py:75
  26.1 1.4 %collective-permute-start.6 = (f32[64,384]{1,0:T(8,128)S(1)}, f32[64,384]{1,0:T(8,128)S(1)}, u32[]{:S(2)}, u32[]{:S(2)}) collective-permute-start(f32[64,384]{1,0:T(8,128)S(1)} %get-tuple-element.27), channel_id=1, source_target_pairs={{0,4},{4,0},{8,12},{12,8},{16,20},{20,16},{24,28},{28,24},{1,5},{5... | collective-permute-start | bytes 294920 | tf_op jit(solution)/shard_map/ppermute | solution.py:55
  27.5 5.1 %collective-permute-start.7 = (bf16[32,384]{1,0:T(8,128)(2,1)S(1)}, bf16[32,384]{1,0:T(8,128)(2,1)S(1)}, u32[]{:S(2)}, u32[]{:S(2)}) collective-permute-start(bf16[32,384]{1,0:T(8,128)(2,1)S(1)} %broadcast_select_fusion.2), channel_id=1, source_target_pairs={{0,7},{1,6},{2,5},{3,4},{4,3},{5,2},{6,1},{7,0},{8,15},{9,14},{10,... | collective-permute-start | bytes 73736 | tf_op jit(solution)/shard_map/ppermute | solution.py:21
  29.9 3.6 %collective-permute-start.8 = (bf16[32,384]{1,0:T(8,128)(2,1)S(1)}, bf16[32,384]{1,0:T(8,128)(2,1)S(1)}, u32[]{:S(2)}, u32[]{:S(2)}) collective-permute-start(bf16[32,384]{1,0:T(8,128)(2,1)S(1)} %get-tuple-element.29), channel_id=1, source_target_pairs={{0,5},{1,4},{2,7},{3,6},{4,1},{5,0},{6,3},{7,2},{8,13},{9,12},{10,... | collective-permute-start | bytes 73736 | tf_op jit(solution)/shard_map/ppermute | solution.py:21
  33.5 4.8 %collective-permute-start.11 = (bf16[64,384]{1,0:T(8,128)(2,1)S(1)}, bf16[64,384]{1,0:T(8,128)(2,1)S(1)}, u32[]{:S(2)}, u32[]{:S(2)}) collective-permute-start(bf16[64,384]{1,0:T(8,128)(2,1)S(1)} %pad_maximum_fusion.3.refs_3_), channel_id=1, source_target_pairs={{0,28},{4,24},{8,20},{12,16},{16,12},{20,8},{24,4},{28,0},{1,29},{... | collective-permute-start | bytes 147464 | tf_op jit(solution)/shard_map/ppermute | solution.py:75
  34.8 4.7 %collective-permute-start.10 = (bf16[64,384]{1,0:T(8,128)(2,1)S(1)}, bf16[64,384]{1,0:T(8,128)(2,1)S(1)}, u32[]{:S(2)}, u32[]{:S(2)}) collective-permute-start(bf16[64,384]{1,0:T(8,128)(2,1)S(1)} %pad_maximum_fusion.3.refs_3_), channel_id=1, source_target_pairs={{0,20},{4,16},{8,28},{12,24},{16,4},{20,0},{24,12},{28,8},{1,21},{... | collective-permute-start | bytes 147464 | tf_op jit(solution)/shard_map/ppermute | solution.py:75
  35.8 3.8 %collective-permute-start.9 = (bf16[64,384]{1,0:T(8,128)(2,1)S(1)}, bf16[64,384]{1,0:T(8,128)(2,1)S(1)}, u32[]{:S(2)}, u32[]{:S(2)}) collective-permute-start(bf16[64,384]{1,0:T(8,128)(2,1)S(1)} %pad_maximum_fusion.3.refs_3_), channel_id=1, source_target_pairs={{0,12},{4,8},{8,4},{12,0},{16,28},{20,24},{24,20},{28,16},{1,13},{... | collective-permute-start | bytes 147464 | tf_op jit(solution)/shard_map/ppermute | solution.py:75
  42.9 1.4 %collective-permute-start.12 = (f32[64,384]{1,0:T(8,128)S(1)}, f32[64,384]{1,0:T(8,128)S(1)}, u32[]{:S(2)}, u32[]{:S(2)}) collective-permute-start(f32[64,384]{1,0:T(8,128)S(1)} %get-tuple-element.31), channel_id=1, source_target_pairs={{0,4},{4,0},{8,12},{12,8},{16,20},{20,16},{24,28},{28,24},{1,5},{5... | collective-permute-start | bytes 294920 | tf_op jit(solution)/shard_map/ppermute | solution.py:55
  44.3 5.1 %collective-permute-start.13 = (bf16[32,384]{1,0:T(8,128)(2,1)S(1)}, bf16[32,384]{1,0:T(8,128)(2,1)S(1)}, u32[]{:S(2)}, u32[]{:S(2)}) collective-permute-start(bf16[32,384]{1,0:T(8,128)(2,1)S(1)} %slice.78), channel_id=1, source_target_pairs={{0,5},{1,6},{2,7},{3,4},{4,1},{5,2},{6,3},{7,0},{8,13},{9,14},{10,... | collective-permute-start | bytes 73736 | tf_op jit(solution)/shard_map/ppermute | solution.py:21
  49.4 4.2 %collective-permute-start.16 = (bf16[32,384]{1,0:T(8,128)(2,1)S(1)}, bf16[32,384]{1,0:T(8,128)(2,1)S(1)}, u32[]{:S(2)}, u32[]{:S(2)}) collective-permute-start(bf16[32,384]{1,0:T(8,128)(2,1)S(1)} %fusion.4), channel_id=1, source_target_pairs={{0,28},{4,24},{8,20},{12,16},{16,12},{20,8},{24,4},{28,0},{1,29},{... | collective-permute-start | bytes 73736 | tf_op jit(solution)/shard_map/ppermute | solution.py:75
  51.2 3.3 %collective-permute-start.15 = (bf16[32,384]{1,0:T(8,128)(2,1)S(1)}, bf16[32,384]{1,0:T(8,128)(2,1)S(1)}, u32[]{:S(2)}, u32[]{:S(2)}) collective-permute-start(bf16[32,384]{1,0:T(8,128)(2,1)S(1)} %fusion.4), channel_id=1, source_target_pairs={{0,20},{4,16},{8,28},{12,24},{16,4},{20,0},{24,12},{28,8},{1,21},{... | collective-permute-start | bytes 73736 | tf_op jit(solution)/shard_map/ppermute | solution.py:75
  51.6 3.3 %collective-permute-start.14 = (bf16[32,384]{1,0:T(8,128)(2,1)S(1)}, bf16[32,384]{1,0:T(8,128)(2,1)S(1)}, u32[]{:S(2)}, u32[]{:S(2)}) collective-permute-start(bf16[32,384]{1,0:T(8,128)(2,1)S(1)} %fusion.4), channel_id=1, source_target_pairs={{0,12},{4,8},{8,4},{12,0},{16,28},{20,24},{24,20},{28,16},{1,13},{... | collective-permute-start | bytes 73736 | tf_op jit(solution)/shard_map/ppermute | solution.py:75

commit v4 on v3

--- a/solution.py
+++ b/solution.py
@@ -29,11 +29,8 @@
     both = lambda value: jnp.concatenate([value, *extra]) if extra else value
     if lax.axis_size("body") % 2:
         return crossed(ahead, ahead_of), crossed(both(back), lambda place: place - 1)
-    far, close = lax.optimization_barrier(
-        (both(jnp.where(even, back, ahead)), both(jnp.where(even, ahead, back)))
-    )
-    wide = crossed(far, lambda place: place + 2 * (place % 2) - 1)
-    near = crossed(close, lambda place: place ^ 1)
+    near = crossed(both(jnp.where(even, ahead, back)), lambda place: place ^ 1)
+    wide = crossed(both(jnp.where(even, back, ahead)), lambda place: place + 2 * (place % 2) - 1)
     rows = ahead.shape[0]
     return jnp.where(even, wide[:rows], near[:rows]), jnp.where(even, near, wide)
 

time: 55.7 us -> 56.1 us (level)
    ppermute x5, waiting for transfers between devices: 12.1 us -> 12.6 us  [crossed(): return lax.ppermute(value, ('contact', 'body'), pairs)]
  transfers between devices with their start and end apart: 17 -> 17, of which waited for: 17 -> 16; matrix products, arithmetic and copies ran while one was open for 0% -> 0% of each run, Pallas kernels for 0% -> 0%
where the time goes in v4:
time: 56.1 us; the launch traced here: 55.9 us
  waiting for transfers between devices  23.8 us (42%)
  starting transfers between devices  17.9 us (32%)
  Pallas kernels  11.8 us (21%)
  between operations  1.48 us (3%)
  other arithmetic  0.85 us (2%)
    ppermute x5, waiting for transfers between devices, crossed(): return lax.ppermute(value, ('contact', 'body'), pairs)  12.6 us
    ppermute x9, starting transfers between devices, over_pairs(): parts.append(lax.ppermute(value, 'contact', pairs))  9.5 us
    ppermute x9, waiting for transfers between devices, over_pairs(): parts.append(lax.ppermute(value, 'contact', pairs))  8.14 us
    ppermute x5, starting transfers between devices, crossed(): return lax.ppermute(value, ('contact', 'body'), pairs)  7.29 us
    pallas_call x2, Pallas kernels, sweep_step(): pl.pallas_call(functools.partial(sweep_kernel, len(parts)), out_shape=res...  6.41 us
    pallas_call x1, Pallas kernels, first_push(): pl.pallas_call(first_kernel, out_shape=[pltpu.VMEM((tiles, rows, cols), j...  5.38 us
    ppermute x3, waiting for transfers between devices, pair_sum(): lax.ppermute(value, 'contact', [(place, place ^ 1) for place in range(cou...  3.04 us
    ppermute x3, starting transfers between devices, pair_sum(): lax.ppermute(value, 'contact', [(place, place ^ 1) for place in range(cou...  1.14 us
  transfers between devices with their start and end apart: 17, of which 16 were waited for; matrix products, arithmetic and copies ran while one was open for 0% of the time, Pallas kernels for 0%

profile of v4, /device:TPU:0, one launch (start us, length us, event | category | flops | bytes accessed | tf_op | source)
XLA Modules:
  0.0 55.9 jit_solution(17843947374166333400)
XLA Ops:
  0.6 0.0 copy-start.3
  0.6 0.0 copy-start.4
  0.7 0.0 copy-start.5
  0.7 0.0 copy-start.2
  0.7 0.0 copy-start.1
  0.7 0.0 copy-start
  1.4 5.4 %first_push.1 = (bf16[16,768,384]{2,1,0:T(8,128)(2,1)S(1)}, bf16[16,384,768]{2,1,0:T(8,128)(2,1)S(1)}, f32[16,384]{1,0:T(8,128)S(1)}, f32[16,384]{1,0:T(8,128)S(1)}, f32[64,384]{1,0:T(8,128)S(1)}) custom-call(s32[1]{0:T(128)S(6)} %copy.11.count_ref, s32[2,16]{1,0:T(2,128)} %bitcast.2, bf16[16,768,384]{2,1,0:T(8,128)(2,1)} %bitcast.5, f32[16,384]{1,0:T(8,128)} %start_ref.1), custom_call_target="tpu_custom_call" | custom-call | flops 9437184 | bytes 9437184 | tf_op jit(solution)/shard_map/first_push/pallas_call | solution.py:186
  6.7 0.5 collective-permute-start
  7.3 0.0 copy-done.4
  7.3 0.9 %collective-permute-done = f32[64,384]{1,0:T(8,128)S(1)} collective-permute-done((f32[64,384]{1,0:T(8,128)S(1)}, f32[64,384]{1,0:T(8,128)S(1)}, u32[]{:S(2)}, u32[]{:S(2)}) %collective-permute-start) | collective-permute-done | bytes 98336 | tf_op jit(solution)/shard_map/ppermute | solution.py:52
  8.2 0.0 copy-done.5
  8.3 4.8 %collective-permute-start.1 = (bf16[64,384]{1,0:T(8,128)(2,1)S(1)}, bf16[64,384]{1,0:T(8,128)(2,1)S(1)}, u32[]{:S(2)}, u32[]{:S(2)}) collective-permute-start(bf16[64,384]{1,0:T(8,128)(2,1)S(1)} %get-tuple-element.32), channel_id=1, source_target_pairs={{0,7},{1,6},{2,5},{3,4},{4,3},{5,2},{6,1},{7,0},{8,15},{9,14},{10,... | collective-permute-start | bytes 147464 | tf_op jit(solution)/shard_map/ppermute | solution.py:21
  13.1 0.0 collective-permute-start.2
  13.1 2.1 %collective-permute-done.1 = bf16[64,384]{1,0:T(8,128)(2,1)S(1)} collective-permute-done((bf16[64,384]{1,0:T(8,128)(2,1)S(1)}, bf16[64,384]{1,0:T(8,128)(2,1)S(1)}, u32[]{:S(2)}, u32[]{:S(2)}) %collective-permute-start.1) | collective-permute-done | bytes 49184 | tf_op jit(solution)/shard_map/ppermute | solution.py:21
  15.2 1.4 %collective-permute-done.2 = bf16[64,384]{1,0:T(8,128)(2,1)S(1)} collective-permute-done((bf16[64,384]{1,0:T(8,128)(2,1)S(1)}, bf16[64,384]{1,0:T(8,128)(2,1)S(1)}, u32[]{:S(2)}, u32[]{:S(2)}) %collective-permute-start.2) | collective-permute-done | bytes 49184 | tf_op jit(solution)/shard_map/ppermute | solution.py:21
  16.7 2.5 %collective-permute-start.5 = (bf16[64,384]{1,0:T(8,128)(2,1)S(1)}, bf16[64,384]{1,0:T(8,128)(2,1)S(1)}, u32[]{:S(2)}, u32[]{:S(2)}) collective-permute-start(bf16[64,384]{1,0:T(8,128)(2,1)S(1)} %pad_maximum_fusion.2.refs_3_), channel_id=1, source_target_pairs={{0,28},{4,24},{8,20},{12,16},{16,12},{20,8},{24,4},{28,0},{1,29},{... | collective-permute-start | bytes 147464 | tf_op jit(solution)/shard_map/ppermute | solution.py:72
  19.1 0.3 collective-permute-start.4
  19.4 0.5 collective-permute-start.3
  19.9 1.3 %collective-permute-done.5.refs_2_ = bf16[64,384]{1,0:T(8,128)(2,1)S(1)} collective-permute-done((bf16[64,384]{1,0:T(8,128)(2,1)S(1)}, bf16[64,384]{1,0:T(8,128)(2,1)S(1)}, u32[]{:S(2)}, u32[]{:S(2)}) %collective-permute-start.5) | collective-permute-done | bytes 49184 | tf_op jit(solution)/shard_map/ppermute | solution.py:72
  21.1 1.7 %collective-permute-done.4.refs_1_ = bf16[64,384]{1,0:T(8,128)(2,1)S(1)} collective-permute-done((bf16[64,384]{1,0:T(8,128)(2,1)S(1)}, bf16[64,384]{1,0:T(8,128)(2,1)S(1)}, u32[]{:S(2)}, u32[]{:S(2)}) %collective-permute-start.4) | collective-permute-done | bytes 49184 | tf_op jit(solution)/shard_map/ppermute | solution.py:72
  22.8 0.1 collective-permute-done.3.refs_0_
  22.9 0.0 copy-done.3
  22.9 0.0 copy-done.2
  22.9 0.0 copy-done.1
  22.9 0.0 copy-done
  22.9 3.1 %sweep_step.2 = (f32[16,384]{1,0:T(8,128)S(1)}, f32[64,384]{1,0:T(8,128)S(1)}) custom-call(s32[2,16]{1,0:T(2,128)S(1)} %bitcast.3, f32[16,384]{1,0:T(8,128)S(1)} %get-tuple-element.14.live_ref, bf16[16,768,384]{2,1,0:T(8,128)(2,1)S(1)} %get-tuple-element.15.jac_ref, bf16[16,384,768]{2,1,0:T(8,128)(2,1)S(1)} %get-tuple-element.16.turned_ref, ...), custom_call_target="tpu_custom_call" | custom-call | flops 18874368 | bytes 18874368 | tf_op jit(solution)/shard_map/sweep_step/pallas_call | solution.py:212
  26.1 0.4 collective-permute-start.6
  26.5 1.0 %collective-permute-done.6 = f32[64,384]{1,0:T(8,128)S(1)} collective-permute-done((f32[64,384]{1,0:T(8,128)S(1)}, f32[64,384]{1,0:T(8,128)S(1)}, u32[]{:S(2)}, u32[]{:S(2)}) %collective-permute-start.6) | collective-permute-done | bytes 98336 | tf_op jit(solution)/shard_map/ppermute | solution.py:52
  27.5 1.5 %collective-permute-start.8 = (bf16[32,384]{1,0:T(8,128)(2,1)S(1)}, bf16[32,384]{1,0:T(8,128)(2,1)S(1)}, u32[]{:S(2)}, u32[]{:S(2)}) collective-permute-start(bf16[32,384]{1,0:T(8,128)(2,1)S(1)} %broadcast_select_fusion.1), channel_id=1, source_target_pairs={{0,5},{1,4},{2,7},{3,6},{4,1},{5,0},{6,3},{7,2},{8,13},{9,12},{10,... | collective-permute-start | bytes 73736 | tf_op jit(solution)/shard_map/ppermute | solution.py:21
  29.0 1.0 %collective-permute-start.7 = (bf16[32,384]{1,0:T(8,128)(2,1)S(1)}, bf16[32,384]{1,0:T(8,128)(2,1)S(1)}, u32[]{:S(2)}, u32[]{:S(2)}) collective-permute-start(bf16[32,384]{1,0:T(8,128)(2,1)S(1)} %get-tuple-element.24), channel_id=1, source_target_pairs={{0,7},{1,6},{2,5},{3,4},{4,3},{5,2},{6,1},{7,0},{8,15},{9,14},{10,... | collective-permute-start | bytes 73736 | tf_op jit(solution)/shard_map/ppermute | solution.py:21
  30.0 0.9 %collective-permute-done.8 = bf16[32,384]{1,0:T(8,128)(2,1)S(1)} collective-permute-done((bf16[32,384]{1,0:T(8,128)(2,1)S(1)}, bf16[32,384]{1,0:T(8,128)(2,1)S(1)}, u32[]{:S(2)}, u32[]{:S(2)}) %collective-permute-start.8) | collective-permute-done | bytes 24608 | tf_op jit(solution)/shard_map/ppermute | solution.py:21
  30.8 3.2 %collective-permute-done.7 = bf16[32,384]{1,0:T(8,128)(2,1)S(1)} collective-permute-done((bf16[32,384]{1,0:T(8,128)(2,1)S(1)}, bf16[32,384]{1,0:T(8,128)(2,1)S(1)}, u32[]{:S(2)}, u32[]{:S(2)}) %collective-permute-start.7) | collective-permute-done | bytes 24608 | tf_op jit(solution)/shard_map/ppermute | solution.py:21
  34.1 1.5 %collective-permute-start.11 = (bf16[64,384]{1,0:T(8,128)(2,1)S(1)}, bf16[64,384]{1,0:T(8,128)(2,1)S(1)}, u32[]{:S(2)}, u32[]{:S(2)}) collective-permute-start(bf16[64,384]{1,0:T(8,128)(2,1)S(1)} %pad_maximum_fusion.3.refs_3_), channel_id=1, source_target_pairs={{0,28},{4,24},{8,20},{12,16},{16,12},{20,8},{24,4},{28,0},{1,29},{... | collective-permute-start | bytes 147464 | tf_op jit(solution)/shard_map/ppermute | solution.py:72
  35.6 0.8 %collective-permute-start.10 = (bf16[64,384]{1,0:T(8,128)(2,1)S(1)}, bf16[64,384]{1,0:T(8,128)(2,1)S(1)}, u32[]{:S(2)}, u32[]{:S(2)}) collective-permute-start(bf16[64,384]{1,0:T(8,128)(2,1)S(1)} %pad_maximum_fusion.3.refs_3_), channel_id=1, source_target_pairs={{0,20},{4,16},{8,28},{12,24},{16,4},{20,0},{24,12},{28,8},{1,21},{... | collective-permute-start | bytes 147464 | tf_op jit(solution)/shard_map/ppermute | solution.py:72
  36.4 0.9 %collective-permute-start.9 = (bf16[64,384]{1,0:T(8,128)(2,1)S(1)}, bf16[64,384]{1,0:T(8,128)(2,1)S(1)}, u32[]{:S(2)}, u32[]{:S(2)}) collective-permute-start(bf16[64,384]{1,0:T(8,128)(2,1)S(1)} %pad_maximum_fusion.3.refs_3_), channel_id=1, source_target_pairs={{0,12},{4,8},{8,4},{12,0},{16,28},{20,24},{24,20},{28,16},{1,13},{... | collective-permute-start | bytes 147464 | tf_op jit(solution)/shard_map/ppermute | solution.py:72
  37.3 1.2 %collective-permute-done.11.refs_2_ = bf16[64,384]{1,0:T(8,128)(2,1)S(1)} collective-permute-done((bf16[64,384]{1,0:T(8,128)(2,1)S(1)}, bf16[64,384]{1,0:T(8,128)(2,1)S(1)}, u32[]{:S(2)}, u32[]{:S(2)}) %collective-permute-start.11) | collective-permute-done | bytes 49184 | tf_op jit(solution)/shard_map/ppermute | solution.py:72
  38.6 1.5 %collective-permute-done.10.refs_1_ = bf16[64,384]{1,0:T(8,128)(2,1)S(1)} collective-permute-done((bf16[64,384]{1,0:T(8,128)(2,1)S(1)}, bf16[64,384]{1,0:T(8,128)(2,1)S(1)}, u32[]{:S(2)}, u32[]{:S(2)}) %collective-permute-start.10) | collective-permute-done | bytes 49184 | tf_op jit(solution)/shard_map/ppermute | solution.py:72
  40.1 0.0 collective-permute-done.9.refs_0_
  40.1 3.3 %sweep_step.3 = (f32[16,384]{1,0:T(8,128)}, f32[64,384]{1,0:T(8,128)S(1)}) custom-call(s32[2,16]{1,0:T(2,128)S(1)} %bitcast.4, f32[16,384]{1,0:T(8,128)S(1)} %get-tuple-element.14.live_ref, bf16[16,768,384]{2,1,0:T(8,128)(2,1)S(1)} %get-tuple-element.15.jac_ref, bf16[16,384,768]{2,1,0:T(8,128)(2,1)S(1)} %get-tuple-element.16.turned_ref, ...), custom_call_target="tpu_custom_call" | custom-call | flops 18874368 | bytes 18874368 | tf_op jit(solution)/shard_map/sweep_step/pallas_call | solution.py:212
  43.4 0.2 collective-permute-start.12
  43.6 1.1 %collective-permute-done.12 = f32[64,384]{1,0:T(8,128)S(1)} collective-permute-done((f32[64,384]{1,0:T(8,128)S(1)}, f32[64,384]{1,0:T(8,128)S(1)}, u32[]{:S(2)}, u32[]{:S(2)}) %collective-permute-start.12) | collective-permute-done | bytes 98336 | tf_op jit(solution)/shard_map/ppermute | solution.py:52
  44.8 0.1 collective-permute-start.13
  44.9 5.0 %collective-permute-done.13 = bf16[32,384]{1,0:T(8,128)(2,1)S(1)} collective-permute-done((bf16[32,384]{1,0:T(8,128)(2,1)S(1)}, bf16[32,384]{1,0:T(8,128)(2,1)S(1)}, u32[]{:S(2)}, u32[]{:S(2)}) %collective-permute-start.13) | collective-permute-done | bytes 24608 | tf_op jit(solution)/shard_map/ppermute | solution.py:21
  49.9 1.7 %collective-permute-start.16 = (bf16[32,384]{1,0:T(8,128)(2,1)S(1)}, bf16[32,384]{1,0:T(8,128)(2,1)S(1)}, u32[]{:S(2)}, u32[]{:S(2)}) collective-permute-start(bf16[32,384]{1,0:T(8,128)(2,1)S(1)} %fusion.4), channel_id=1, source_target_pairs={{0,28},{4,24},{8,20},{12,16},{16,12},{20,8},{24,4},{28,0},{1,29},{... | collective-permute-start | bytes 73736 | tf_op jit(solution)/shard_map/ppermute | solution.py:72
  51.6 0.4 collective-permute-start.15
  52.0 0.9 %collective-permute-start.14 = (bf16[32,384]{1,0:T(8,128)(2,1)S(1)}, bf16[32,384]{1,0:T(8,128)(2,1)S(1)}, u32[]{:S(2)}, u32[]{:S(2)}) collective-permute-start(bf16[32,384]{1,0:T(8,128)(2,1)S(1)} %fusion.4), channel_id=1, source_target_pairs={{0,12},{4,8},{8,4},{12,0},{16,28},{20,24},{24,20},{28,16},{1,13},{... | collective-permute-start | bytes 73736 | tf_op jit(solution)/shard_map/ppermute | solution.py:72
  52.9 1.2 %collective-permute-done.16 = bf16[32,384]{1,0:T(8,128)(2,1)S(1)} collective-permute-done((bf16[32,384]{1,0:T(8,128)(2,1)S(1)}, bf16[32,384]{1,0:T(8,128)(2,1)S(1)}, u32[]{:S(2)}, u32[]{:S(2)}) %collective-permute-start.16) | collective-permute-done | bytes 24608 | tf_op jit(solution)/shard_map/ppermute | solution.py:72
  54.1 0.8 %collective-permute-done.15 = bf16[32,384]{1,0:T(8,128)(2,1)S(1)} collective-permute-done((bf16[32,384]{1,0:T(8,128)(2,1)S(1)}, bf16[32,384]{1,0:T(8,128)(2,1)S(1)}, u32[]{:S(2)}, u32[]{:S(2)}) %collective-permute-start.15) | collective-permute-done | bytes 24608 | tf_op jit(solution)/shard_map/ppermute | solution.py:72
  54.9 0.4 collective-permute-done.14
  55.3 0.6 %multiply_add_fusion = f32[32,384]{1,0:T(8,128)} fusion(f32[32,384]{1,0:T(8,128)S(1)} %copy-done.5, f32[32,384]{1,0:T(8,128)S(1)} %copy-done.4, bf16[32,384]{1,0:T(8,128)(2,1)S(1)} %fusion.4, bf16[32,384]{1,0:T(8,128)(2,1)S(1)} %collective-permute-done.16, bf16[32,384]{1,0:T(8,128)(2,1)S(1)} %collective-permute-done.15, ...), kind=kLoop, calls=%fused_computation.13 | loop fusion | flops 110592 | bytes 245760 | tf_op jit(solution)/shard_map/add | solution.py:263
  (16 shorter events, 0.2 us)
Async XLA Ops:
  0.6 22.3 %copy-start.3 = (s32[16,2]{0,1:T(2,128)S(1)}, s32[16,2]{0,1:T(2,128)}, u32[]{:S(2)}) copy-start(s32[16,2]{0,1:T(2,128)} %param.10) | copy-start | bytes 388
  0.6 6.6 %copy-start.4 = (f32[32,384]{1,0:T(8,128)S(1)}, f32[32,384]{1,0:T(8,128)}, u32[]{:S(2)}) copy-start(f32[32,384]{1,0:T(8,128)} %param.13) | copy-start | bytes 147460
  0.7 7.6 %copy-start.5 = (f32[32,384]{1,0:T(8,128)S(1)}, f32[32,384]{1,0:T(8,128)}, u32[]{:S(2)}) copy-start(f32[32,384]{1,0:T(8,128)} %param.12) | copy-start | bytes 147460
  0.7 22.3 %copy-start.2 = (f32[16,128]{1,0:T(8,128)S(1)}, f32[16,128]{1,0:T(8,128)}, u32[]{:S(2)}) copy-start(f32[16,128]{1,0:T(8,128)} %friction_ref.3) | copy-start | bytes 24580
  0.7 22.3 %copy-start.1 = (f32[16,384]{1,0:T(8,128)S(1)}, f32[16,384]{1,0:T(8,128)}, u32[]{:S(2)}) copy-start(f32[16,384]{1,0:T(8,128)} %step_ref.3) | copy-start | bytes 73732
  0.7 22.2 %copy-start = (f32[16,384]{1,0:T(8,128)S(1)}, f32[16,384]{1,0:T(8,128)}, u32[]{:S(2)}) copy-start(f32[16,384]{1,0:T(8,128)} %bias_ref.3) | copy-start | bytes 73732
  6.7 1.5 %collective-permute-start = (f32[64,384]{1,0:T(8,128)S(1)}, f32[64,384]{1,0:T(8,128)S(1)}, u32[]{:S(2)}, u32[]{:S(2)}) collective-permute-start(f32[64,384]{1,0:T(8,128)S(1)} %get-tuple-element.18), channel_id=1, source_target_pairs={{0,4},{4,0},{8,12},{12,8},{16,20},{20,16},{24,28},{28,24},{1,5},{5... | collective-permute-start | bytes 294920 | tf_op jit(solution)/shard_map/ppermute | solution.py:52
  8.3 6.9 %collective-permute-start.1 = (bf16[64,384]{1,0:T(8,128)(2,1)S(1)}, bf16[64,384]{1,0:T(8,128)(2,1)S(1)}, u32[]{:S(2)}, u32[]{:S(2)}) collective-permute-start(bf16[64,384]{1,0:T(8,128)(2,1)S(1)} %get-tuple-element.32), channel_id=1, source_target_pairs={{0,7},{1,6},{2,5},{3,4},{4,3},{5,2},{6,1},{7,0},{8,15},{9,14},{10,... | collective-permute-start | bytes 147464 | tf_op jit(solution)/shard_map/ppermute | solution.py:21
  13.1 3.5 %collective-permute-start.2 = (bf16[64,384]{1,0:T(8,128)(2,1)S(1)}, bf16[64,384]{1,0:T(8,128)(2,1)S(1)}, u32[]{:S(2)}, u32[]{:S(2)}) collective-permute-start(bf16[64,384]{1,0:T(8,128)(2,1)S(1)} %get-tuple-element.33), channel_id=1, source_target_pairs={{0,5},{1,4},{2,7},{3,6},{4,1},{5,0},{6,3},{7,2},{8,13},{9,12},{10,... | collective-permute-start | bytes 147464 | tf_op jit(solution)/shard_map/ppermute | solution.py:21
  16.7 4.5 %collective-permute-start.5 = (bf16[64,384]{1,0:T(8,128)(2,1)S(1)}, bf16[64,384]{1,0:T(8,128)(2,1)S(1)}, u32[]{:S(2)}, u32[]{:S(2)}) collective-permute-start(bf16[64,384]{1,0:T(8,128)(2,1)S(1)} %pad_maximum_fusion.2.refs_3_), channel_id=1, source_target_pairs={{0,28},{4,24},{8,20},{12,16},{16,12},{20,8},{24,4},{28,0},{1,29},{... | collective-permute-start | bytes 147464 | tf_op jit(solution)/shard_map/ppermute | solution.py:72
  19.1 3.7 %collective-permute-start.4 = (bf16[64,384]{1,0:T(8,128)(2,1)S(1)}, bf16[64,384]{1,0:T(8,128)(2,1)S(1)}, u32[]{:S(2)}, u32[]{:S(2)}) collective-permute-start(bf16[64,384]{1,0:T(8,128)(2,1)S(1)} %pad_maximum_fusion.2.refs_3_), channel_id=1, source_target_pairs={{0,20},{4,16},{8,28},{12,24},{16,4},{20,0},{24,12},{28,8},{1,21},{... | collective-permute-start | bytes 147464 | tf_op jit(solution)/shard_map/ppermute | solution.py:72
  19.4 3.5 %collective-permute-start.3 = (bf16[64,384]{1,0:T(8,128)(2,1)S(1)}, bf16[64,384]{1,0:T(8,128)(2,1)S(1)}, u32[]{:S(2)}, u32[]{:S(2)}) collective-permute-start(bf16[64,384]{1,0:T(8,128)(2,1)S(1)} %pad_maximum_fusion.2.refs_3_), channel_id=1, source_target_pairs={{0,12},{4,8},{8,4},{12,0},{16,28},{20,24},{24,20},{28,16},{1,13},{... | collective-permute-start | bytes 147464 | tf_op jit(solution)/shard_map/ppermute | solution.py:72
  26.1 1.4 %collective-permute-start.6 = (f32[64,384]{1,0:T(8,128)S(1)}, f32[64,384]{1,0:T(8,128)S(1)}, u32[]{:S(2)}, u32[]{:S(2)}) collective-permute-start(f32[64,384]{1,0:T(8,128)S(1)} %get-tuple-element.21), channel_id=1, source_target_pairs={{0,4},{4,0},{8,12},{12,8},{16,20},{20,16},{24,28},{28,24},{1,5},{5... | collective-permute-start | bytes 294920 | tf_op jit(solution)/shard_map/ppermute | solution.py:52
  27.5 3.3 %collective-permute-start.8 = (bf16[32,384]{1,0:T(8,128)(2,1)S(1)}, bf16[32,384]{1,0:T(8,128)(2,1)S(1)}, u32[]{:S(2)}, u32[]{:S(2)}) collective-permute-start(bf16[32,384]{1,0:T(8,128)(2,1)S(1)} %broadcast_select_fusion.1), channel_id=1, source_target_pairs={{0,5},{1,4},{2,7},{3,6},{4,1},{5,0},{6,3},{7,2},{8,13},{9,12},{10,... | collective-permute-start | bytes 73736 | tf_op jit(solution)/shard_map/ppermute | solution.py:21
  29.0 5.0 %collective-permute-start.7 = (bf16[32,384]{1,0:T(8,128)(2,1)S(1)}, bf16[32,384]{1,0:T(8,128)(2,1)S(1)}, u32[]{:S(2)}, u32[]{:S(2)}) collective-permute-start(bf16[32,384]{1,0:T(8,128)(2,1)S(1)} %get-tuple-element.24), channel_id=1, source_target_pairs={{0,7},{1,6},{2,5},{3,4},{4,3},{5,2},{6,1},{7,0},{8,15},{9,14},{10,... | collective-permute-start | bytes 73736 | tf_op jit(solution)/shard_map/ppermute | solution.py:21
  34.1 4.5 %collective-permute-start.11 = (bf16[64,384]{1,0:T(8,128)(2,1)S(1)}, bf16[64,384]{1,0:T(8,128)(2,1)S(1)}, u32[]{:S(2)}, u32[]{:S(2)}) collective-permute-start(bf16[64,384]{1,0:T(8,128)(2,1)S(1)} %pad_maximum_fusion.3.refs_3_), channel_id=1, source_target_pairs={{0,28},{4,24},{8,20},{12,16},{16,12},{20,8},{24,4},{28,0},{1,29},{... | collective-permute-start | bytes 147464 | tf_op jit(solution)/shard_map/ppermute | solution.py:72
  35.6 4.5 %collective-permute-start.10 = (bf16[64,384]{1,0:T(8,128)(2,1)S(1)}, bf16[64,384]{1,0:T(8,128)(2,1)S(1)}, u32[]{:S(2)}, u32[]{:S(2)}) collective-permute-start(bf16[64,384]{1,0:T(8,128)(2,1)S(1)} %pad_maximum_fusion.3.refs_3_), channel_id=1, source_target_pairs={{0,20},{4,16},{8,28},{12,24},{16,4},{20,0},{24,12},{28,8},{1,21},{... | collective-permute-start | bytes 147464 | tf_op jit(solution)/shard_map/ppermute | solution.py:72
  36.4 3.7 %collective-permute-start.9 = (bf16[64,384]{1,0:T(8,128)(2,1)S(1)}, bf16[64,384]{1,0:T(8,128)(2,1)S(1)}, u32[]{:S(2)}, u32[]{:S(2)}) collective-permute-start(bf16[64,384]{1,0:T(8,128)(2,1)S(1)} %pad_maximum_fusion.3.refs_3_), channel_id=1, source_target_pairs={{0,12},{4,8},{8,4},{12,0},{16,28},{20,24},{24,20},{28,16},{1,13},{... | collective-permute-start | bytes 147464 | tf_op jit(solution)/shard_map/ppermute | solution.py:72
  43.4 1.4 %collective-permute-start.12 = (f32[64,384]{1,0:T(8,128)S(1)}, f32[64,384]{1,0:T(8,128)S(1)}, u32[]{:S(2)}, u32[]{:S(2)}) collective-permute-start(f32[64,384]{1,0:T(8,128)S(1)} %get-tuple-element.23), channel_id=1, source_target_pairs={{0,4},{4,0},{8,12},{12,8},{16,20},{20,16},{24,28},{28,24},{1,5},{5... | collective-permute-start | bytes 294920 | tf_op jit(solution)/shard_map/ppermute | solution.py:52
  44.8 5.1 %collective-permute-start.13 = (bf16[32,384]{1,0:T(8,128)(2,1)S(1)}, bf16[32,384]{1,0:T(8,128)(2,1)S(1)}, u32[]{:S(2)}, u32[]{:S(2)}) collective-permute-start(bf16[32,384]{1,0:T(8,128)(2,1)S(1)} %slice.78), channel_id=1, source_target_pairs={{0,5},{1,6},{2,7},{3,4},{4,1},{5,2},{6,3},{7,0},{8,13},{9,14},{10,... | collective-permute-start | bytes 73736 | tf_op jit(solution)/shard_map/ppermute | solution.py:21
  49.9 4.2 %collective-permute-start.16 = (bf16[32,384]{1,0:T(8,128)(2,1)S(1)}, bf16[32,384]{1,0:T(8,128)(2,1)S(1)}, u32[]{:S(2)}, u32[]{:S(2)}) collective-permute-start(bf16[32,384]{1,0:T(8,128)(2,1)S(1)} %fusion.4), channel_id=1, source_target_pairs={{0,28},{4,24},{8,20},{12,16},{16,12},{20,8},{24,4},{28,0},{1,29},{... | collective-permute-start | bytes 73736 | tf_op jit(solution)/shard_map/ppermute | solution.py:72
  51.6 3.3 %collective-permute-start.15 = (bf16[32,384]{1,0:T(8,128)(2,1)S(1)}, bf16[32,384]{1,0:T(8,128)(2,1)S(1)}, u32[]{:S(2)}, u32[]{:S(2)}) collective-permute-start(bf16[32,384]{1,0:T(8,128)(2,1)S(1)} %fusion.4), channel_id=1, source_target_pairs={{0,20},{4,16},{8,28},{12,24},{16,4},{20,0},{24,12},{28,8},{1,21},{... | collective-permute-start | bytes 73736 | tf_op jit(solution)/shard_map/ppermute | solution.py:72
  52.0 3.3 %collective-permute-start.14 = (bf16[32,384]{1,0:T(8,128)(2,1)S(1)}, bf16[32,384]{1,0:T(8,128)(2,1)S(1)}, u32[]{:S(2)}, u32[]{:S(2)}) collective-permute-start(bf16[32,384]{1,0:T(8,128)(2,1)S(1)} %fusion.4), channel_id=1, source_target_pairs={{0,12},{4,8},{8,4},{12,0},{16,28},{20,24},{24,20},{28,16},{1,13},{... | collective-permute-start | bytes 73736 | tf_op jit(solution)/shard_map/ppermute | solution.py:72

commit v5 on v3

--- a/solution.py
+++ b/solution.py
@@ -148,20 +148,35 @@
     blocks, dofs = vel_ref.shape[0] // 2, vel_ref.shape[1]
     vel_ref[...] = tree([ref[...].astype(jnp.float32) for ref in part_refs])
     sums_ref[...] = jnp.zeros_like(sums_ref)
-    for tile in range(tiles):
-        own_row = vel_ref[pl.ds(block_ref[0, tile], 1), :]
-        next_row = vel_ref[pl.ds(blocks + block_ref[1, tile], 1), :]
-        row = jnp.broadcast_to(jnp.concatenate([own_row, next_row], axis=1), (16, 2 * dofs))
-        rel = jnp.dot(row.astype(jnp.bfloat16), jac_ref[tile], preferred_element_type=jnp.float32)
-        rel_ref[pl.ds(tile, 1), :] = rel[:1]
-    trial = old_ref[...] - step_ref[...] * (rel_ref[...] + bias_ref[...])
-    lam = project(trial, friction_ref[...], friction_ref.shape[1])
-    lam_ref[...] = lam * live_ref[...]
+    step = 8 if tiles % 8 == 0 else tiles
+    halves = [range(first, first + step) for first in range(0, tiles, step)]
+
+    def rel_tiles(half):
+        for tile in half:
+            own_row = vel_ref[pl.ds(block_ref[0, tile], 1), :]
+            next_row = vel_ref[pl.ds(blocks + block_ref[1, tile], 1), :]
+            row = jnp.broadcast_to(jnp.concatenate([own_row, next_row], axis=1), (16, 2 * dofs))
+            rel = jnp.dot(
+                row.astype(jnp.bfloat16), jac_ref[tile], preferred_element_type=jnp.float32
+            )
+            rel_ref[pl.ds(tile, 1), :] = rel[:1]
+
+    def project_tiles(half):
+        part = slice(half[0], half[-1] + 1)
+        trial = old_ref[part] - step_ref[part] * (rel_ref[part] + bias_ref[part])
+        lam = project(trial, friction_ref[part], friction_ref.shape[1])
+        lam_ref[part] = lam * live_ref[part]
+
+    rel_tiles(halves[0])
     copies = [pltpu.make_async_copy(lam_ref, out_ref, held[1])] if held else []
-    for copy in copies:
-        copy.start()
-    for tile in range(tiles):
-        push_tile(tile, lam_ref, turned_ref, block_ref, sums_ref)
+    for half, after in zip(halves, halves[1:] + [[]]):
+        project_tiles(half)
+        rel_tiles(after)
+        if not after:
+            for copy in copies:
+                copy.start()
+        for tile in half:
+            push_tile(tile, lam_ref, turned_ref, block_ref, sums_ref)
     for copy in copies:
         copy.wait()
 

time: 55.7 us -> 55.7 us (level)
  no operation moved by 1% of the time
where the time goes in v5:
time: 55.7 us; the launch traced here: 55.5 us
  waiting for transfers between devices  23.7 us (43%)
  starting transfers between devices  17.7 us (32%)
  Pallas kernels  11.8 us (21%)
  between operations  1.47 us (3%)
  other arithmetic  0.85 us (2%)
    ppermute x5, waiting for transfers between devices, crossed(): return lax.ppermute(value, ('contact', 'body'), pairs)  12.1 us
    ppermute x9, starting transfers between devices, over_pairs(): parts.append(lax.ppermute(value, 'contact', pairs))  9.26 us
    ppermute x9, waiting for transfers between devices, over_pairs(): parts.append(lax.ppermute(value, 'contact', pairs))  8.57 us
    ppermute x5, starting transfers between devices, crossed(): return lax.ppermute(value, ('contact', 'body'), pairs)  7.29 us
    pallas_call x2, Pallas kernels, sweep_step(): pl.pallas_call(functools.partial(sweep_kernel, len(parts)), out_shape=res...  6.41 us
    pallas_call x1, Pallas kernels, first_push(): pl.pallas_call(first_kernel, out_shape=[pltpu.VMEM((tiles, rows, cols), j...  5.38 us
    ppermute x3, waiting for transfers between devices, pair_sum(): lax.ppermute(value, 'contact', [(place, place ^ 1) for place in range(cou...  3.08 us
  transfers between devices with their start and end apart: 17, of which 17 were waited for; matrix products, arithmetic and copies ran while one was open for 0% of the time, Pallas kernels for 0%

profile of v5, /device:TPU:0, one launch (start us, length us, event | category | flops | bytes accessed | tf_op | source)
XLA Modules:
  0.0 55.5 jit_solution(11319783852059809090)
XLA Ops:
  0.6 0.0 copy-start.3
  0.6 0.0 copy-start.4
  0.7 0.0 copy-start.5
  0.7 0.0 copy-start.2
  0.7 0.0 copy-start.1
  0.7 0.0 copy-start
  1.4 5.4 %first_push.1 = (bf16[16,768,384]{2,1,0:T(8,128)(2,1)S(1)}, bf16[16,384,768]{2,1,0:T(8,128)(2,1)S(1)}, f32[16,384]{1,0:T(8,128)S(1)}, f32[16,384]{1,0:T(8,128)S(1)}, f32[64,384]{1,0:T(8,128)S(1)}) custom-call(s32[1]{0:T(128)S(6)} %copy.11.count_ref, s32[2,16]{1,0:T(2,128)} %bitcast.2, bf16[16,768,384]{2,1,0:T(8,128)(2,1)} %bitcast.5, f32[16,384]{1,0:T(8,128)} %start_ref.1), custom_call_target="tpu_custom_call" | custom-call | flops 9437184 | bytes 9437184 | tf_op jit(solution)/shard_map/first_push/pallas_call | solution.py:204
  6.7 0.5 collective-permute-start
  7.3 0.0 copy-done.4
  7.3 0.9 %collective-permute-done = f32[64,384]{1,0:T(8,128)S(1)} collective-permute-done((f32[64,384]{1,0:T(8,128)S(1)}, f32[64,384]{1,0:T(8,128)S(1)}, u32[]{:S(2)}, u32[]{:S(2)}) %collective-permute-start) | collective-permute-done | bytes 98336 | tf_op jit(solution)/shard_map/ppermute | solution.py:55
  8.2 0.0 copy-done.5
  8.3 4.8 %collective-permute-start.1 = (bf16[64,384]{1,0:T(8,128)(2,1)S(1)}, bf16[64,384]{1,0:T(8,128)(2,1)S(1)}, u32[]{:S(2)}, u32[]{:S(2)}) collective-permute-start(bf16[64,384]{1,0:T(8,128)(2,1)S(1)} %get-tuple-element.24), channel_id=1, source_target_pairs={{0,7},{1,6},{2,5},{3,4},{4,3},{5,2},{6,1},{7,0},{8,15},{9,14},{10,... | collective-permute-start | bytes 147464 | tf_op jit(solution)/shard_map/ppermute | solution.py:21
  13.1 0.0 collective-permute-start.2
  13.1 2.1 %collective-permute-done.1 = bf16[64,384]{1,0:T(8,128)(2,1)S(1)} collective-permute-done((bf16[64,384]{1,0:T(8,128)(2,1)S(1)}, bf16[64,384]{1,0:T(8,128)(2,1)S(1)}, u32[]{:S(2)}, u32[]{:S(2)}) %collective-permute-start.1) | collective-permute-done | bytes 49184 | tf_op jit(solution)/shard_map/ppermute | solution.py:21
  15.2 1.4 %collective-permute-done.2 = bf16[64,384]{1,0:T(8,128)(2,1)S(1)} collective-permute-done((bf16[64,384]{1,0:T(8,128)(2,1)S(1)}, bf16[64,384]{1,0:T(8,128)(2,1)S(1)}, u32[]{:S(2)}, u32[]{:S(2)}) %collective-permute-start.2) | collective-permute-done | bytes 49184 | tf_op jit(solution)/shard_map/ppermute | solution.py:21
  16.7 2.5 %collective-permute-start.5 = (bf16[64,384]{1,0:T(8,128)(2,1)S(1)}, bf16[64,384]{1,0:T(8,128)(2,1)S(1)}, u32[]{:S(2)}, u32[]{:S(2)}) collective-permute-start(bf16[64,384]{1,0:T(8,128)(2,1)S(1)} %pad_maximum_fusion.2.refs_3_), channel_id=1, source_target_pairs={{0,28},{4,24},{8,20},{12,16},{16,12},{20,8},{24,4},{28,0},{1,29},{... | collective-permute-start | bytes 147464 | tf_op jit(solution)/shard_map/ppermute | solution.py:75
  19.1 0.3 collective-permute-start.4
  19.4 0.5 collective-permute-start.3
  19.9 1.3 %collective-permute-done.5.refs_2_ = bf16[64,384]{1,0:T(8,128)(2,1)S(1)} collective-permute-done((bf16[64,384]{1,0:T(8,128)(2,1)S(1)}, bf16[64,384]{1,0:T(8,128)(2,1)S(1)}, u32[]{:S(2)}, u32[]{:S(2)}) %collective-permute-start.5) | collective-permute-done | bytes 49184 | tf_op jit(solution)/shard_map/ppermute | solution.py:75
  21.1 1.7 %collective-permute-done.4.refs_1_ = bf16[64,384]{1,0:T(8,128)(2,1)S(1)} collective-permute-done((bf16[64,384]{1,0:T(8,128)(2,1)S(1)}, bf16[64,384]{1,0:T(8,128)(2,1)S(1)}, u32[]{:S(2)}, u32[]{:S(2)}) %collective-permute-start.4) | collective-permute-done | bytes 49184 | tf_op jit(solution)/shard_map/ppermute | solution.py:75
  22.8 0.1 collective-permute-done.3.refs_0_
  22.9 0.0 copy-done.3
  22.9 0.0 copy-done.2
  22.9 0.0 copy-done.1
  22.9 0.0 copy-done
  22.9 3.2 %sweep_step.2 = (f32[16,384]{1,0:T(8,128)S(1)}, f32[64,384]{1,0:T(8,128)S(1)}) custom-call(s32[2,16]{1,0:T(2,128)S(1)} %bitcast.3, f32[16,384]{1,0:T(8,128)S(1)} %get-tuple-element.18.live_ref, bf16[16,768,384]{2,1,0:T(8,128)(2,1)S(1)} %get-tuple-element.19.jac_ref, bf16[16,384,768]{2,1,0:T(8,128)(2,1)S(1)} %get-tuple-element.20.turned_ref, ...), custom_call_target="tpu_custom_call" | custom-call | flops 18874368 | bytes 18874368 | tf_op jit(solution)/shard_map/sweep_step/pallas_call | solution.py:230
  26.1 0.4 collective-permute-start.6
  26.5 1.0 %collective-permute-done.6 = f32[64,384]{1,0:T(8,128)S(1)} collective-permute-done((f32[64,384]{1,0:T(8,128)S(1)}, f32[64,384]{1,0:T(8,128)S(1)}, u32[]{:S(2)}, u32[]{:S(2)}) %collective-permute-start.6) | collective-permute-done | bytes 98336 | tf_op jit(solution)/shard_map/ppermute | solution.py:55
  27.5 2.4 %collective-permute-start.7 = (bf16[32,384]{1,0:T(8,128)(2,1)S(1)}, bf16[32,384]{1,0:T(8,128)(2,1)S(1)}, u32[]{:S(2)}, u32[]{:S(2)}) collective-permute-start(bf16[32,384]{1,0:T(8,128)(2,1)S(1)} %broadcast_select_fusion.2), channel_id=1, source_target_pairs={{0,7},{1,6},{2,5},{3,4},{4,3},{5,2},{6,1},{7,0},{8,15},{9,14},{10,... | collective-permute-start | bytes 73736 | tf_op jit(solution)/shard_map/ppermute | solution.py:21
  29.9 0.0 collective-permute-start.8
  29.9 2.7 %collective-permute-done.7 = bf16[32,384]{1,0:T(8,128)(2,1)S(1)} collective-permute-done((bf16[32,384]{1,0:T(8,128)(2,1)S(1)}, bf16[32,384]{1,0:T(8,128)(2,1)S(1)}, u32[]{:S(2)}, u32[]{:S(2)}) %collective-permute-start.7) | collective-permute-done | bytes 24608 | tf_op jit(solution)/shard_map/ppermute | solution.py:21
  32.6 0.8 %collective-permute-done.8 = bf16[32,384]{1,0:T(8,128)(2,1)S(1)} collective-permute-done((bf16[32,384]{1,0:T(8,128)(2,1)S(1)}, bf16[32,384]{1,0:T(8,128)(2,1)S(1)}, u32[]{:S(2)}, u32[]{:S(2)}) %collective-permute-start.8) | collective-permute-done | bytes 24608 | tf_op jit(solution)/shard_map/ppermute | solution.py:21
  33.5 1.3 %collective-permute-start.11 = (bf16[64,384]{1,0:T(8,128)(2,1)S(1)}, bf16[64,384]{1,0:T(8,128)(2,1)S(1)}, u32[]{:S(2)}, u32[]{:S(2)}) collective-permute-start(bf16[64,384]{1,0:T(8,128)(2,1)S(1)} %pad_maximum_fusion.3.refs_3_), channel_id=1, source_target_pairs={{0,28},{4,24},{8,20},{12,16},{16,12},{20,8},{24,4},{28,0},{1,29},{... | collective-permute-start | bytes 147464 | tf_op jit(solution)/shard_map/ppermute | solution.py:75
  34.8 1.0 %collective-permute-start.10 = (bf16[64,384]{1,0:T(8,128)(2,1)S(1)}, bf16[64,384]{1,0:T(8,128)(2,1)S(1)}, u32[]{:S(2)}, u32[]{:S(2)}) collective-permute-start(bf16[64,384]{1,0:T(8,128)(2,1)S(1)} %pad_maximum_fusion.3.refs_3_), channel_id=1, source_target_pairs={{0,20},{4,16},{8,28},{12,24},{16,4},{20,0},{24,12},{28,8},{1,21},{... | collective-permute-start | bytes 147464 | tf_op jit(solution)/shard_map/ppermute | solution.py:75
  35.8 0.7 %collective-permute-start.9 = (bf16[64,384]{1,0:T(8,128)(2,1)S(1)}, bf16[64,384]{1,0:T(8,128)(2,1)S(1)}, u32[]{:S(2)}, u32[]{:S(2)}) collective-permute-start(bf16[64,384]{1,0:T(8,128)(2,1)S(1)} %pad_maximum_fusion.3.refs_3_), channel_id=1, source_target_pairs={{0,12},{4,8},{8,4},{12,0},{16,28},{20,24},{24,20},{28,16},{1,13},{... | collective-permute-start | bytes 147464 | tf_op jit(solution)/shard_map/ppermute | solution.py:75
  36.5 1.8 %collective-permute-done.11.refs_2_ = bf16[64,384]{1,0:T(8,128)(2,1)S(1)} collective-permute-done((bf16[64,384]{1,0:T(8,128)(2,1)S(1)}, bf16[64,384]{1,0:T(8,128)(2,1)S(1)}, u32[]{:S(2)}, u32[]{:S(2)}) %collective-permute-start.11) | collective-permute-done | bytes 49184 | tf_op jit(solution)/shard_map/ppermute | solution.py:75
  38.3 1.2 %collective-permute-done.10.refs_1_ = bf16[64,384]{1,0:T(8,128)(2,1)S(1)} collective-permute-done((bf16[64,384]{1,0:T(8,128)(2,1)S(1)}, bf16[64,384]{1,0:T(8,128)(2,1)S(1)}, u32[]{:S(2)}, u32[]{:S(2)}) %collective-permute-start.10) | collective-permute-done | bytes 49184 | tf_op jit(solution)/shard_map/ppermute | solution.py:75
  39.5 0.1 collective-permute-done.9.refs_0_
  39.6 3.3 %sweep_step.3 = (f32[16,384]{1,0:T(8,128)}, f32[64,384]{1,0:T(8,128)S(1)}) custom-call(s32[2,16]{1,0:T(2,128)S(1)} %bitcast.4, f32[16,384]{1,0:T(8,128)S(1)} %get-tuple-element.18.live_ref, bf16[16,768,384]{2,1,0:T(8,128)(2,1)S(1)} %get-tuple-element.19.jac_ref, bf16[16,384,768]{2,1,0:T(8,128)(2,1)S(1)} %get-tuple-element.20.turned_ref, ...), custom_call_target="tpu_custom_call" | custom-call | flops 18874368 | bytes 18874368 | tf_op jit(solution)/shard_map/sweep_step/pallas_call | solution.py:230
  42.9 0.2 collective-permute-start.12
  43.0 1.2 %collective-permute-done.12 = f32[64,384]{1,0:T(8,128)S(1)} collective-permute-done((f32[64,384]{1,0:T(8,128)S(1)}, f32[64,384]{1,0:T(8,128)S(1)}, u32[]{:S(2)}, u32[]{:S(2)}) %collective-permute-start.12) | collective-permute-done | bytes 98336 | tf_op jit(solution)/shard_map/ppermute | solution.py:55
  44.3 0.1 collective-permute-start.13
  44.4 5.0 %collective-permute-done.13 = bf16[32,384]{1,0:T(8,128)(2,1)S(1)} collective-permute-done((bf16[32,384]{1,0:T(8,128)(2,1)S(1)}, bf16[32,384]{1,0:T(8,128)(2,1)S(1)}, u32[]{:S(2)}, u32[]{:S(2)}) %collective-permute-start.13) | collective-permute-done | bytes 24608 | tf_op jit(solution)/shard_map/ppermute | solution.py:21
  49.4 1.8 %collective-permute-start.16 = (bf16[32,384]{1,0:T(8,128)(2,1)S(1)}, bf16[32,384]{1,0:T(8,128)(2,1)S(1)}, u32[]{:S(2)}, u32[]{:S(2)}) collective-permute-start(bf16[32,384]{1,0:T(8,128)(2,1)S(1)} %fusion.4), channel_id=1, source_target_pairs={{0,28},{4,24},{8,20},{12,16},{16,12},{20,8},{24,4},{28,0},{1,29},{... | collective-permute-start | bytes 73736 | tf_op jit(solution)/shard_map/ppermute | solution.py:75
  51.2 0.4 collective-permute-start.15
  51.6 0.8 %collective-permute-start.14 = (bf16[32,384]{1,0:T(8,128)(2,1)S(1)}, bf16[32,384]{1,0:T(8,128)(2,1)S(1)}, u32[]{:S(2)}, u32[]{:S(2)}) collective-permute-start(bf16[32,384]{1,0:T(8,128)(2,1)S(1)} %fusion.4), channel_id=1, source_target_pairs={{0,12},{4,8},{8,4},{12,0},{16,28},{20,24},{24,20},{28,16},{1,13},{... | collective-permute-start | bytes 73736 | tf_op jit(solution)/shard_map/ppermute | solution.py:75
  52.4 1.2 %collective-permute-done.16 = bf16[32,384]{1,0:T(8,128)(2,1)S(1)} collective-permute-done((bf16[32,384]{1,0:T(8,128)(2,1)S(1)}, bf16[32,384]{1,0:T(8,128)(2,1)S(1)}, u32[]{:S(2)}, u32[]{:S(2)}) %collective-permute-start.16) | collective-permute-done | bytes 24608 | tf_op jit(solution)/shard_map/ppermute | solution.py:75
  53.6 0.8 %collective-permute-done.15 = bf16[32,384]{1,0:T(8,128)(2,1)S(1)} collective-permute-done((bf16[32,384]{1,0:T(8,128)(2,1)S(1)}, bf16[32,384]{1,0:T(8,128)(2,1)S(1)}, u32[]{:S(2)}, u32[]{:S(2)}) %collective-permute-start.15) | collective-permute-done | bytes 24608 | tf_op jit(solution)/shard_map/ppermute | solution.py:75
  54.4 0.4 collective-permute-done.14
  54.9 0.6 %multiply_add_fusion = f32[32,384]{1,0:T(8,128)} fusion(f32[32,384]{1,0:T(8,128)S(1)} %copy-done.5, f32[32,384]{1,0:T(8,128)S(1)} %copy-done.4, bf16[32,384]{1,0:T(8,128)(2,1)S(1)} %fusion.4, bf16[32,384]{1,0:T(8,128)(2,1)S(1)} %collective-permute-done.16, bf16[32,384]{1,0:T(8,128)(2,1)S(1)} %collective-permute-done.15, ...), kind=kLoop, calls=%fused_computation.13 | loop fusion | flops 110592 | bytes 245760 | tf_op jit(solution)/shard_map/add | solution.py:281
  (16 shorter events, 0.2 us)
Async XLA Ops:
  0.6 22.3 %copy-start.3 = (s32[16,2]{0,1:T(2,128)S(1)}, s32[16,2]{0,1:T(2,128)}, u32[]{:S(2)}) copy-start(s32[16,2]{0,1:T(2,128)} %param.10) | copy-start | bytes 388
  0.6 6.6 %copy-start.4 = (f32[32,384]{1,0:T(8,128)S(1)}, f32[32,384]{1,0:T(8,128)}, u32[]{:S(2)}) copy-start(f32[32,384]{1,0:T(8,128)} %param.13) | copy-start | bytes 147460
  0.7 7.6 %copy-start.5 = (f32[32,384]{1,0:T(8,128)S(1)}, f32[32,384]{1,0:T(8,128)}, u32[]{:S(2)}) copy-start(f32[32,384]{1,0:T(8,128)} %param.12) | copy-start | bytes 147460
  0.7 22.3 %copy-start.2 = (f32[16,128]{1,0:T(8,128)S(1)}, f32[16,128]{1,0:T(8,128)}, u32[]{:S(2)}) copy-start(f32[16,128]{1,0:T(8,128)} %friction_ref.3) | copy-start | bytes 24580
  0.7 22.3 %copy-start.1 = (f32[16,384]{1,0:T(8,128)S(1)}, f32[16,384]{1,0:T(8,128)}, u32[]{:S(2)}) copy-start(f32[16,384]{1,0:T(8,128)} %step_ref.3) | copy-start | bytes 73732
  0.7 22.2 %copy-start = (f32[16,384]{1,0:T(8,128)S(1)}, f32[16,384]{1,0:T(8,128)}, u32[]{:S(2)}) copy-start(f32[16,384]{1,0:T(8,128)} %bias_ref.3) | copy-start | bytes 73732
  6.7 1.5 %collective-permute-start = (f32[64,384]{1,0:T(8,128)S(1)}, f32[64,384]{1,0:T(8,128)S(1)}, u32[]{:S(2)}, u32[]{:S(2)}) collective-permute-start(f32[64,384]{1,0:T(8,128)S(1)} %get-tuple-element.22), channel_id=1, source_target_pairs={{0,4},{4,0},{8,12},{12,8},{16,20},{20,16},{24,28},{28,24},{1,5},{5... | collective-permute-start | bytes 294920 | tf_op jit(solution)/shard_map/ppermute | solution.py:55
  8.3 6.9 %collective-permute-start.1 = (bf16[64,384]{1,0:T(8,128)(2,1)S(1)}, bf16[64,384]{1,0:T(8,128)(2,1)S(1)}, u32[]{:S(2)}, u32[]{:S(2)}) collective-permute-start(bf16[64,384]{1,0:T(8,128)(2,1)S(1)} %get-tuple-element.24), channel_id=1, source_target_pairs={{0,7},{1,6},{2,5},{3,4},{4,3},{5,2},{6,1},{7,0},{8,15},{9,14},{10,... | collective-permute-start | bytes 147464 | tf_op jit(solution)/shard_map/ppermute | solution.py:21
  13.1 3.5 %collective-permute-start.2 = (bf16[64,384]{1,0:T(8,128)(2,1)S(1)}, bf16[64,384]{1,0:T(8,128)(2,1)S(1)}, u32[]{:S(2)}, u32[]{:S(2)}) collective-permute-start(bf16[64,384]{1,0:T(8,128)(2,1)S(1)} %get-tuple-element.25), channel_id=1, source_target_pairs={{0,5},{1,4},{2,7},{3,6},{4,1},{5,0},{6,3},{7,2},{8,13},{9,12},{10,... | collective-permute-start | bytes 147464 | tf_op jit(solution)/shard_map/ppermute | solution.py:21
  16.7 4.5 %collective-permute-start.5 = (bf16[64,384]{1,0:T(8,128)(2,1)S(1)}, bf16[64,384]{1,0:T(8,128)(2,1)S(1)}, u32[]{:S(2)}, u32[]{:S(2)}) collective-permute-start(bf16[64,384]{1,0:T(8,128)(2,1)S(1)} %pad_maximum_fusion.2.refs_3_), channel_id=1, source_target_pairs={{0,28},{4,24},{8,20},{12,16},{16,12},{20,8},{24,4},{28,0},{1,29},{... | collective-permute-start | bytes 147464 | tf_op jit(solution)/shard_map/ppermute | solution.py:75
  19.1 3.7 %collective-permute-start.4 = (bf16[64,384]{1,0:T(8,128)(2,1)S(1)}, bf16[64,384]{1,0:T(8,128)(2,1)S(1)}, u32[]{:S(2)}, u32[]{:S(2)}) collective-permute-start(bf16[64,384]{1,0:T(8,128)(2,1)S(1)} %pad_maximum_fusion.2.refs_3_), channel_id=1, source_target_pairs={{0,20},{4,16},{8,28},{12,24},{16,4},{20,0},{24,12},{28,8},{1,21},{... | collective-permute-start | bytes 147464 | tf_op jit(solution)/shard_map/ppermute | solution.py:75
  19.4 3.5 %collective-permute-start.3 = (bf16[64,384]{1,0:T(8,128)(2,1)S(1)}, bf16[64,384]{1,0:T(8,128)(2,1)S(1)}, u32[]{:S(2)}, u32[]{:S(2)}) collective-permute-start(bf16[64,384]{1,0:T(8,128)(2,1)S(1)} %pad_maximum_fusion.2.refs_3_), channel_id=1, source_target_pairs={{0,12},{4,8},{8,4},{12,0},{16,28},{20,24},{24,20},{28,16},{1,13},{... | collective-permute-start | bytes 147464 | tf_op jit(solution)/shard_map/ppermute | solution.py:75
  26.1 1.4 %collective-permute-start.6 = (f32[64,384]{1,0:T(8,128)S(1)}, f32[64,384]{1,0:T(8,128)S(1)}, u32[]{:S(2)}, u32[]{:S(2)}) collective-permute-start(f32[64,384]{1,0:T(8,128)S(1)} %get-tuple-element.27), channel_id=1, source_target_pairs={{0,4},{4,0},{8,12},{12,8},{16,20},{20,16},{24,28},{28,24},{1,5},{5... | collective-permute-start | bytes 294920 | tf_op jit(solution)/shard_map/ppermute | solution.py:55
  27.5 5.1 %collective-permute-start.7 = (bf16[32,384]{1,0:T(8,128)(2,1)S(1)}, bf16[32,384]{1,0:T(8,128)(2,1)S(1)}, u32[]{:S(2)}, u32[]{:S(2)}) collective-permute-start(bf16[32,384]{1,0:T(8,128)(2,1)S(1)} %broadcast_select_fusion.2), channel_id=1, source_target_pairs={{0,7},{1,6},{2,5},{3,4},{4,3},{5,2},{6,1},{7,0},{8,15},{9,14},{10,... | collective-permute-start | bytes 73736 | tf_op jit(solution)/shard_map/ppermute | solution.py:21
  29.9 3.6 %collective-permute-start.8 = (bf16[32,384]{1,0:T(8,128)(2,1)S(1)}, bf16[32,384]{1,0:T(8,128)(2,1)S(1)}, u32[]{:S(2)}, u32[]{:S(2)}) collective-permute-start(bf16[32,384]{1,0:T(8,128)(2,1)S(1)} %get-tuple-element.29), channel_id=1, source_target_pairs={{0,5},{1,4},{2,7},{3,6},{4,1},{5,0},{6,3},{7,2},{8,13},{9,12},{10,... | collective-permute-start | bytes 73736 | tf_op jit(solution)/shard_map/ppermute | solution.py:21
  33.5 4.8 %collective-permute-start.11 = (bf16[64,384]{1,0:T(8,128)(2,1)S(1)}, bf16[64,384]{1,0:T(8,128)(2,1)S(1)}, u32[]{:S(2)}, u32[]{:S(2)}) collective-permute-start(bf16[64,384]{1,0:T(8,128)(2,1)S(1)} %pad_maximum_fusion.3.refs_3_), channel_id=1, source_target_pairs={{0,28},{4,24},{8,20},{12,16},{16,12},{20,8},{24,4},{28,0},{1,29},{... | collective-permute-start | bytes 147464 | tf_op jit(solution)/shard_map/ppermute | solution.py:75
  34.8 4.7 %collective-permute-start.10 = (bf16[64,384]{1,0:T(8,128)(2,1)S(1)}, bf16[64,384]{1,0:T(8,128)(2,1)S(1)}, u32[]{:S(2)}, u32[]{:S(2)}) collective-permute-start(bf16[64,384]{1,0:T(8,128)(2,1)S(1)} %pad_maximum_fusion.3.refs_3_), channel_id=1, source_target_pairs={{0,20},{4,16},{8,28},{12,24},{16,4},{20,0},{24,12},{28,8},{1,21},{... | collective-permute-start | bytes 147464 | tf_op jit(solution)/shard_map/ppermute | solution.py:75
  35.8 3.8 %collective-permute-start.9 = (bf16[64,384]{1,0:T(8,128)(2,1)S(1)}, bf16[64,384]{1,0:T(8,128)(2,1)S(1)}, u32[]{:S(2)}, u32[]{:S(2)}) collective-permute-start(bf16[64,384]{1,0:T(8,128)(2,1)S(1)} %pad_maximum_fusion.3.refs_3_), channel_id=1, source_target_pairs={{0,12},{4,8},{8,4},{12,0},{16,28},{20,24},{24,20},{28,16},{1,13},{... | collective-permute-start | bytes 147464 | tf_op jit(solution)/shard_map/ppermute | solution.py:75
  42.9 1.4 %collective-permute-start.12 = (f32[64,384]{1,0:T(8,128)S(1)}, f32[64,384]{1,0:T(8,128)S(1)}, u32[]{:S(2)}, u32[]{:S(2)}) collective-permute-start(f32[64,384]{1,0:T(8,128)S(1)} %get-tuple-element.31), channel_id=1, source_target_pairs={{0,4},{4,0},{8,12},{12,8},{16,20},{20,16},{24,28},{28,24},{1,5},{5... | collective-permute-start | bytes 294920 | tf_op jit(solution)/shard_map/ppermute | solution.py:55
  44.3 5.1 %collective-permute-start.13 = (bf16[32,384]{1,0:T(8,128)(2,1)S(1)}, bf16[32,384]{1,0:T(8,128)(2,1)S(1)}, u32[]{:S(2)}, u32[]{:S(2)}) collective-permute-start(bf16[32,384]{1,0:T(8,128)(2,1)S(1)} %slice.78), channel_id=1, source_target_pairs={{0,5},{1,6},{2,7},{3,4},{4,1},{5,2},{6,3},{7,0},{8,13},{9,14},{10,... | collective-permute-start | bytes 73736 | tf_op jit(solution)/shard_map/ppermute | solution.py:21
  49.4 4.2 %collective-permute-start.16 = (bf16[32,384]{1,0:T(8,128)(2,1)S(1)}, bf16[32,384]{1,0:T(8,128)(2,1)S(1)}, u32[]{:S(2)}, u32[]{:S(2)}) collective-permute-start(bf16[32,384]{1,0:T(8,128)(2,1)S(1)} %fusion.4), channel_id=1, source_target_pairs={{0,28},{4,24},{8,20},{12,16},{16,12},{20,8},{24,4},{28,0},{1,29},{... | collective-permute-start | bytes 73736 | tf_op jit(solution)/shard_map/ppermute | solution.py:75
  51.2 3.3 %collective-permute-start.15 = (bf16[32,384]{1,0:T(8,128)(2,1)S(1)}, bf16[32,384]{1,0:T(8,128)(2,1)S(1)}, u32[]{:S(2)}, u32[]{:S(2)}) collective-permute-start(bf16[32,384]{1,0:T(8,128)(2,1)S(1)} %fusion.4), channel_id=1, source_target_pairs={{0,20},{4,16},{8,28},{12,24},{16,4},{20,0},{24,12},{28,8},{1,21},{... | collective-permute-start | bytes 73736 | tf_op jit(solution)/shard_map/ppermute | solution.py:75
  51.6 3.3 %collective-permute-start.14 = (bf16[32,384]{1,0:T(8,128)(2,1)S(1)}, bf16[32,384]{1,0:T(8,128)(2,1)S(1)}, u32[]{:S(2)}, u32[]{:S(2)}) collective-permute-start(bf16[32,384]{1,0:T(8,128)(2,1)S(1)} %fusion.4), channel_id=1, source_target_pairs={{0,12},{4,8},{8,4},{12,0},{16,28},{20,24},{24,20},{28,16},{1,13},{... | collective-permute-start | bytes 73736 | tf_op jit(solution)/shard_map/ppermute | solution.py:75

commit v6 on v5

--- a/solution.py
+++ b/solution.py
@@ -70,7 +70,7 @@
         radix = min(count // stride, 4)
         value = rounded(tree([part.astype(jnp.float32) for part in parts]))
         parts = []
-        for digit in range(1, radix):
+        for digit in [1, 3, 2][: radix - 1]:
             pairs = [(place, place ^ (digit * stride) ^ 1) for place in range(count)]
             parts.append(lax.ppermute(value, "contact", pairs))
         parts.append(value)

time: 55.7 us -> 56 us (level)
  no operation moved by 1% of the time
where the time goes in v6:
time: 56 us; the launch traced here: 55.8 us
  waiting for transfers between devices  23.6 us (42%)
  starting transfers between devices  18.1 us (32%)
  Pallas kernels  11.8 us (21%)
  between operations  1.47 us (3%)
  other arithmetic  0.85 us (2%)
    ppermute x5, waiting for transfers between devices, crossed(): return lax.ppermute(value, ('contact', 'body'), pairs)  11.8 us
    ppermute x9, starting transfers between devices, over_pairs(): parts.append(lax.ppermute(value, 'contact', pairs))  9.3 us
    ppermute x9, waiting for transfers between devices, over_pairs(): parts.append(lax.ppermute(value, 'contact', pairs))  8.84 us
    ppermute x5, starting transfers between devices, crossed(): return lax.ppermute(value, ('contact', 'body'), pairs)  7.57 us
    pallas_call x2, Pallas kernels, sweep_step(): pl.pallas_call(functools.partial(sweep_kernel, len(parts)), out_shape=res...  6.41 us
    pallas_call x1, Pallas kernels, first_push(): pl.pallas_call(first_kernel, out_shape=[pltpu.VMEM((tiles, rows, cols), j...  5.38 us
    ppermute x3, waiting for transfers between devices, pair_sum(): lax.ppermute(value, 'contact', [(place, place ^ 1) for place in range(cou...  2.98 us
    ppermute x3, starting transfers between devices, pair_sum(): lax.ppermute(value, 'contact', [(place, place ^ 1) for place in range(cou...  1.19 us
  transfers between devices with their start and end apart: 17, of which 17 were waited for; matrix products, arithmetic and copies ran while one was open for 0% of the time, Pallas kernels for 0%

profile of v6, /device:TPU:0, one launch (start us, length us, event | category | flops | bytes accessed | tf_op | source)
XLA Modules:
  0.0 55.8 jit_solution(6068663874609777261)
XLA Ops:
  0.6 0.0 copy-start.3
  0.6 0.0 copy-start.4
  0.7 0.0 copy-start.5
  0.7 0.0 copy-start.2
  0.7 0.0 copy-start.1
  0.7 0.0 copy-start
  1.4 5.4 %first_push.1 = (bf16[16,768,384]{2,1,0:T(8,128)(2,1)S(1)}, bf16[16,384,768]{2,1,0:T(8,128)(2,1)S(1)}, f32[16,384]{1,0:T(8,128)S(1)}, f32[16,384]{1,0:T(8,128)S(1)}, f32[64,384]{1,0:T(8,128)S(1)}) custom-call(s32[1]{0:T(128)S(6)} %copy.11.count_ref, s32[2,16]{1,0:T(2,128)} %bitcast.2, bf16[16,768,384]{2,1,0:T(8,128)(2,1)} %bitcast.5, f32[16,384]{1,0:T(8,128)} %start_ref.1), custom_call_target="tpu_custom_call" | custom-call | flops 9437184 | bytes 9437184 | tf_op jit(solution)/shard_map/first_push/pallas_call | solution.py:204
  6.7 0.5 collective-permute-start
  7.3 0.0 copy-done.4
  7.3 0.9 %collective-permute-done = f32[64,384]{1,0:T(8,128)S(1)} collective-permute-done((f32[64,384]{1,0:T(8,128)S(1)}, f32[64,384]{1,0:T(8,128)S(1)}, u32[]{:S(2)}, u32[]{:S(2)}) %collective-permute-start) | collective-permute-done | bytes 98336 | tf_op jit(solution)/shard_map/ppermute | solution.py:55
  8.2 0.0 copy-done.5
  8.3 4.8 %collective-permute-start.1 = (bf16[64,384]{1,0:T(8,128)(2,1)S(1)}, bf16[64,384]{1,0:T(8,128)(2,1)S(1)}, u32[]{:S(2)}, u32[]{:S(2)}) collective-permute-start(bf16[64,384]{1,0:T(8,128)(2,1)S(1)} %get-tuple-element.24), channel_id=1, source_target_pairs={{0,7},{1,6},{2,5},{3,4},{4,3},{5,2},{6,1},{7,0},{8,15},{9,14},{10,... | collective-permute-start | bytes 147464 | tf_op jit(solution)/shard_map/ppermute | solution.py:21
  13.1 0.0 collective-permute-start.2
  13.1 2.1 %collective-permute-done.1 = bf16[64,384]{1,0:T(8,128)(2,1)S(1)} collective-permute-done((bf16[64,384]{1,0:T(8,128)(2,1)S(1)}, bf16[64,384]{1,0:T(8,128)(2,1)S(1)}, u32[]{:S(2)}, u32[]{:S(2)}) %collective-permute-start.1) | collective-permute-done | bytes 49184 | tf_op jit(solution)/shard_map/ppermute | solution.py:21
  15.2 1.4 %collective-permute-done.2 = bf16[64,384]{1,0:T(8,128)(2,1)S(1)} collective-permute-done((bf16[64,384]{1,0:T(8,128)(2,1)S(1)}, bf16[64,384]{1,0:T(8,128)(2,1)S(1)}, u32[]{:S(2)}, u32[]{:S(2)}) %collective-permute-start.2) | collective-permute-done | bytes 49184 | tf_op jit(solution)/shard_map/ppermute | solution.py:21
  16.7 1.5 %collective-permute-start.5 = (bf16[64,384]{1,0:T(8,128)(2,1)S(1)}, bf16[64,384]{1,0:T(8,128)(2,1)S(1)}, u32[]{:S(2)}, u32[]{:S(2)}) collective-permute-start(bf16[64,384]{1,0:T(8,128)(2,1)S(1)} %pad_maximum_fusion.2.refs_3_), channel_id=1, source_target_pairs={{0,20},{4,16},{8,28},{12,24},{16,4},{20,0},{24,12},{28,8},{1,21},{... | collective-permute-start | bytes 147464 | tf_op jit(solution)/shard_map/ppermute | solution.py:75
  18.2 1.2 %collective-permute-start.4 = (bf16[64,384]{1,0:T(8,128)(2,1)S(1)}, bf16[64,384]{1,0:T(8,128)(2,1)S(1)}, u32[]{:S(2)}, u32[]{:S(2)}) collective-permute-start(bf16[64,384]{1,0:T(8,128)(2,1)S(1)} %pad_maximum_fusion.2.refs_3_), channel_id=1, source_target_pairs={{0,28},{4,24},{8,20},{12,16},{16,12},{20,8},{24,4},{28,0},{1,29},{... | collective-permute-start | bytes 147464 | tf_op jit(solution)/shard_map/ppermute | solution.py:75
  19.4 0.5 collective-permute-start.3
  19.9 0.4 collective-permute-done.5.refs_2_
  20.2 2.6 %collective-permute-done.4.refs_1_ = bf16[64,384]{1,0:T(8,128)(2,1)S(1)} collective-permute-done((bf16[64,384]{1,0:T(8,128)(2,1)S(1)}, bf16[64,384]{1,0:T(8,128)(2,1)S(1)}, u32[]{:S(2)}, u32[]{:S(2)}) %collective-permute-start.4) | collective-permute-done | bytes 49184 | tf_op jit(solution)/shard_map/ppermute | solution.py:75
  22.8 0.1 collective-permute-done.3.refs_0_
  22.9 0.0 copy-done.3
  22.9 0.0 copy-done.2
  22.9 0.0 copy-done.1
  22.9 0.0 copy-done
  22.9 3.1 %sweep_step.2 = (f32[16,384]{1,0:T(8,128)S(1)}, f32[64,384]{1,0:T(8,128)S(1)}) custom-call(s32[2,16]{1,0:T(2,128)S(1)} %bitcast.3, f32[16,384]{1,0:T(8,128)S(1)} %get-tuple-element.18.live_ref, bf16[16,768,384]{2,1,0:T(8,128)(2,1)S(1)} %get-tuple-element.19.jac_ref, bf16[16,384,768]{2,1,0:T(8,128)(2,1)S(1)} %get-tuple-element.20.turned_ref, ...), custom_call_target="tpu_custom_call" | custom-call | flops 18874368 | bytes 18874368 | tf_op jit(solution)/shard_map/sweep_step/pallas_call | solution.py:230
  26.1 0.4 collective-permute-start.6
  26.5 1.0 %collective-permute-done.6 = f32[64,384]{1,0:T(8,128)S(1)} collective-permute-done((f32[64,384]{1,0:T(8,128)S(1)}, f32[64,384]{1,0:T(8,128)S(1)}, u32[]{:S(2)}, u32[]{:S(2)}) %collective-permute-start.6) | collective-permute-done | bytes 98336 | tf_op jit(solution)/shard_map/ppermute | solution.py:55
  27.5 2.4 %collective-permute-start.7 = (bf16[32,384]{1,0:T(8,128)(2,1)S(1)}, bf16[32,384]{1,0:T(8,128)(2,1)S(1)}, u32[]{:S(2)}, u32[]{:S(2)}) collective-permute-start(bf16[32,384]{1,0:T(8,128)(2,1)S(1)} %broadcast_select_fusion.2), channel_id=1, source_target_pairs={{0,7},{1,6},{2,5},{3,4},{4,3},{5,2},{6,1},{7,0},{8,15},{9,14},{10,... | collective-permute-start | bytes 73736 | tf_op jit(solution)/shard_map/ppermute | solution.py:21
  29.9 0.0 collective-permute-start.8
  29.9 2.7 %collective-permute-done.7 = bf16[32,384]{1,0:T(8,128)(2,1)S(1)} collective-permute-done((bf16[32,384]{1,0:T(8,128)(2,1)S(1)}, bf16[32,384]{1,0:T(8,128)(2,1)S(1)}, u32[]{:S(2)}, u32[]{:S(2)}) %collective-permute-start.7) | collective-permute-done | bytes 24608 | tf_op jit(solution)/shard_map/ppermute | solution.py:21
  32.6 0.8 %collective-permute-done.8 = bf16[32,384]{1,0:T(8,128)(2,1)S(1)} collective-permute-done((bf16[32,384]{1,0:T(8,128)(2,1)S(1)}, bf16[32,384]{1,0:T(8,128)(2,1)S(1)}, u32[]{:S(2)}, u32[]{:S(2)}) %collective-permute-start.8) | collective-permute-done | bytes 24608 | tf_op jit(solution)/shard_map/ppermute | solution.py:21
  33.5 1.3 %collective-permute-start.11 = (bf16[64,384]{1,0:T(8,128)(2,1)S(1)}, bf16[64,384]{1,0:T(8,128)(2,1)S(1)}, u32[]{:S(2)}, u32[]{:S(2)}) collective-permute-start(bf16[64,384]{1,0:T(8,128)(2,1)S(1)} %pad_maximum_fusion.3.refs_3_), channel_id=1, source_target_pairs={{0,20},{4,16},{8,28},{12,24},{16,4},{20,0},{24,12},{28,8},{1,21},{... | collective-permute-start | bytes 147464 | tf_op jit(solution)/shard_map/ppermute | solution.py:75
  34.8 1.2 %collective-permute-start.10 = (bf16[64,384]{1,0:T(8,128)(2,1)S(1)}, bf16[64,384]{1,0:T(8,128)(2,1)S(1)}, u32[]{:S(2)}, u32[]{:S(2)}) collective-permute-start(bf16[64,384]{1,0:T(8,128)(2,1)S(1)} %pad_maximum_fusion.3.refs_3_), channel_id=1, source_target_pairs={{0,28},{4,24},{8,20},{12,16},{16,12},{20,8},{24,4},{28,0},{1,29},{... | collective-permute-start | bytes 147464 | tf_op jit(solution)/shard_map/ppermute | solution.py:75
  36.0 0.5 collective-permute-start.9
  36.5 0.8 %collective-permute-done.11.refs_2_ = bf16[64,384]{1,0:T(8,128)(2,1)S(1)} collective-permute-done((bf16[64,384]{1,0:T(8,128)(2,1)S(1)}, bf16[64,384]{1,0:T(8,128)(2,1)S(1)}, u32[]{:S(2)}, u32[]{:S(2)}) %collective-permute-start.11) | collective-permute-done | bytes 49184 | tf_op jit(solution)/shard_map/ppermute | solution.py:75
  37.3 1.9 %collective-permute-done.10.refs_1_ = bf16[64,384]{1,0:T(8,128)(2,1)S(1)} collective-permute-done((bf16[64,384]{1,0:T(8,128)(2,1)S(1)}, bf16[64,384]{1,0:T(8,128)(2,1)S(1)}, u32[]{:S(2)}, u32[]{:S(2)}) %collective-permute-start.10) | collective-permute-done | bytes 49184 | tf_op jit(solution)/shard_map/ppermute | solution.py:75
  39.2 0.4 collective-permute-done.9.refs_0_
  39.6 3.3 %sweep_step.3 = (f32[16,384]{1,0:T(8,128)}, f32[64,384]{1,0:T(8,128)S(1)}) custom-call(s32[2,16]{1,0:T(2,128)S(1)} %bitcast.4, f32[16,384]{1,0:T(8,128)S(1)} %get-tuple-element.18.live_ref, bf16[16,768,384]{2,1,0:T(8,128)(2,1)S(1)} %get-tuple-element.19.jac_ref, bf16[16,384,768]{2,1,0:T(8,128)(2,1)S(1)} %get-tuple-element.20.turned_ref, ...), custom_call_target="tpu_custom_call" | custom-call | flops 18874368 | bytes 18874368 | tf_op jit(solution)/shard_map/sweep_step/pallas_call | solution.py:230
  42.9 0.3 collective-permute-start.12
  43.2 1.1 %collective-permute-done.12 = f32[64,384]{1,0:T(8,128)S(1)} collective-permute-done((f32[64,384]{1,0:T(8,128)S(1)}, f32[64,384]{1,0:T(8,128)S(1)}, u32[]{:S(2)}, u32[]{:S(2)}) %collective-permute-start.12) | collective-permute-done | bytes 98336 | tf_op jit(solution)/shard_map/ppermute | solution.py:55
  44.3 0.4 collective-permute-start.13
  44.7 4.7 %collective-permute-done.13 = bf16[32,384]{1,0:T(8,128)(2,1)S(1)} collective-permute-done((bf16[32,384]{1,0:T(8,128)(2,1)S(1)}, bf16[32,384]{1,0:T(8,128)(2,1)S(1)}, u32[]{:S(2)}, u32[]{:S(2)}) %collective-permute-start.13) | collective-permute-done | bytes 24608 | tf_op jit(solution)/shard_map/ppermute | solution.py:21
  49.4 1.5 %collective-permute-start.16 = (bf16[32,384]{1,0:T(8,128)(2,1)S(1)}, bf16[32,384]{1,0:T(8,128)(2,1)S(1)}, u32[]{:S(2)}, u32[]{:S(2)}) collective-permute-start(bf16[32,384]{1,0:T(8,128)(2,1)S(1)} %fusion.4), channel_id=1, source_target_pairs={{0,20},{4,16},{8,28},{12,24},{16,4},{20,0},{24,12},{28,8},{1,21},{... | collective-permute-start | bytes 73736 | tf_op jit(solution)/shard_map/ppermute | solution.py:75
  50.9 1.1 %collective-permute-start.15 = (bf16[32,384]{1,0:T(8,128)(2,1)S(1)}, bf16[32,384]{1,0:T(8,128)(2,1)S(1)}, u32[]{:S(2)}, u32[]{:S(2)}) collective-permute-start(bf16[32,384]{1,0:T(8,128)(2,1)S(1)} %fusion.4), channel_id=1, source_target_pairs={{0,28},{4,24},{8,20},{12,16},{16,12},{20,8},{24,4},{28,0},{1,29},{... | collective-permute-start | bytes 73736 | tf_op jit(solution)/shard_map/ppermute | solution.py:75
  51.9 0.6 %collective-permute-start.14 = (bf16[32,384]{1,0:T(8,128)(2,1)S(1)}, bf16[32,384]{1,0:T(8,128)(2,1)S(1)}, u32[]{:S(2)}, u32[]{:S(2)}) collective-permute-start(bf16[32,384]{1,0:T(8,128)(2,1)S(1)} %fusion.4), channel_id=1, source_target_pairs={{0,12},{4,8},{8,4},{12,0},{16,28},{20,24},{24,20},{28,16},{1,13},{... | collective-permute-start | bytes 73736 | tf_op jit(solution)/shard_map/ppermute | solution.py:75
  52.5 0.2 collective-permute-done.16
  52.7 2.3 %collective-permute-done.15 = bf16[32,384]{1,0:T(8,128)(2,1)S(1)} collective-permute-done((bf16[32,384]{1,0:T(8,128)(2,1)S(1)}, bf16[32,384]{1,0:T(8,128)(2,1)S(1)}, u32[]{:S(2)}, u32[]{:S(2)}) %collective-permute-start.15) | collective-permute-done | bytes 24608 | tf_op jit(solution)/shard_map/ppermute | solution.py:75
  55.0 0.2 collective-permute-done.14
  55.2 0.6 %multiply_add_fusion = f32[32,384]{1,0:T(8,128)} fusion(f32[32,384]{1,0:T(8,128)S(1)} %copy-done.5, f32[32,384]{1,0:T(8,128)S(1)} %copy-done.4, bf16[32,384]{1,0:T(8,128)(2,1)S(1)} %fusion.4, bf16[32,384]{1,0:T(8,128)(2,1)S(1)} %collective-permute-done.16, bf16[32,384]{1,0:T(8,128)(2,1)S(1)} %collective-permute-done.15, ...), kind=kLoop, calls=%fused_computation.13 | loop fusion | flops 110592 | bytes 245760 | tf_op jit(solution)/shard_map/add | solution.py:281
  (16 shorter events, 0.2 us)
Async XLA Ops:
  0.6 22.3 %copy-start.3 = (s32[16,2]{0,1:T(2,128)S(1)}, s32[16,2]{0,1:T(2,128)}, u32[]{:S(2)}) copy-start(s32[16,2]{0,1:T(2,128)} %param.10) | copy-start | bytes 388
  0.6 6.6 %copy-start.4 = (f32[32,384]{1,0:T(8,128)S(1)}, f32[32,384]{1,0:T(8,128)}, u32[]{:S(2)}) copy-start(f32[32,384]{1,0:T(8,128)} %param.13) | copy-start | bytes 147460
  0.7 7.6 %copy-start.5 = (f32[32,384]{1,0:T(8,128)S(1)}, f32[32,384]{1,0:T(8,128)}, u32[]{:S(2)}) copy-start(f32[32,384]{1,0:T(8,128)} %param.12) | copy-start | bytes 147460
  0.7 22.3 %copy-start.2 = (f32[16,128]{1,0:T(8,128)S(1)}, f32[16,128]{1,0:T(8,128)}, u32[]{:S(2)}) copy-start(f32[16,128]{1,0:T(8,128)} %friction_ref.3) | copy-start | bytes 24580
  0.7 22.3 %copy-start.1 = (f32[16,384]{1,0:T(8,128)S(1)}, f32[16,384]{1,0:T(8,128)}, u32[]{:S(2)}) copy-start(f32[16,384]{1,0:T(8,128)} %step_ref.3) | copy-start | bytes 73732
  0.7 22.2 %copy-start = (f32[16,384]{1,0:T(8,128)S(1)}, f32[16,384]{1,0:T(8,128)}, u32[]{:S(2)}) copy-start(f32[16,384]{1,0:T(8,128)} %bias_ref.3) | copy-start | bytes 73732
  6.7 1.5 %collective-permute-start = (f32[64,384]{1,0:T(8,128)S(1)}, f32[64,384]{1,0:T(8,128)S(1)}, u32[]{:S(2)}, u32[]{:S(2)}) collective-permute-start(f32[64,384]{1,0:T(8,128)S(1)} %get-tuple-element.22), channel_id=1, source_target_pairs={{0,4},{4,0},{8,12},{12,8},{16,20},{20,16},{24,28},{28,24},{1,5},{5... | collective-permute-start | bytes 294920 | tf_op jit(solution)/shard_map/ppermute | solution.py:55
  8.3 6.9 %collective-permute-start.1 = (bf16[64,384]{1,0:T(8,128)(2,1)S(1)}, bf16[64,384]{1,0:T(8,128)(2,1)S(1)}, u32[]{:S(2)}, u32[]{:S(2)}) collective-permute-start(bf16[64,384]{1,0:T(8,128)(2,1)S(1)} %get-tuple-element.24), channel_id=1, source_target_pairs={{0,7},{1,6},{2,5},{3,4},{4,3},{5,2},{6,1},{7,0},{8,15},{9,14},{10,... | collective-permute-start | bytes 147464 | tf_op jit(solution)/shard_map/ppermute | solution.py:21
  13.1 3.5 %collective-permute-start.2 = (bf16[64,384]{1,0:T(8,128)(2,1)S(1)}, bf16[64,384]{1,0:T(8,128)(2,1)S(1)}, u32[]{:S(2)}, u32[]{:S(2)}) collective-permute-start(bf16[64,384]{1,0:T(8,128)(2,1)S(1)} %get-tuple-element.25), channel_id=1, source_target_pairs={{0,5},{1,4},{2,7},{3,6},{4,1},{5,0},{6,3},{7,2},{8,13},{9,12},{10,... | collective-permute-start | bytes 147464 | tf_op jit(solution)/shard_map/ppermute | solution.py:21
  16.7 3.6 %collective-permute-start.5 = (bf16[64,384]{1,0:T(8,128)(2,1)S(1)}, bf16[64,384]{1,0:T(8,128)(2,1)S(1)}, u32[]{:S(2)}, u32[]{:S(2)}) collective-permute-start(bf16[64,384]{1,0:T(8,128)(2,1)S(1)} %pad_maximum_fusion.2.refs_3_), channel_id=1, source_target_pairs={{0,20},{4,16},{8,28},{12,24},{16,4},{20,0},{24,12},{28,8},{1,21},{... | collective-permute-start | bytes 147464 | tf_op jit(solution)/shard_map/ppermute | solution.py:75
  18.2 4.6 %collective-permute-start.4 = (bf16[64,384]{1,0:T(8,128)(2,1)S(1)}, bf16[64,384]{1,0:T(8,128)(2,1)S(1)}, u32[]{:S(2)}, u32[]{:S(2)}) collective-permute-start(bf16[64,384]{1,0:T(8,128)(2,1)S(1)} %pad_maximum_fusion.2.refs_3_), channel_id=1, source_target_pairs={{0,28},{4,24},{8,20},{12,16},{16,12},{20,8},{24,4},{28,0},{1,29},{... | collective-permute-start | bytes 147464 | tf_op jit(solution)/shard_map/ppermute | solution.py:75
  19.4 3.5 %collective-permute-start.3 = (bf16[64,384]{1,0:T(8,128)(2,1)S(1)}, bf16[64,384]{1,0:T(8,128)(2,1)S(1)}, u32[]{:S(2)}, u32[]{:S(2)}) collective-permute-start(bf16[64,384]{1,0:T(8,128)(2,1)S(1)} %pad_maximum_fusion.2.refs_3_), channel_id=1, source_target_pairs={{0,12},{4,8},{8,4},{12,0},{16,28},{20,24},{24,20},{28,16},{1,13},{... | collective-permute-start | bytes 147464 | tf_op jit(solution)/shard_map/ppermute | solution.py:75
  26.1 1.4 %collective-permute-start.6 = (f32[64,384]{1,0:T(8,128)S(1)}, f32[64,384]{1,0:T(8,128)S(1)}, u32[]{:S(2)}, u32[]{:S(2)}) collective-permute-start(f32[64,384]{1,0:T(8,128)S(1)} %get-tuple-element.27), channel_id=1, source_target_pairs={{0,4},{4,0},{8,12},{12,8},{16,20},{20,16},{24,28},{28,24},{1,5},{5... | collective-permute-start | bytes 294920 | tf_op jit(solution)/shard_map/ppermute | solution.py:55
  27.5 5.1 %collective-permute-start.7 = (bf16[32,384]{1,0:T(8,128)(2,1)S(1)}, bf16[32,384]{1,0:T(8,128)(2,1)S(1)}, u32[]{:S(2)}, u32[]{:S(2)}) collective-permute-start(bf16[32,384]{1,0:T(8,128)(2,1)S(1)} %broadcast_select_fusion.2), channel_id=1, source_target_pairs={{0,7},{1,6},{2,5},{3,4},{4,3},{5,2},{6,1},{7,0},{8,15},{9,14},{10,... | collective-permute-start | bytes 73736 | tf_op jit(solution)/shard_map/ppermute | solution.py:21
  29.9 3.6 %collective-permute-start.8 = (bf16[32,384]{1,0:T(8,128)(2,1)S(1)}, bf16[32,384]{1,0:T(8,128)(2,1)S(1)}, u32[]{:S(2)}, u32[]{:S(2)}) collective-permute-start(bf16[32,384]{1,0:T(8,128)(2,1)S(1)} %get-tuple-element.29), channel_id=1, source_target_pairs={{0,5},{1,4},{2,7},{3,6},{4,1},{5,0},{6,3},{7,2},{8,13},{9,12},{10,... | collective-permute-start | bytes 73736 | tf_op jit(solution)/shard_map/ppermute | solution.py:21
  33.5 3.8 %collective-permute-start.11 = (bf16[64,384]{1,0:T(8,128)(2,1)S(1)}, bf16[64,384]{1,0:T(8,128)(2,1)S(1)}, u32[]{:S(2)}, u32[]{:S(2)}) collective-permute-start(bf16[64,384]{1,0:T(8,128)(2,1)S(1)} %pad_maximum_fusion.3.refs_3_), channel_id=1, source_target_pairs={{0,20},{4,16},{8,28},{12,24},{16,4},{20,0},{24,12},{28,8},{1,21},{... | collective-permute-start | bytes 147464 | tf_op jit(solution)/shard_map/ppermute | solution.py:75
  34.8 4.4 %collective-permute-start.10 = (bf16[64,384]{1,0:T(8,128)(2,1)S(1)}, bf16[64,384]{1,0:T(8,128)(2,1)S(1)}, u32[]{:S(2)}, u32[]{:S(2)}) collective-permute-start(bf16[64,384]{1,0:T(8,128)(2,1)S(1)} %pad_maximum_fusion.3.refs_3_), channel_id=1, source_target_pairs={{0,28},{4,24},{8,20},{12,16},{16,12},{20,8},{24,4},{28,0},{1,29},{... | collective-permute-start | bytes 147464 | tf_op jit(solution)/shard_map/ppermute | solution.py:75
  36.0 3.7 %collective-permute-start.9 = (bf16[64,384]{1,0:T(8,128)(2,1)S(1)}, bf16[64,384]{1,0:T(8,128)(2,1)S(1)}, u32[]{:S(2)}, u32[]{:S(2)}) collective-permute-start(bf16[64,384]{1,0:T(8,128)(2,1)S(1)} %pad_maximum_fusion.3.refs_3_), channel_id=1, source_target_pairs={{0,12},{4,8},{8,4},{12,0},{16,28},{20,24},{24,20},{28,16},{1,13},{... | collective-permute-start | bytes 147464 | tf_op jit(solution)/shard_map/ppermute | solution.py:75
  42.9 1.4 %collective-permute-start.12 = (f32[64,384]{1,0:T(8,128)S(1)}, f32[64,384]{1,0:T(8,128)S(1)}, u32[]{:S(2)}, u32[]{:S(2)}) collective-permute-start(f32[64,384]{1,0:T(8,128)S(1)} %get-tuple-element.31), channel_id=1, source_target_pairs={{0,4},{4,0},{8,12},{12,8},{16,20},{20,16},{24,28},{28,24},{1,5},{5... | collective-permute-start | bytes 294920 | tf_op jit(solution)/shard_map/ppermute | solution.py:55
  44.3 5.1 %collective-permute-start.13 = (bf16[32,384]{1,0:T(8,128)(2,1)S(1)}, bf16[32,384]{1,0:T(8,128)(2,1)S(1)}, u32[]{:S(2)}, u32[]{:S(2)}) collective-permute-start(bf16[32,384]{1,0:T(8,128)(2,1)S(1)} %slice.78), channel_id=1, source_target_pairs={{0,5},{1,6},{2,7},{3,4},{4,1},{5,2},{6,3},{7,0},{8,13},{9,14},{10,... | collective-permute-start | bytes 73736 | tf_op jit(solution)/shard_map/ppermute | solution.py:21
  49.4 3.3 %collective-permute-start.16 = (bf16[32,384]{1,0:T(8,128)(2,1)S(1)}, bf16[32,384]{1,0:T(8,128)(2,1)S(1)}, u32[]{:S(2)}, u32[]{:S(2)}) collective-permute-start(bf16[32,384]{1,0:T(8,128)(2,1)S(1)} %fusion.4), channel_id=1, source_target_pairs={{0,20},{4,16},{8,28},{12,24},{16,4},{20,0},{24,12},{28,8},{1,21},{... | collective-permute-start | bytes 73736 | tf_op jit(solution)/shard_map/ppermute | solution.py:75
  50.9 4.2 %collective-permute-start.15 = (bf16[32,384]{1,0:T(8,128)(2,1)S(1)}, bf16[32,384]{1,0:T(8,128)(2,1)S(1)}, u32[]{:S(2)}, u32[]{:S(2)}) collective-permute-start(bf16[32,384]{1,0:T(8,128)(2,1)S(1)} %fusion.4), channel_id=1, source_target_pairs={{0,28},{4,24},{8,20},{12,16},{16,12},{20,8},{24,4},{28,0},{1,29},{... | collective-permute-start | bytes 73736 | tf_op jit(solution)/shard_map/ppermute | solution.py:75
  51.9 3.3 %collective-permute-start.14 = (bf16[32,384]{1,0:T(8,128)(2,1)S(1)}, bf16[32,384]{1,0:T(8,128)(2,1)S(1)}, u32[]{:S(2)}, u32[]{:S(2)}) collective-permute-start(bf16[32,384]{1,0:T(8,128)(2,1)S(1)} %fusion.4), channel_id=1, source_target_pairs={{0,12},{4,8},{8,4},{12,0},{16,28},{20,24},{24,20},{28,16},{1,13},{... | collective-permute-start | bytes 73736 | tf_op jit(solution)/shard_map/ppermute | solution.py:75

commit v7 on v5

--- a/solution.py
+++ b/solution.py
@@ -113,13 +113,16 @@
             [(block_ref, block), (start_ref, lam_ref)]
         )
     ]
+    groups = [range(first, min(first + GROUP, tiles)) for first in range(0, tiles, GROUP)]
     copies = [
-        pltpu.make_async_copy(jac_ref.at[tile], kept_ref.at[tile], sems.at[tile])
-        for tile in range(tiles)
-    ]
-    groups = [range(first, min(first + GROUP, tiles)) for first in range(0, tiles, GROUP)]
-    started = 3 * GROUP
-    for copy in small + copies[:started]:
+        pltpu.make_async_copy(
+            jac_ref.at[pl.ds(group[0], len(group))],
+            kept_ref.at[pl.ds(group[0], len(group))],
+            sems.at[place],
+        )
+        for place, group in enumerate(groups)
+    ]
+    for copy in small + copies[:AHEAD]:
         copy.start()
     sums_ref[...] = jnp.zeros_like(sums_ref)
     for copy in small:
@@ -127,12 +130,11 @@
     order = lax.broadcasted_iota(jnp.int32, lam_ref.shape, 0)
     live_ref[...] = jnp.where(order < count_ref[0], 1.0, 0.0)
     lam_ref[...] = lam_ref[...] * live_ref[...]
-    for group, before in zip(groups + [[]], [[]] + groups):
-        for tile in group:
-            copies[tile].wait()
-        for copy in copies[started : started + len(group)]:
+    for place, (group, before) in enumerate(zip(groups + [[]], [[]] + groups)):
+        if group:
+            copies[place].wait()
+        for copy in copies[place + AHEAD : place + AHEAD + 1]:
             copy.start()
-        started += len(group)
         for tile in group:
             turned_ref[tile] = kept_ref[tile].T
         for tile in before:
@@ -182,6 +184,7 @@
 
 
 GROUP = 2
+AHEAD = 3
 LIMIT = 24 * 1024 * 1024
 SMEM = pl.BlockSpec(memory_space=pltpu.SMEM)
 VMEM = pl.BlockSpec(memory_space=pltpu.VMEM)

time: 55.7 us -> 55.6 us (level)
  no operation moved by 1% of the time
where the time goes in v7:
time: 55.6 us; the launch traced here: 55.4 us
  waiting for transfers between devices  23.7 us (43%)
  starting transfers between devices  17.7 us (32%)
  Pallas kernels  11.7 us (21%)
  between operations  1.47 us (3%)
  other arithmetic  0.85 us (2%)
    ppermute x5, waiting for transfers between devices, crossed(): return lax.ppermute(value, ('contact', 'body'), pairs)  12.1 us
    ppermute x9, starting transfers between devices, over_pairs(): parts.append(lax.ppermute(value, 'contact', pairs))  9.26 us
    ppermute x9, waiting for transfers between devices, over_pairs(): parts.append(lax.ppermute(value, 'contact', pairs))  8.57 us
    ppermute x5, starting transfers between devices, crossed(): return lax.ppermute(value, ('contact', 'body'), pairs)  7.3 us
    pallas_call x2, Pallas kernels, sweep_step(): pl.pallas_call(functools.partial(sweep_kernel, len(parts)), out_shape=res...  6.4 us
    pallas_call x1, Pallas kernels, first_push(): pl.pallas_call(first_kernel, out_shape=[pltpu.VMEM((tiles, rows, cols), j...  5.3 us
    ppermute x3, waiting for transfers between devices, pair_sum(): lax.ppermute(value, 'contact', [(place, place ^ 1) for place in range(cou...  3.07 us
  transfers between devices with their start and end apart: 17, of which 17 were waited for; matrix products, arithmetic and copies ran while one was open for 0% of the time, Pallas kernels for 0%

profile of v7, /device:TPU:0, one launch (start us, length us, event | category | flops | bytes accessed | tf_op | source)
XLA Modules:
  0.0 55.4 jit_solution(12848825443307658600)
XLA Ops:
  0.6 0.0 copy-start.3
  0.6 0.0 copy-start.4
  0.7 0.0 copy-start.5
  0.7 0.0 copy-start.2
  0.7 0.0 copy-start.1
  0.7 0.0 copy-start
  1.4 5.3 %first_push.1 = (bf16[16,768,384]{2,1,0:T(8,128)(2,1)S(1)}, bf16[16,384,768]{2,1,0:T(8,128)(2,1)S(1)}, f32[16,384]{1,0:T(8,128)S(1)}, f32[16,384]{1,0:T(8,128)S(1)}, f32[64,384]{1,0:T(8,128)S(1)}) custom-call(s32[1]{0:T(128)S(6)} %copy.11.count_ref, s32[2,16]{1,0:T(2,128)} %bitcast.2, bf16[16,768,384]{2,1,0:T(8,128)(2,1)} %bitcast.5, f32[16,384]{1,0:T(8,128)} %start_ref.1), custom_call_target="tpu_custom_call" | custom-call | flops 9437184 | bytes 9437184 | tf_op jit(solution)/shard_map/first_push/pallas_call | solution.py:207
  6.7 0.5 collective-permute-start
  7.2 0.0 copy-done.4
  7.2 0.9 %collective-permute-done = f32[64,384]{1,0:T(8,128)S(1)} collective-permute-done((f32[64,384]{1,0:T(8,128)S(1)}, f32[64,384]{1,0:T(8,128)S(1)}, u32[]{:S(2)}, u32[]{:S(2)}) %collective-permute-start) | collective-permute-done | bytes 98336 | tf_op jit(solution)/shard_map/ppermute | solution.py:55
  8.1 0.0 copy-done.5
  8.2 4.8 %collective-permute-start.1 = (bf16[64,384]{1,0:T(8,128)(2,1)S(1)}, bf16[64,384]{1,0:T(8,128)(2,1)S(1)}, u32[]{:S(2)}, u32[]{:S(2)}) collective-permute-start(bf16[64,384]{1,0:T(8,128)(2,1)S(1)} %get-tuple-element.24), channel_id=1, source_target_pairs={{0,7},{1,6},{2,5},{3,4},{4,3},{5,2},{6,1},{7,0},{8,15},{9,14},{10,... | collective-permute-start | bytes 147464 | tf_op jit(solution)/shard_map/ppermute | solution.py:21
  13.0 0.0 collective-permute-start.2
  13.0 2.1 %collective-permute-done.1 = bf16[64,384]{1,0:T(8,128)(2,1)S(1)} collective-permute-done((bf16[64,384]{1,0:T(8,128)(2,1)S(1)}, bf16[64,384]{1,0:T(8,128)(2,1)S(1)}, u32[]{:S(2)}, u32[]{:S(2)}) %collective-permute-start.1) | collective-permute-done | bytes 49184 | tf_op jit(solution)/shard_map/ppermute | solution.py:21
  15.1 1.4 %collective-permute-done.2 = bf16[64,384]{1,0:T(8,128)(2,1)S(1)} collective-permute-done((bf16[64,384]{1,0:T(8,128)(2,1)S(1)}, bf16[64,384]{1,0:T(8,128)(2,1)S(1)}, u32[]{:S(2)}, u32[]{:S(2)}) %collective-permute-start.2) | collective-permute-done | bytes 49184 | tf_op jit(solution)/shard_map/ppermute | solution.py:21
  16.6 2.5 %collective-permute-start.5 = (bf16[64,384]{1,0:T(8,128)(2,1)S(1)}, bf16[64,384]{1,0:T(8,128)(2,1)S(1)}, u32[]{:S(2)}, u32[]{:S(2)}) collective-permute-start(bf16[64,384]{1,0:T(8,128)(2,1)S(1)} %pad_maximum_fusion.2.refs_3_), channel_id=1, source_target_pairs={{0,28},{4,24},{8,20},{12,16},{16,12},{20,8},{24,4},{28,0},{1,29},{... | collective-permute-start | bytes 147464 | tf_op jit(solution)/shard_map/ppermute | solution.py:75
  19.0 0.3 collective-permute-start.4
  19.3 0.5 collective-permute-start.3
  19.8 1.3 %collective-permute-done.5.refs_2_ = bf16[64,384]{1,0:T(8,128)(2,1)S(1)} collective-permute-done((bf16[64,384]{1,0:T(8,128)(2,1)S(1)}, bf16[64,384]{1,0:T(8,128)(2,1)S(1)}, u32[]{:S(2)}, u32[]{:S(2)}) %collective-permute-start.5) | collective-permute-done | bytes 49184 | tf_op jit(solution)/shard_map/ppermute | solution.py:75
  21.1 1.7 %collective-permute-done.4.refs_1_ = bf16[64,384]{1,0:T(8,128)(2,1)S(1)} collective-permute-done((bf16[64,384]{1,0:T(8,128)(2,1)S(1)}, bf16[64,384]{1,0:T(8,128)(2,1)S(1)}, u32[]{:S(2)}, u32[]{:S(2)}) %collective-permute-start.4) | collective-permute-done | bytes 49184 | tf_op jit(solution)/shard_map/ppermute | solution.py:75
  22.7 0.1 collective-permute-done.3.refs_0_
  22.8 0.0 copy-done.3
  22.8 0.0 copy-done.2
  22.8 0.0 copy-done.1
  22.9 0.0 copy-done
  22.9 3.1 %sweep_step.2 = (f32[16,384]{1,0:T(8,128)S(1)}, f32[64,384]{1,0:T(8,128)S(1)}) custom-call(s32[2,16]{1,0:T(2,128)S(1)} %bitcast.3, f32[16,384]{1,0:T(8,128)S(1)} %get-tuple-element.18.live_ref, bf16[16,768,384]{2,1,0:T(8,128)(2,1)S(1)} %get-tuple-element.19.jac_ref, bf16[16,384,768]{2,1,0:T(8,128)(2,1)S(1)} %get-tuple-element.20.turned_ref, ...), custom_call_target="tpu_custom_call" | custom-call | flops 18874368 | bytes 18874368 | tf_op jit(solution)/shard_map/sweep_step/pallas_call | solution.py:233
  26.0 0.4 collective-permute-start.6
  26.4 1.0 %collective-permute-done.6 = f32[64,384]{1,0:T(8,128)S(1)} collective-permute-done((f32[64,384]{1,0:T(8,128)S(1)}, f32[64,384]{1,0:T(8,128)S(1)}, u32[]{:S(2)}, u32[]{:S(2)}) %collective-permute-start.6) | collective-permute-done | bytes 98336 | tf_op jit(solution)/shard_map/ppermute | solution.py:55
  27.4 2.4 %collective-permute-start.7 = (bf16[32,384]{1,0:T(8,128)(2,1)S(1)}, bf16[32,384]{1,0:T(8,128)(2,1)S(1)}, u32[]{:S(2)}, u32[]{:S(2)}) collective-permute-start(bf16[32,384]{1,0:T(8,128)(2,1)S(1)} %broadcast_select_fusion.2), channel_id=1, source_target_pairs={{0,7},{1,6},{2,5},{3,4},{4,3},{5,2},{6,1},{7,0},{8,15},{9,14},{10,... | collective-permute-start | bytes 73736 | tf_op jit(solution)/shard_map/ppermute | solution.py:21
  29.8 0.0 collective-permute-start.8
  29.8 2.7 %collective-permute-done.7 = bf16[32,384]{1,0:T(8,128)(2,1)S(1)} collective-permute-done((bf16[32,384]{1,0:T(8,128)(2,1)S(1)}, bf16[32,384]{1,0:T(8,128)(2,1)S(1)}, u32[]{:S(2)}, u32[]{:S(2)}) %collective-permute-start.7) | collective-permute-done | bytes 24608 | tf_op jit(solution)/shard_map/ppermute | solution.py:21
  32.5 0.8 %collective-permute-done.8 = bf16[32,384]{1,0:T(8,128)(2,1)S(1)} collective-permute-done((bf16[32,384]{1,0:T(8,128)(2,1)S(1)}, bf16[32,384]{1,0:T(8,128)(2,1)S(1)}, u32[]{:S(2)}, u32[]{:S(2)}) %collective-permute-start.8) | collective-permute-done | bytes 24608 | tf_op jit(solution)/shard_map/ppermute | solution.py:21
  33.4 1.3 %collective-permute-start.11 = (bf16[64,384]{1,0:T(8,128)(2,1)S(1)}, bf16[64,384]{1,0:T(8,128)(2,1)S(1)}, u32[]{:S(2)}, u32[]{:S(2)}) collective-permute-start(bf16[64,384]{1,0:T(8,128)(2,1)S(1)} %pad_maximum_fusion.3.refs_3_), channel_id=1, source_target_pairs={{0,28},{4,24},{8,20},{12,16},{16,12},{20,8},{24,4},{28,0},{1,29},{... | collective-permute-start | bytes 147464 | tf_op jit(solution)/shard_map/ppermute | solution.py:75
  34.7 1.0 %collective-permute-start.10 = (bf16[64,384]{1,0:T(8,128)(2,1)S(1)}, bf16[64,384]{1,0:T(8,128)(2,1)S(1)}, u32[]{:S(2)}, u32[]{:S(2)}) collective-permute-start(bf16[64,384]{1,0:T(8,128)(2,1)S(1)} %pad_maximum_fusion.3.refs_3_), channel_id=1, source_target_pairs={{0,20},{4,16},{8,28},{12,24},{16,4},{20,0},{24,12},{28,8},{1,21},{... | collective-permute-start | bytes 147464 | tf_op jit(solution)/shard_map/ppermute | solution.py:75
  35.7 0.7 %collective-permute-start.9 = (bf16[64,384]{1,0:T(8,128)(2,1)S(1)}, bf16[64,384]{1,0:T(8,128)(2,1)S(1)}, u32[]{:S(2)}, u32[]{:S(2)}) collective-permute-start(bf16[64,384]{1,0:T(8,128)(2,1)S(1)} %pad_maximum_fusion.3.refs_3_), channel_id=1, source_target_pairs={{0,12},{4,8},{8,4},{12,0},{16,28},{20,24},{24,20},{28,16},{1,13},{... | collective-permute-start | bytes 147464 | tf_op jit(solution)/shard_map/ppermute | solution.py:75
  36.4 1.8 %collective-permute-done.11.refs_2_ = bf16[64,384]{1,0:T(8,128)(2,1)S(1)} collective-permute-done((bf16[64,384]{1,0:T(8,128)(2,1)S(1)}, bf16[64,384]{1,0:T(8,128)(2,1)S(1)}, u32[]{:S(2)}, u32[]{:S(2)}) %collective-permute-start.11) | collective-permute-done | bytes 49184 | tf_op jit(solution)/shard_map/ppermute | solution.py:75
  38.2 1.2 %collective-permute-done.10.refs_1_ = bf16[64,384]{1,0:T(8,128)(2,1)S(1)} collective-permute-done((bf16[64,384]{1,0:T(8,128)(2,1)S(1)}, bf16[64,384]{1,0:T(8,128)(2,1)S(1)}, u32[]{:S(2)}, u32[]{:S(2)}) %collective-permute-start.10) | collective-permute-done | bytes 49184 | tf_op jit(solution)/shard_map/ppermute | solution.py:75
  39.4 0.1 collective-permute-done.9.refs_0_
  39.5 3.3 %sweep_step.3 = (f32[16,384]{1,0:T(8,128)}, f32[64,384]{1,0:T(8,128)S(1)}) custom-call(s32[2,16]{1,0:T(2,128)S(1)} %bitcast.4, f32[16,384]{1,0:T(8,128)S(1)} %get-tuple-element.18.live_ref, bf16[16,768,384]{2,1,0:T(8,128)(2,1)S(1)} %get-tuple-element.19.jac_ref, bf16[16,384,768]{2,1,0:T(8,128)(2,1)S(1)} %get-tuple-element.20.turned_ref, ...), custom_call_target="tpu_custom_call" | custom-call | flops 18874368 | bytes 18874368 | tf_op jit(solution)/shard_map/sweep_step/pallas_call | solution.py:233
  42.8 0.2 collective-permute-start.12
  43.0 1.2 %collective-permute-done.12 = f32[64,384]{1,0:T(8,128)S(1)} collective-permute-done((f32[64,384]{1,0:T(8,128)S(1)}, f32[64,384]{1,0:T(8,128)S(1)}, u32[]{:S(2)}, u32[]{:S(2)}) %collective-permute-start.12) | collective-permute-done | bytes 98336 | tf_op jit(solution)/shard_map/ppermute | solution.py:55
  44.2 0.1 collective-permute-start.13
  44.3 5.0 %collective-permute-done.13 = bf16[32,384]{1,0:T(8,128)(2,1)S(1)} collective-permute-done((bf16[32,384]{1,0:T(8,128)(2,1)S(1)}, bf16[32,384]{1,0:T(8,128)(2,1)S(1)}, u32[]{:S(2)}, u32[]{:S(2)}) %collective-permute-start.13) | collective-permute-done | bytes 24608 | tf_op jit(solution)/shard_map/ppermute | solution.py:21
  49.3 1.8 %collective-permute-start.16 = (bf16[32,384]{1,0:T(8,128)(2,1)S(1)}, bf16[32,384]{1,0:T(8,128)(2,1)S(1)}, u32[]{:S(2)}, u32[]{:S(2)}) collective-permute-start(bf16[32,384]{1,0:T(8,128)(2,1)S(1)} %fusion.4), channel_id=1, source_target_pairs={{0,28},{4,24},{8,20},{12,16},{16,12},{20,8},{24,4},{28,0},{1,29},{... | collective-permute-start | bytes 73736 | tf_op jit(solution)/shard_map/ppermute | solution.py:75
  51.1 0.4 collective-permute-start.15
  51.5 0.8 %collective-permute-start.14 = (bf16[32,384]{1,0:T(8,128)(2,1)S(1)}, bf16[32,384]{1,0:T(8,128)(2,1)S(1)}, u32[]{:S(2)}, u32[]{:S(2)}) collective-permute-start(bf16[32,384]{1,0:T(8,128)(2,1)S(1)} %fusion.4), channel_id=1, source_target_pairs={{0,12},{4,8},{8,4},{12,0},{16,28},{20,24},{24,20},{28,16},{1,13},{... | collective-permute-start | bytes 73736 | tf_op jit(solution)/shard_map/ppermute | solution.py:75
  52.3 1.2 %collective-permute-done.16 = bf16[32,384]{1,0:T(8,128)(2,1)S(1)} collective-permute-done((bf16[32,384]{1,0:T(8,128)(2,1)S(1)}, bf16[32,384]{1,0:T(8,128)(2,1)S(1)}, u32[]{:S(2)}, u32[]{:S(2)}) %collective-permute-start.16) | collective-permute-done | bytes 24608 | tf_op jit(solution)/shard_map/ppermute | solution.py:75
  53.5 0.8 %collective-permute-done.15 = bf16[32,384]{1,0:T(8,128)(2,1)S(1)} collective-permute-done((bf16[32,384]{1,0:T(8,128)(2,1)S(1)}, bf16[32,384]{1,0:T(8,128)(2,1)S(1)}, u32[]{:S(2)}, u32[]{:S(2)}) %collective-permute-start.15) | collective-permute-done | bytes 24608 | tf_op jit(solution)/shard_map/ppermute | solution.py:75
  54.4 0.4 collective-permute-done.14
  54.8 0.6 %multiply_add_fusion = f32[32,384]{1,0:T(8,128)} fusion(f32[32,384]{1,0:T(8,128)S(1)} %copy-done.5, f32[32,384]{1,0:T(8,128)S(1)} %copy-done.4, bf16[32,384]{1,0:T(8,128)(2,1)S(1)} %fusion.4, bf16[32,384]{1,0:T(8,128)(2,1)S(1)} %collective-permute-done.16, bf16[32,384]{1,0:T(8,128)(2,1)S(1)} %collective-permute-done.15, ...), kind=kLoop, calls=%fused_computation.13 | loop fusion | flops 110592 | bytes 245760 | tf_op jit(solution)/shard_map/add | solution.py:284
  (16 shorter events, 0.2 us)
Async XLA Ops:
  0.6 22.2 %copy-start.3 = (s32[16,2]{0,1:T(2,128)S(1)}, s32[16,2]{0,1:T(2,128)}, u32[]{:S(2)}) copy-start(s32[16,2]{0,1:T(2,128)} %param.10) | copy-start | bytes 388
  0.6 6.5 %copy-start.4 = (f32[32,384]{1,0:T(8,128)S(1)}, f32[32,384]{1,0:T(8,128)}, u32[]{:S(2)}) copy-start(f32[32,384]{1,0:T(8,128)} %param.13) | copy-start | bytes 147460
  0.7 7.5 %copy-start.5 = (f32[32,384]{1,0:T(8,128)S(1)}, f32[32,384]{1,0:T(8,128)}, u32[]{:S(2)}) copy-start(f32[32,384]{1,0:T(8,128)} %param.12) | copy-start | bytes 147460
  0.7 22.2 %copy-start.2 = (f32[16,128]{1,0:T(8,128)S(1)}, f32[16,128]{1,0:T(8,128)}, u32[]{:S(2)}) copy-start(f32[16,128]{1,0:T(8,128)} %friction_ref.3) | copy-start | bytes 24580
  0.7 22.2 %copy-start.1 = (f32[16,384]{1,0:T(8,128)S(1)}, f32[16,384]{1,0:T(8,128)}, u32[]{:S(2)}) copy-start(f32[16,384]{1,0:T(8,128)} %step_ref.3) | copy-start | bytes 73732
  0.7 22.2 %copy-start = (f32[16,384]{1,0:T(8,128)S(1)}, f32[16,384]{1,0:T(8,128)}, u32[]{:S(2)}) copy-start(f32[16,384]{1,0:T(8,128)} %bias_ref.3) | copy-start | bytes 73732
  6.7 1.5 %collective-permute-start = (f32[64,384]{1,0:T(8,128)S(1)}, f32[64,384]{1,0:T(8,128)S(1)}, u32[]{:S(2)}, u32[]{:S(2)}) collective-permute-start(f32[64,384]{1,0:T(8,128)S(1)} %get-tuple-element.22), channel_id=1, source_target_pairs={{0,4},{4,0},{8,12},{12,8},{16,20},{20,16},{24,28},{28,24},{1,5},{5... | collective-permute-start | bytes 294920 | tf_op jit(solution)/shard_map/ppermute | solution.py:55
  8.2 6.9 %collective-permute-start.1 = (bf16[64,384]{1,0:T(8,128)(2,1)S(1)}, bf16[64,384]{1,0:T(8,128)(2,1)S(1)}, u32[]{:S(2)}, u32[]{:S(2)}) collective-permute-start(bf16[64,384]{1,0:T(8,128)(2,1)S(1)} %get-tuple-element.24), channel_id=1, source_target_pairs={{0,7},{1,6},{2,5},{3,4},{4,3},{5,2},{6,1},{7,0},{8,15},{9,14},{10,... | collective-permute-start | bytes 147464 | tf_op jit(solution)/shard_map/ppermute | solution.py:21
  13.0 3.5 %collective-permute-start.2 = (bf16[64,384]{1,0:T(8,128)(2,1)S(1)}, bf16[64,384]{1,0:T(8,128)(2,1)S(1)}, u32[]{:S(2)}, u32[]{:S(2)}) collective-permute-start(bf16[64,384]{1,0:T(8,128)(2,1)S(1)} %get-tuple-element.25), channel_id=1, source_target_pairs={{0,5},{1,4},{2,7},{3,6},{4,1},{5,0},{6,3},{7,2},{8,13},{9,12},{10,... | collective-permute-start | bytes 147464 | tf_op jit(solution)/shard_map/ppermute | solution.py:21
  16.6 4.5 %collective-permute-start.5 = (bf16[64,384]{1,0:T(8,128)(2,1)S(1)}, bf16[64,384]{1,0:T(8,128)(2,1)S(1)}, u32[]{:S(2)}, u32[]{:S(2)}) collective-permute-start(bf16[64,384]{1,0:T(8,128)(2,1)S(1)} %pad_maximum_fusion.2.refs_3_), channel_id=1, source_target_pairs={{0,28},{4,24},{8,20},{12,16},{16,12},{20,8},{24,4},{28,0},{1,29},{... | collective-permute-start | bytes 147464 | tf_op jit(solution)/shard_map/ppermute | solution.py:75
  19.0 3.7 %collective-permute-start.4 = (bf16[64,384]{1,0:T(8,128)(2,1)S(1)}, bf16[64,384]{1,0:T(8,128)(2,1)S(1)}, u32[]{:S(2)}, u32[]{:S(2)}) collective-permute-start(bf16[64,384]{1,0:T(8,128)(2,1)S(1)} %pad_maximum_fusion.2.refs_3_), channel_id=1, source_target_pairs={{0,20},{4,16},{8,28},{12,24},{16,4},{20,0},{24,12},{28,8},{1,21},{... | collective-permute-start | bytes 147464 | tf_op jit(solution)/shard_map/ppermute | solution.py:75
  19.3 3.5 %collective-permute-start.3 = (bf16[64,384]{1,0:T(8,128)(2,1)S(1)}, bf16[64,384]{1,0:T(8,128)(2,1)S(1)}, u32[]{:S(2)}, u32[]{:S(2)}) collective-permute-start(bf16[64,384]{1,0:T(8,128)(2,1)S(1)} %pad_maximum_fusion.2.refs_3_), channel_id=1, source_target_pairs={{0,12},{4,8},{8,4},{12,0},{16,28},{20,24},{24,20},{28,16},{1,13},{... | collective-permute-start | bytes 147464 | tf_op jit(solution)/shard_map/ppermute | solution.py:75
  26.0 1.4 %collective-permute-start.6 = (f32[64,384]{1,0:T(8,128)S(1)}, f32[64,384]{1,0:T(8,128)S(1)}, u32[]{:S(2)}, u32[]{:S(2)}) collective-permute-start(f32[64,384]{1,0:T(8,128)S(1)} %get-tuple-element.27), channel_id=1, source_target_pairs={{0,4},{4,0},{8,12},{12,8},{16,20},{20,16},{24,28},{28,24},{1,5},{5... | collective-permute-start | bytes 294920 | tf_op jit(solution)/shard_map/ppermute | solution.py:55
  27.4 5.1 %collective-permute-start.7 = (bf16[32,384]{1,0:T(8,128)(2,1)S(1)}, bf16[32,384]{1,0:T(8,128)(2,1)S(1)}, u32[]{:S(2)}, u32[]{:S(2)}) collective-permute-start(bf16[32,384]{1,0:T(8,128)(2,1)S(1)} %broadcast_select_fusion.2), channel_id=1, source_target_pairs={{0,7},{1,6},{2,5},{3,4},{4,3},{5,2},{6,1},{7,0},{8,15},{9,14},{10,... | collective-permute-start | bytes 73736 | tf_op jit(solution)/shard_map/ppermute | solution.py:21
  29.8 3.6 %collective-permute-start.8 = (bf16[32,384]{1,0:T(8,128)(2,1)S(1)}, bf16[32,384]{1,0:T(8,128)(2,1)S(1)}, u32[]{:S(2)}, u32[]{:S(2)}) collective-permute-start(bf16[32,384]{1,0:T(8,128)(2,1)S(1)} %get-tuple-element.29), channel_id=1, source_target_pairs={{0,5},{1,4},{2,7},{3,6},{4,1},{5,0},{6,3},{7,2},{8,13},{9,12},{10,... | collective-permute-start | bytes 73736 | tf_op jit(solution)/shard_map/ppermute | solution.py:21
  33.4 4.8 %collective-permute-start.11 = (bf16[64,384]{1,0:T(8,128)(2,1)S(1)}, bf16[64,384]{1,0:T(8,128)(2,1)S(1)}, u32[]{:S(2)}, u32[]{:S(2)}) collective-permute-start(bf16[64,384]{1,0:T(8,128)(2,1)S(1)} %pad_maximum_fusion.3.refs_3_), channel_id=1, source_target_pairs={{0,28},{4,24},{8,20},{12,16},{16,12},{20,8},{24,4},{28,0},{1,29},{... | collective-permute-start | bytes 147464 | tf_op jit(solution)/shard_map/ppermute | solution.py:75
  34.7 4.7 %collective-permute-start.10 = (bf16[64,384]{1,0:T(8,128)(2,1)S(1)}, bf16[64,384]{1,0:T(8,128)(2,1)S(1)}, u32[]{:S(2)}, u32[]{:S(2)}) collective-permute-start(bf16[64,384]{1,0:T(8,128)(2,1)S(1)} %pad_maximum_fusion.3.refs_3_), channel_id=1, source_target_pairs={{0,20},{4,16},{8,28},{12,24},{16,4},{20,0},{24,12},{28,8},{1,21},{... | collective-permute-start | bytes 147464 | tf_op jit(solution)/shard_map/ppermute | solution.py:75
  35.7 3.8 %collective-permute-start.9 = (bf16[64,384]{1,0:T(8,128)(2,1)S(1)}, bf16[64,384]{1,0:T(8,128)(2,1)S(1)}, u32[]{:S(2)}, u32[]{:S(2)}) collective-permute-start(bf16[64,384]{1,0:T(8,128)(2,1)S(1)} %pad_maximum_fusion.3.refs_3_), channel_id=1, source_target_pairs={{0,12},{4,8},{8,4},{12,0},{16,28},{20,24},{24,20},{28,16},{1,13},{... | collective-permute-start | bytes 147464 | tf_op jit(solution)/shard_map/ppermute | solution.py:75
  42.8 1.4 %collective-permute-start.12 = (f32[64,384]{1,0:T(8,128)S(1)}, f32[64,384]{1,0:T(8,128)S(1)}, u32[]{:S(2)}, u32[]{:S(2)}) collective-permute-start(f32[64,384]{1,0:T(8,128)S(1)} %get-tuple-element.31), channel_id=1, source_target_pairs={{0,4},{4,0},{8,12},{12,8},{16,20},{20,16},{24,28},{28,24},{1,5},{5... | collective-permute-start | bytes 294920 | tf_op jit(solution)/shard_map/ppermute | solution.py:55
  44.2 5.1 %collective-permute-start.13 = (bf16[32,384]{1,0:T(8,128)(2,1)S(1)}, bf16[32,384]{1,0:T(8,128)(2,1)S(1)}, u32[]{:S(2)}, u32[]{:S(2)}) collective-permute-start(bf16[32,384]{1,0:T(8,128)(2,1)S(1)} %slice.78), channel_id=1, source_target_pairs={{0,5},{1,6},{2,7},{3,4},{4,1},{5,2},{6,3},{7,0},{8,13},{9,14},{10,... | collective-permute-start | bytes 73736 | tf_op jit(solution)/shard_map/ppermute | solution.py:21
  49.3 4.2 %collective-permute-start.16 = (bf16[32,384]{1,0:T(8,128)(2,1)S(1)}, bf16[32,384]{1,0:T(8,128)(2,1)S(1)}, u32[]{:S(2)}, u32[]{:S(2)}) collective-permute-start(bf16[32,384]{1,0:T(8,128)(2,1)S(1)} %fusion.4), channel_id=1, source_target_pairs={{0,28},{4,24},{8,20},{12,16},{16,12},{20,8},{24,4},{28,0},{1,29},{... | collective-permute-start | bytes 73736 | tf_op jit(solution)/shard_map/ppermute | solution.py:75
  51.1 3.3 %collective-permute-start.15 = (bf16[32,384]{1,0:T(8,128)(2,1)S(1)}, bf16[32,384]{1,0:T(8,128)(2,1)S(1)}, u32[]{:S(2)}, u32[]{:S(2)}) collective-permute-start(bf16[32,384]{1,0:T(8,128)(2,1)S(1)} %fusion.4), channel_id=1, source_target_pairs={{0,20},{4,16},{8,28},{12,24},{16,4},{20,0},{24,12},{28,8},{1,21},{... | collective-permute-start | bytes 73736 | tf_op jit(solution)/shard_map/ppermute | solution.py:75
  51.5 3.3 %collective-permute-start.14 = (bf16[32,384]{1,0:T(8,128)(2,1)S(1)}, bf16[32,384]{1,0:T(8,128)(2,1)S(1)}, u32[]{:S(2)}, u32[]{:S(2)}) collective-permute-start(bf16[32,384]{1,0:T(8,128)(2,1)S(1)} %fusion.4), channel_id=1, source_target_pairs={{0,12},{4,8},{8,4},{12,0},{16,28},{20,24},{24,20},{28,16},{1,13},{... | collective-permute-start | bytes 73736 | tf_op jit(solution)/shard_map/ppermute | solution.py:75

commit v8 on v7

--- a/solution.py
+++ b/solution.py
@@ -184,7 +184,7 @@
 
 
 GROUP = 2
-AHEAD = 3
+AHEAD = 4
 LIMIT = 24 * 1024 * 1024
 SMEM = pl.BlockSpec(memory_space=pltpu.SMEM)
 VMEM = pl.BlockSpec(memory_space=pltpu.VMEM)

time: 55.6 us -> 55.3 us (level)
  no operation moved by 1% of the time
where the time goes in v8:
time: 55.3 us; the launch traced here: 55.2 us
  waiting for transfers between devices  23.7 us (43%)
  starting transfers between devices  17.7 us (32%)
  Pallas kernels  11.4 us (21%)
  between operations  1.47 us (3%)
  other arithmetic  0.85 us (2%)
    ppermute x5, waiting for transfers between devices, crossed(): return lax.ppermute(value, ('contact', 'body'), pairs)  12.1 us
    ppermute x9, starting transfers between devices, over_pairs(): parts.append(lax.ppermute(value, 'contact', pairs))  9.26 us
    ppermute x9, waiting for transfers between devices, over_pairs(): parts.append(lax.ppermute(value, 'contact', pairs))  8.57 us
    ppermute x5, starting transfers between devices, crossed(): return lax.ppermute(value, ('contact', 'body'), pairs)  7.3 us
    pallas_call x2, Pallas kernels, sweep_step(): pl.pallas_call(functools.partial(sweep_kernel, len(parts)), out_shape=res...  6.41 us
    pallas_call x1, Pallas kernels, first_push(): pl.pallas_call(first_kernel, out_shape=[pltpu.VMEM((tiles, rows, cols), j...  5.03 us
    ppermute x3, waiting for transfers between devices, pair_sum(): lax.ppermute(value, 'contact', [(place, place ^ 1) for place in range(cou...  3.07 us
  transfers between devices with their start and end apart: 17, of which 17 were waited for; matrix products, arithmetic and copies ran while one was open for 0% of the time, Pallas kernels for 0%

profile of v8, /device:TPU:0, one launch (start us, length us, event | category | flops | bytes accessed | tf_op | source)
XLA Modules:
  0.0 55.2 jit_solution(7833077312906177968)
XLA Ops:
  0.6 0.0 copy-start.3
  0.6 0.0 copy-start.4
  0.7 0.0 copy-start.5
  0.7 0.0 copy-start.2
  0.7 0.0 copy-start.1
  0.7 0.0 copy-start
  1.4 5.0 %first_push.1 = (bf16[16,768,384]{2,1,0:T(8,128)(2,1)S(1)}, bf16[16,384,768]{2,1,0:T(8,128)(2,1)S(1)}, f32[16,384]{1,0:T(8,128)S(1)}, f32[16,384]{1,0:T(8,128)S(1)}, f32[64,384]{1,0:T(8,128)S(1)}) custom-call(s32[1]{0:T(128)S(6)} %copy.11.count_ref, s32[2,16]{1,0:T(2,128)} %bitcast.2, bf16[16,768,384]{2,1,0:T(8,128)(2,1)} %bitcast.5, f32[16,384]{1,0:T(8,128)} %start_ref.1), custom_call_target="tpu_custom_call" | custom-call | flops 9437184 | bytes 9437184 | tf_op jit(solution)/shard_map/first_push/pallas_call | solution.py:207
  6.4 0.5 collective-permute-start
  6.9 0.0 copy-done.4
  6.9 0.9 %collective-permute-done = f32[64,384]{1,0:T(8,128)S(1)} collective-permute-done((f32[64,384]{1,0:T(8,128)S(1)}, f32[64,384]{1,0:T(8,128)S(1)}, u32[]{:S(2)}, u32[]{:S(2)}) %collective-permute-start) | collective-permute-done | bytes 98336 | tf_op jit(solution)/shard_map/ppermute | solution.py:55
  7.9 0.0 copy-done.5
  7.9 4.8 %collective-permute-start.1 = (bf16[64,384]{1,0:T(8,128)(2,1)S(1)}, bf16[64,384]{1,0:T(8,128)(2,1)S(1)}, u32[]{:S(2)}, u32[]{:S(2)}) collective-permute-start(bf16[64,384]{1,0:T(8,128)(2,1)S(1)} %get-tuple-element.24), channel_id=1, source_target_pairs={{0,7},{1,6},{2,5},{3,4},{4,3},{5,2},{6,1},{7,0},{8,15},{9,14},{10,... | collective-permute-start | bytes 147464 | tf_op jit(solution)/shard_map/ppermute | solution.py:21
  12.7 0.0 collective-permute-start.2
  12.7 2.1 %collective-permute-done.1 = bf16[64,384]{1,0:T(8,128)(2,1)S(1)} collective-permute-done((bf16[64,384]{1,0:T(8,128)(2,1)S(1)}, bf16[64,384]{1,0:T(8,128)(2,1)S(1)}, u32[]{:S(2)}, u32[]{:S(2)}) %collective-permute-start.1) | collective-permute-done | bytes 49184 | tf_op jit(solution)/shard_map/ppermute | solution.py:21
  14.8 1.4 %collective-permute-done.2 = bf16[64,384]{1,0:T(8,128)(2,1)S(1)} collective-permute-done((bf16[64,384]{1,0:T(8,128)(2,1)S(1)}, bf16[64,384]{1,0:T(8,128)(2,1)S(1)}, u32[]{:S(2)}, u32[]{:S(2)}) %collective-permute-start.2) | collective-permute-done | bytes 49184 | tf_op jit(solution)/shard_map/ppermute | solution.py:21
  16.3 2.5 %collective-permute-start.5 = (bf16[64,384]{1,0:T(8,128)(2,1)S(1)}, bf16[64,384]{1,0:T(8,128)(2,1)S(1)}, u32[]{:S(2)}, u32[]{:S(2)}) collective-permute-start(bf16[64,384]{1,0:T(8,128)(2,1)S(1)} %pad_maximum_fusion.2.refs_3_), channel_id=1, source_target_pairs={{0,28},{4,24},{8,20},{12,16},{16,12},{20,8},{24,4},{28,0},{1,29},{... | collective-permute-start | bytes 147464 | tf_op jit(solution)/shard_map/ppermute | solution.py:75
  18.8 0.3 collective-permute-start.4
  19.1 0.5 collective-permute-start.3
  19.5 1.3 %collective-permute-done.5.refs_2_ = bf16[64,384]{1,0:T(8,128)(2,1)S(1)} collective-permute-done((bf16[64,384]{1,0:T(8,128)(2,1)S(1)}, bf16[64,384]{1,0:T(8,128)(2,1)S(1)}, u32[]{:S(2)}, u32[]{:S(2)}) %collective-permute-start.5) | collective-permute-done | bytes 49184 | tf_op jit(solution)/shard_map/ppermute | solution.py:75
  20.8 1.7 %collective-permute-done.4.refs_1_ = bf16[64,384]{1,0:T(8,128)(2,1)S(1)} collective-permute-done((bf16[64,384]{1,0:T(8,128)(2,1)S(1)}, bf16[64,384]{1,0:T(8,128)(2,1)S(1)}, u32[]{:S(2)}, u32[]{:S(2)}) %collective-permute-start.4) | collective-permute-done | bytes 49184 | tf_op jit(solution)/shard_map/ppermute | solution.py:75
  22.5 0.1 collective-permute-done.3.refs_0_
  22.6 0.0 copy-done.3
  22.6 0.0 copy-done.2
  22.6 0.0 copy-done.1
  22.6 0.0 copy-done
  22.6 3.2 %sweep_step.2 = (f32[16,384]{1,0:T(8,128)S(1)}, f32[64,384]{1,0:T(8,128)S(1)}) custom-call(s32[2,16]{1,0:T(2,128)S(1)} %bitcast.3, f32[16,384]{1,0:T(8,128)S(1)} %get-tuple-element.18.live_ref, bf16[16,768,384]{2,1,0:T(8,128)(2,1)S(1)} %get-tuple-element.19.jac_ref, bf16[16,384,768]{2,1,0:T(8,128)(2,1)S(1)} %get-tuple-element.20.turned_ref, ...), custom_call_target="tpu_custom_call" | custom-call | flops 18874368 | bytes 18874368 | tf_op jit(solution)/shard_map/sweep_step/pallas_call | solution.py:233
  25.7 0.4 collective-permute-start.6
  26.1 1.0 %collective-permute-done.6 = f32[64,384]{1,0:T(8,128)S(1)} collective-permute-done((f32[64,384]{1,0:T(8,128)S(1)}, f32[64,384]{1,0:T(8,128)S(1)}, u32[]{:S(2)}, u32[]{:S(2)}) %collective-permute-start.6) | collective-permute-done | bytes 98336 | tf_op jit(solution)/shard_map/ppermute | solution.py:55
  27.2 2.4 %collective-permute-start.7 = (bf16[32,384]{1,0:T(8,128)(2,1)S(1)}, bf16[32,384]{1,0:T(8,128)(2,1)S(1)}, u32[]{:S(2)}, u32[]{:S(2)}) collective-permute-start(bf16[32,384]{1,0:T(8,128)(2,1)S(1)} %broadcast_select_fusion.2), channel_id=1, source_target_pairs={{0,7},{1,6},{2,5},{3,4},{4,3},{5,2},{6,1},{7,0},{8,15},{9,14},{10,... | collective-permute-start | bytes 73736 | tf_op jit(solution)/shard_map/ppermute | solution.py:21
  29.5 0.0 collective-permute-start.8
  29.5 2.7 %collective-permute-done.7 = bf16[32,384]{1,0:T(8,128)(2,1)S(1)} collective-permute-done((bf16[32,384]{1,0:T(8,128)(2,1)S(1)}, bf16[32,384]{1,0:T(8,128)(2,1)S(1)}, u32[]{:S(2)}, u32[]{:S(2)}) %collective-permute-start.7) | collective-permute-done | bytes 24608 | tf_op jit(solution)/shard_map/ppermute | solution.py:21
  32.3 0.8 %collective-permute-done.8 = bf16[32,384]{1,0:T(8,128)(2,1)S(1)} collective-permute-done((bf16[32,384]{1,0:T(8,128)(2,1)S(1)}, bf16[32,384]{1,0:T(8,128)(2,1)S(1)}, u32[]{:S(2)}, u32[]{:S(2)}) %collective-permute-start.8) | collective-permute-done | bytes 24608 | tf_op jit(solution)/shard_map/ppermute | solution.py:21
  33.1 1.3 %collective-permute-start.11 = (bf16[64,384]{1,0:T(8,128)(2,1)S(1)}, bf16[64,384]{1,0:T(8,128)(2,1)S(1)}, u32[]{:S(2)}, u32[]{:S(2)}) collective-permute-start(bf16[64,384]{1,0:T(8,128)(2,1)S(1)} %pad_maximum_fusion.3.refs_3_), channel_id=1, source_target_pairs={{0,28},{4,24},{8,20},{12,16},{16,12},{20,8},{24,4},{28,0},{1,29},{... | collective-permute-start | bytes 147464 | tf_op jit(solution)/shard_map/ppermute | solution.py:75
  34.4 1.0 %collective-permute-start.10 = (bf16[64,384]{1,0:T(8,128)(2,1)S(1)}, bf16[64,384]{1,0:T(8,128)(2,1)S(1)}, u32[]{:S(2)}, u32[]{:S(2)}) collective-permute-start(bf16[64,384]{1,0:T(8,128)(2,1)S(1)} %pad_maximum_fusion.3.refs_3_), channel_id=1, source_target_pairs={{0,20},{4,16},{8,28},{12,24},{16,4},{20,0},{24,12},{28,8},{1,21},{... | collective-permute-start | bytes 147464 | tf_op jit(solution)/shard_map/ppermute | solution.py:75
  35.5 0.7 %collective-permute-start.9 = (bf16[64,384]{1,0:T(8,128)(2,1)S(1)}, bf16[64,384]{1,0:T(8,128)(2,1)S(1)}, u32[]{:S(2)}, u32[]{:S(2)}) collective-permute-start(bf16[64,384]{1,0:T(8,128)(2,1)S(1)} %pad_maximum_fusion.3.refs_3_), channel_id=1, source_target_pairs={{0,12},{4,8},{8,4},{12,0},{16,28},{20,24},{24,20},{28,16},{1,13},{... | collective-permute-start | bytes 147464 | tf_op jit(solution)/shard_map/ppermute | solution.py:75
  36.1 1.8 %collective-permute-done.11.refs_2_ = bf16[64,384]{1,0:T(8,128)(2,1)S(1)} collective-permute-done((bf16[64,384]{1,0:T(8,128)(2,1)S(1)}, bf16[64,384]{1,0:T(8,128)(2,1)S(1)}, u32[]{:S(2)}, u32[]{:S(2)}) %collective-permute-start.11) | collective-permute-done | bytes 49184 | tf_op jit(solution)/shard_map/ppermute | solution.py:75
  37.9 1.2 %collective-permute-done.10.refs_1_ = bf16[64,384]{1,0:T(8,128)(2,1)S(1)} collective-permute-done((bf16[64,384]{1,0:T(8,128)(2,1)S(1)}, bf16[64,384]{1,0:T(8,128)(2,1)S(1)}, u32[]{:S(2)}, u32[]{:S(2)}) %collective-permute-start.10) | collective-permute-done | bytes 49184 | tf_op jit(solution)/shard_map/ppermute | solution.py:75
  39.1 0.1 collective-permute-done.9.refs_0_
  39.3 3.3 %sweep_step.3 = (f32[16,384]{1,0:T(8,128)}, f32[64,384]{1,0:T(8,128)S(1)}) custom-call(s32[2,16]{1,0:T(2,128)S(1)} %bitcast.4, f32[16,384]{1,0:T(8,128)S(1)} %get-tuple-element.18.live_ref, bf16[16,768,384]{2,1,0:T(8,128)(2,1)S(1)} %get-tuple-element.19.jac_ref, bf16[16,384,768]{2,1,0:T(8,128)(2,1)S(1)} %get-tuple-element.20.turned_ref, ...), custom_call_target="tpu_custom_call" | custom-call | flops 18874368 | bytes 18874368 | tf_op jit(solution)/shard_map/sweep_step/pallas_call | solution.py:233
  42.5 0.2 collective-permute-start.12
  42.7 1.2 %collective-permute-done.12 = f32[64,384]{1,0:T(8,128)S(1)} collective-permute-done((f32[64,384]{1,0:T(8,128)S(1)}, f32[64,384]{1,0:T(8,128)S(1)}, u32[]{:S(2)}, u32[]{:S(2)}) %collective-permute-start.12) | collective-permute-done | bytes 98336 | tf_op jit(solution)/shard_map/ppermute | solution.py:55
  43.9 0.1 collective-permute-start.13
  44.1 5.0 %collective-permute-done.13 = bf16[32,384]{1,0:T(8,128)(2,1)S(1)} collective-permute-done((bf16[32,384]{1,0:T(8,128)(2,1)S(1)}, bf16[32,384]{1,0:T(8,128)(2,1)S(1)}, u32[]{:S(2)}, u32[]{:S(2)}) %collective-permute-start.13) | collective-permute-done | bytes 24608 | tf_op jit(solution)/shard_map/ppermute | solution.py:21
  49.0 1.8 %collective-permute-start.16 = (bf16[32,384]{1,0:T(8,128)(2,1)S(1)}, bf16[32,384]{1,0:T(8,128)(2,1)S(1)}, u32[]{:S(2)}, u32[]{:S(2)}) collective-permute-start(bf16[32,384]{1,0:T(8,128)(2,1)S(1)} %fusion.4), channel_id=1, source_target_pairs={{0,28},{4,24},{8,20},{12,16},{16,12},{20,8},{24,4},{28,0},{1,29},{... | collective-permute-start | bytes 73736 | tf_op jit(solution)/shard_map/ppermute | solution.py:75
  50.8 0.4 collective-permute-start.15
  51.3 0.8 %collective-permute-start.14 = (bf16[32,384]{1,0:T(8,128)(2,1)S(1)}, bf16[32,384]{1,0:T(8,128)(2,1)S(1)}, u32[]{:S(2)}, u32[]{:S(2)}) collective-permute-start(bf16[32,384]{1,0:T(8,128)(2,1)S(1)} %fusion.4), channel_id=1, source_target_pairs={{0,12},{4,8},{8,4},{12,0},{16,28},{20,24},{24,20},{28,16},{1,13},{... | collective-permute-start | bytes 73736 | tf_op jit(solution)/shard_map/ppermute | solution.py:75
  52.1 1.2 %collective-permute-done.16 = bf16[32,384]{1,0:T(8,128)(2,1)S(1)} collective-permute-done((bf16[32,384]{1,0:T(8,128)(2,1)S(1)}, bf16[32,384]{1,0:T(8,128)(2,1)S(1)}, u32[]{:S(2)}, u32[]{:S(2)}) %collective-permute-start.16) | collective-permute-done | bytes 24608 | tf_op jit(solution)/shard_map/ppermute | solution.py:75
  53.2 0.8 %collective-permute-done.15 = bf16[32,384]{1,0:T(8,128)(2,1)S(1)} collective-permute-done((bf16[32,384]{1,0:T(8,128)(2,1)S(1)}, bf16[32,384]{1,0:T(8,128)(2,1)S(1)}, u32[]{:S(2)}, u32[]{:S(2)}) %collective-permute-start.15) | collective-permute-done | bytes 24608 | tf_op jit(solution)/shard_map/ppermute | solution.py:75
  54.1 0.4 collective-permute-done.14
  54.5 0.6 %multiply_add_fusion = f32[32,384]{1,0:T(8,128)} fusion(f32[32,384]{1,0:T(8,128)S(1)} %copy-done.5, f32[32,384]{1,0:T(8,128)S(1)} %copy-done.4, bf16[32,384]{1,0:T(8,128)(2,1)S(1)} %fusion.4, bf16[32,384]{1,0:T(8,128)(2,1)S(1)} %collective-permute-done.16, bf16[32,384]{1,0:T(8,128)(2,1)S(1)} %collective-permute-done.15, ...), kind=kLoop, calls=%fused_computation.13 | loop fusion | flops 110592 | bytes 245760 | tf_op jit(solution)/shard_map/add | solution.py:284
  (16 shorter events, 0.2 us)
Async XLA Ops:
  0.6 21.9 %copy-start.3 = (s32[16,2]{0,1:T(2,128)S(1)}, s32[16,2]{0,1:T(2,128)}, u32[]{:S(2)}) copy-start(s32[16,2]{0,1:T(2,128)} %param.10) | copy-start | bytes 388
  0.6 6.3 %copy-start.4 = (f32[32,384]{1,0:T(8,128)S(1)}, f32[32,384]{1,0:T(8,128)}, u32[]{:S(2)}) copy-start(f32[32,384]{1,0:T(8,128)} %param.13) | copy-start | bytes 147460
  0.7 7.2 %copy-start.5 = (f32[32,384]{1,0:T(8,128)S(1)}, f32[32,384]{1,0:T(8,128)}, u32[]{:S(2)}) copy-start(f32[32,384]{1,0:T(8,128)} %param.12) | copy-start | bytes 147460
  0.7 21.9 %copy-start.2 = (f32[16,128]{1,0:T(8,128)S(1)}, f32[16,128]{1,0:T(8,128)}, u32[]{:S(2)}) copy-start(f32[16,128]{1,0:T(8,128)} %friction_ref.3) | copy-start | bytes 24580
  0.7 21.9 %copy-start.1 = (f32[16,384]{1,0:T(8,128)S(1)}, f32[16,384]{1,0:T(8,128)}, u32[]{:S(2)}) copy-start(f32[16,384]{1,0:T(8,128)} %step_ref.3) | copy-start | bytes 73732
  0.7 21.9 %copy-start = (f32[16,384]{1,0:T(8,128)S(1)}, f32[16,384]{1,0:T(8,128)}, u32[]{:S(2)}) copy-start(f32[16,384]{1,0:T(8,128)} %bias_ref.3) | copy-start | bytes 73732
  6.4 1.5 %collective-permute-start = (f32[64,384]{1,0:T(8,128)S(1)}, f32[64,384]{1,0:T(8,128)S(1)}, u32[]{:S(2)}, u32[]{:S(2)}) collective-permute-start(f32[64,384]{1,0:T(8,128)S(1)} %get-tuple-element.22), channel_id=1, source_target_pairs={{0,4},{4,0},{8,12},{12,8},{16,20},{20,16},{24,28},{28,24},{1,5},{5... | collective-permute-start | bytes 294920 | tf_op jit(solution)/shard_map/ppermute | solution.py:55
  7.9 6.9 %collective-permute-start.1 = (bf16[64,384]{1,0:T(8,128)(2,1)S(1)}, bf16[64,384]{1,0:T(8,128)(2,1)S(1)}, u32[]{:S(2)}, u32[]{:S(2)}) collective-permute-start(bf16[64,384]{1,0:T(8,128)(2,1)S(1)} %get-tuple-element.24), channel_id=1, source_target_pairs={{0,7},{1,6},{2,5},{3,4},{4,3},{5,2},{6,1},{7,0},{8,15},{9,14},{10,... | collective-permute-start | bytes 147464 | tf_op jit(solution)/shard_map/ppermute | solution.py:21
  12.7 3.5 %collective-permute-start.2 = (bf16[64,384]{1,0:T(8,128)(2,1)S(1)}, bf16[64,384]{1,0:T(8,128)(2,1)S(1)}, u32[]{:S(2)}, u32[]{:S(2)}) collective-permute-start(bf16[64,384]{1,0:T(8,128)(2,1)S(1)} %get-tuple-element.25), channel_id=1, source_target_pairs={{0,5},{1,4},{2,7},{3,6},{4,1},{5,0},{6,3},{7,2},{8,13},{9,12},{10,... | collective-permute-start | bytes 147464 | tf_op jit(solution)/shard_map/ppermute | solution.py:21
  16.3 4.5 %collective-permute-start.5 = (bf16[64,384]{1,0:T(8,128)(2,1)S(1)}, bf16[64,384]{1,0:T(8,128)(2,1)S(1)}, u32[]{:S(2)}, u32[]{:S(2)}) collective-permute-start(bf16[64,384]{1,0:T(8,128)(2,1)S(1)} %pad_maximum_fusion.2.refs_3_), channel_id=1, source_target_pairs={{0,28},{4,24},{8,20},{12,16},{16,12},{20,8},{24,4},{28,0},{1,29},{... | collective-permute-start | bytes 147464 | tf_op jit(solution)/shard_map/ppermute | solution.py:75
  18.8 3.7 %collective-permute-start.4 = (bf16[64,384]{1,0:T(8,128)(2,1)S(1)}, bf16[64,384]{1,0:T(8,128)(2,1)S(1)}, u32[]{:S(2)}, u32[]{:S(2)}) collective-permute-start(bf16[64,384]{1,0:T(8,128)(2,1)S(1)} %pad_maximum_fusion.2.refs_3_), channel_id=1, source_target_pairs={{0,20},{4,16},{8,28},{12,24},{16,4},{20,0},{24,12},{28,8},{1,21},{... | collective-permute-start | bytes 147464 | tf_op jit(solution)/shard_map/ppermute | solution.py:75
  19.1 3.5 %collective-permute-start.3 = (bf16[64,384]{1,0:T(8,128)(2,1)S(1)}, bf16[64,384]{1,0:T(8,128)(2,1)S(1)}, u32[]{:S(2)}, u32[]{:S(2)}) collective-permute-start(bf16[64,384]{1,0:T(8,128)(2,1)S(1)} %pad_maximum_fusion.2.refs_3_), channel_id=1, source_target_pairs={{0,12},{4,8},{8,4},{12,0},{16,28},{20,24},{24,20},{28,16},{1,13},{... | collective-permute-start | bytes 147464 | tf_op jit(solution)/shard_map/ppermute | solution.py:75
  25.7 1.4 %collective-permute-start.6 = (f32[64,384]{1,0:T(8,128)S(1)}, f32[64,384]{1,0:T(8,128)S(1)}, u32[]{:S(2)}, u32[]{:S(2)}) collective-permute-start(f32[64,384]{1,0:T(8,128)S(1)} %get-tuple-element.27), channel_id=1, source_target_pairs={{0,4},{4,0},{8,12},{12,8},{16,20},{20,16},{24,28},{28,24},{1,5},{5... | collective-permute-start | bytes 294920 | tf_op jit(solution)/shard_map/ppermute | solution.py:55
  27.2 5.1 %collective-permute-start.7 = (bf16[32,384]{1,0:T(8,128)(2,1)S(1)}, bf16[32,384]{1,0:T(8,128)(2,1)S(1)}, u32[]{:S(2)}, u32[]{:S(2)}) collective-permute-start(bf16[32,384]{1,0:T(8,128)(2,1)S(1)} %broadcast_select_fusion.2), channel_id=1, source_target_pairs={{0,7},{1,6},{2,5},{3,4},{4,3},{5,2},{6,1},{7,0},{8,15},{9,14},{10,... | collective-permute-start | bytes 73736 | tf_op jit(solution)/shard_map/ppermute | solution.py:21
  29.5 3.6 %collective-permute-start.8 = (bf16[32,384]{1,0:T(8,128)(2,1)S(1)}, bf16[32,384]{1,0:T(8,128)(2,1)S(1)}, u32[]{:S(2)}, u32[]{:S(2)}) collective-permute-start(bf16[32,384]{1,0:T(8,128)(2,1)S(1)} %get-tuple-element.29), channel_id=1, source_target_pairs={{0,5},{1,4},{2,7},{3,6},{4,1},{5,0},{6,3},{7,2},{8,13},{9,12},{10,... | collective-permute-start | bytes 73736 | tf_op jit(solution)/shard_map/ppermute | solution.py:21
  33.1 4.8 %collective-permute-start.11 = (bf16[64,384]{1,0:T(8,128)(2,1)S(1)}, bf16[64,384]{1,0:T(8,128)(2,1)S(1)}, u32[]{:S(2)}, u32[]{:S(2)}) collective-permute-start(bf16[64,384]{1,0:T(8,128)(2,1)S(1)} %pad_maximum_fusion.3.refs_3_), channel_id=1, source_target_pairs={{0,28},{4,24},{8,20},{12,16},{16,12},{20,8},{24,4},{28,0},{1,29},{... | collective-permute-start | bytes 147464 | tf_op jit(solution)/shard_map/ppermute | solution.py:75
  34.4 4.7 %collective-permute-start.10 = (bf16[64,384]{1,0:T(8,128)(2,1)S(1)}, bf16[64,384]{1,0:T(8,128)(2,1)S(1)}, u32[]{:S(2)}, u32[]{:S(2)}) collective-permute-start(bf16[64,384]{1,0:T(8,128)(2,1)S(1)} %pad_maximum_fusion.3.refs_3_), channel_id=1, source_target_pairs={{0,20},{4,16},{8,28},{12,24},{16,4},{20,0},{24,12},{28,8},{1,21},{... | collective-permute-start | bytes 147464 | tf_op jit(solution)/shard_map/ppermute | solution.py:75
  35.5 3.8 %collective-permute-start.9 = (bf16[64,384]{1,0:T(8,128)(2,1)S(1)}, bf16[64,384]{1,0:T(8,128)(2,1)S(1)}, u32[]{:S(2)}, u32[]{:S(2)}) collective-permute-start(bf16[64,384]{1,0:T(8,128)(2,1)S(1)} %pad_maximum_fusion.3.refs_3_), channel_id=1, source_target_pairs={{0,12},{4,8},{8,4},{12,0},{16,28},{20,24},{24,20},{28,16},{1,13},{... | collective-permute-start | bytes 147464 | tf_op jit(solution)/shard_map/ppermute | solution.py:75
  42.5 1.4 %collective-permute-start.12 = (f32[64,384]{1,0:T(8,128)S(1)}, f32[64,384]{1,0:T(8,128)S(1)}, u32[]{:S(2)}, u32[]{:S(2)}) collective-permute-start(f32[64,384]{1,0:T(8,128)S(1)} %get-tuple-element.31), channel_id=1, source_target_pairs={{0,4},{4,0},{8,12},{12,8},{16,20},{20,16},{24,28},{28,24},{1,5},{5... | collective-permute-start | bytes 294920 | tf_op jit(solution)/shard_map/ppermute | solution.py:55
  43.9 5.1 %collective-permute-start.13 = (bf16[32,384]{1,0:T(8,128)(2,1)S(1)}, bf16[32,384]{1,0:T(8,128)(2,1)S(1)}, u32[]{:S(2)}, u32[]{:S(2)}) collective-permute-start(bf16[32,384]{1,0:T(8,128)(2,1)S(1)} %slice.78), channel_id=1, source_target_pairs={{0,5},{1,6},{2,7},{3,4},{4,1},{5,2},{6,3},{7,0},{8,13},{9,14},{10,... | collective-permute-start | bytes 73736 | tf_op jit(solution)/shard_map/ppermute | solution.py:21
  49.0 4.2 %collective-permute-start.16 = (bf16[32,384]{1,0:T(8,128)(2,1)S(1)}, bf16[32,384]{1,0:T(8,128)(2,1)S(1)}, u32[]{:S(2)}, u32[]{:S(2)}) collective-permute-start(bf16[32,384]{1,0:T(8,128)(2,1)S(1)} %fusion.4), channel_id=1, source_target_pairs={{0,28},{4,24},{8,20},{12,16},{16,12},{20,8},{24,4},{28,0},{1,29},{... | collective-permute-start | bytes 73736 | tf_op jit(solution)/shard_map/ppermute | solution.py:75
  50.8 3.3 %collective-permute-start.15 = (bf16[32,384]{1,0:T(8,128)(2,1)S(1)}, bf16[32,384]{1,0:T(8,128)(2,1)S(1)}, u32[]{:S(2)}, u32[]{:S(2)}) collective-permute-start(bf16[32,384]{1,0:T(8,128)(2,1)S(1)} %fusion.4), channel_id=1, source_target_pairs={{0,20},{4,16},{8,28},{12,24},{16,4},{20,0},{24,12},{28,8},{1,21},{... | collective-permute-start | bytes 73736 | tf_op jit(solution)/shard_map/ppermute | solution.py:75
  51.3 3.3 %collective-permute-start.14 = (bf16[32,384]{1,0:T(8,128)(2,1)S(1)}, bf16[32,384]{1,0:T(8,128)(2,1)S(1)}, u32[]{:S(2)}, u32[]{:S(2)}) collective-permute-start(bf16[32,384]{1,0:T(8,128)(2,1)S(1)} %fusion.4), channel_id=1, source_target_pairs={{0,12},{4,8},{8,4},{12,0},{16,28},{20,24},{24,20},{28,16},{1,13},{... | collective-permute-start | bytes 73736 | tf_op jit(solution)/shard_map/ppermute | solution.py:75
